TPU v7x, 128 devices: a whole 4x4x4 slice. The times are simulated.
128 devices in a mesh: seq: 8 (over z, x_hi), fsdp: 16 (over x_lo, y, core).
Axes of the slice: x: 4 (x_hi: 2, x_lo: 2; x = x_hi * 2 + x_lo), y: 4, z: 4, core: 2. Of those that a mesh axis runs over, the one named last changes fastest.
Arguments:
- tokens: bfloat16 [16384, 1024], P(('fsdp', 'seq')), may hold values from -6 to 6
- segments: int32 [16384], replicated, may hold values from 0 to 3, as said below
- cotangent: bfloat16 [16384, 1024], P(('fsdp', 'seq')), may hold values from -6 to 6
- attention_gain: bfloat16 [1024], P('fsdp'), may hold values from 0.5 to 1.5
- query_gain: bfloat16 [64], P('fsdp'), may hold values from 0.69921875 to 2
- key_gain: bfloat16 [64], P('fsdp'), may hold values from 0.69921875 to 2
- query_weight: bfloat16 [1024, 1024], P('fsdp'), may hold values from -0.1875 to 0.1875
- key_weight: bfloat16 [1024, 512], P('fsdp'), may hold values from -0.1875 to 0.1875
- value_weight: bfloat16 [1024, 512], P('fsdp'), may hold values from -0.1875 to 0.1875
- out_weight: bfloat16 [1024, 1024], P('fsdp'), may hold values from -1.5 to 1.5
- feedforward_gain: bfloat16 [1024], P('fsdp'), may hold values from 0.5 to 1.5
- gate_weight: bfloat16 [1024, 4608], P('fsdp'), may hold values from -0.1875 to 0.1875
- up_weight: bfloat16 [1024, 4608], P('fsdp'), may hold values from -0.1875 to 0.1875
- down_weight: bfloat16 [4608, 1024], P('fsdp'), may hold values from -0.09375 to 0.09375
Outputs:
- layer_out: bfloat16 [16384, 1024], P(('fsdp', 'seq'))
- input_grad: float32 [16384, 1024], P(('fsdp', 'seq'))
- grad_attention_gain: float32 [1024], P('fsdp')
- grad_query_gain: float32 [64], P('fsdp')
- grad_key_gain: float32 [64], P('fsdp')
- grad_query_weight: float32 [1024, 1024], P('fsdp')
- grad_key_weight: float32 [1024, 512], P('fsdp')
- grad_value_weight: float32 [1024, 512], P('fsdp')
- grad_out_weight: float32 [1024, 1024], P('fsdp')
- grad_feedforward_gain: float32 [1024], P('fsdp')
- grad_gate_weight: float32 [1024, 4608], P('fsdp')
- grad_up_weight: float32 [1024, 4608], P('fsdp')
- grad_down_weight: float32 [4608, 1024], P('fsdp')
Inputs may be any that keep to these rules, and one draw needn't show every extreme that they name: `segments`: segment ids never fall along the stream, every id from 0 to 3 occurs, no document has more than 8192 tokens, and one has exactly 8192.
All inputs are finite; a program needn't handle non-finite values.
Results may differ from a plain program's by a relative error of at most 0.03.
Values may be sent and summed in bfloat16 or wider, within the bound.
A program may use at most 192 MiB of HBM per device.

v0:
```python
import jax
import jax.numpy as jnp
from jax import lax
from jax.sharding import PartitionSpec as P

H = 16
KVH = 8
HD = 64
DOCS = 4


EPSILON = 1e-06
THETA = 1000000.0


def rms_scale(values):
    return lax.rsqrt(jnp.mean(values * values, axis=-1, keepdims=True) + EPSILON)


def norm_back(values, inverse, gain, grad, axes):
    normalized = values * inverse
    gain_term = jnp.sum(grad * normalized, axis=axes)
    weighted = grad * gain
    inner = jnp.mean(weighted * normalized, axis=-1, keepdims=True)
    return (gain_term, inverse * (weighted - normalized * inner))


def doc_positions(segments, first, count):
    labels = jnp.arange(DOCS, dtype=jnp.int32)
    member = (segments[None, :] == labels[:, None]).astype(jnp.int32)
    lengths = jnp.sum(member, axis=1)
    starts = jnp.cumsum(lengths) - lengths
    local_ids = lax.dynamic_slice_in_dim(segments, first, count)
    picked = (local_ids[:, None] == labels[None, :]).astype(jnp.int32)
    index = first + jnp.arange(count, dtype=jnp.int32)
    return index - jnp.sum(picked * starts[None, :], axis=1)


def rope_tables(positions, width):
    half = width // 2
    freqs = THETA ** (-2.0 * jnp.arange(half, dtype=jnp.float32) / width)
    angles = positions.astype(jnp.float32)[:, None] * freqs[None, :]
    return (jnp.cos(angles), jnp.sin(angles))


def rotate(values, cosine, sine):
    half = values.shape[-1] // 2
    first_half = values[..., :half]
    second_half = values[..., half:]
    cos_rows = cosine[:, None, :]
    sin_rows = sine[:, None, :]
    return jnp.concatenate(
        [
            first_half * cos_rows - second_half * sin_rows,
            second_half * cos_rows + first_half * sin_rows,
        ],
        axis=-1,
    )


def local(
    tokens,
    segments,
    cotangent,
    attention_gain,
    query_gain,
    key_gain,
    query_weight,
    key_weight,
    value_weight,
    out_weight,
    feedforward_gain,
    gate_weight,
    up_weight,
    down_weight,
):
    seq_count = lax.axis_size("seq")
    fsdp_count = lax.axis_size("fsdp")
    rows = tokens.shape[0]
    block_rows = rows * seq_count
    total_rows = block_rows * fsdp_count
    groups = KVH // seq_count
    repeat = H // KVH
    scale = HD ** (-0.5)
    fsdp_index = lax.axis_index("fsdp")
    seq_index = lax.axis_index("seq")
    token_start = (fsdp_index * seq_count + seq_index) * rows
    block_start = fsdp_index * block_rows
    block_last = block_start + block_rows - 1
    multiple = 1
    while block_rows * multiple < 512 and fsdp_count % (2 * multiple) == 0:
        multiple = multiple * 2
    key_block = block_rows * multiple
    (
        full_gain_one,
        full_query_gain,
        full_key_gain,
        full_query,
        full_key,
        full_value,
        full_out,
        full_gain_two,
        full_gate,
        full_up,
        full_down,
    ) = (
        lax.all_gather(attention_gain, "fsdp", axis=0, tiled=True),
        lax.all_gather(query_gain, "fsdp", axis=0, tiled=True),
        lax.all_gather(key_gain, "fsdp", axis=0, tiled=True),
        lax.all_gather(query_weight, "fsdp", axis=0, tiled=True),
        lax.all_gather(key_weight, "fsdp", axis=0, tiled=True),
        lax.all_gather(value_weight, "fsdp", axis=0, tiled=True),
        lax.all_gather(out_weight, "fsdp", axis=0, tiled=True),
        lax.all_gather(feedforward_gain, "fsdp", axis=0, tiled=True),
        lax.all_gather(gate_weight, "fsdp", axis=0, tiled=True),
        lax.all_gather(up_weight, "fsdp", axis=0, tiled=True),
        lax.all_gather(down_weight, "fsdp", axis=0, tiled=True),
    )
    gain_one = full_gain_one.astype(jnp.float32)
    query_scale = full_query_gain.astype(jnp.float32)
    key_scale = full_key_gain.astype(jnp.float32)
    gain_two = full_gain_two.astype(jnp.float32)
    bound = scale * HD * jnp.max(jnp.abs(query_scale)) * jnp.max(jnp.abs(key_scale))
    positions = doc_positions(segments, token_start, rows)
    cosine, sine = rope_tables(positions, HD)
    inputs = tokens.astype(jnp.float32)
    inverse_one = rms_scale(inputs)
    normed_one = (inputs * inverse_one * gain_one).astype(jnp.bfloat16)
    query_heads = jnp.dot(normed_one, full_query, preferred_element_type=jnp.float32).reshape(
        rows, H, HD
    )
    key_heads = jnp.dot(normed_one, full_key, preferred_element_type=jnp.float32).reshape(
        rows, KVH, HD
    )
    value_heads = (
        jnp.dot(normed_one, full_value, preferred_element_type=jnp.float32)
        .astype(jnp.bfloat16)
        .reshape(rows, KVH, HD)
    )
    inverse_query = rms_scale(query_heads)
    inverse_key = rms_scale(key_heads)
    query_rot = rotate(query_heads * inverse_query * query_scale, cosine, sine).astype(jnp.bfloat16)
    key_rot = rotate(key_heads * inverse_key * key_scale, cosine, sine).astype(jnp.bfloat16)
    packed = jnp.concatenate(
        [query_rot.reshape(rows, KVH, repeat * HD), key_rot, value_heads], axis=2
    )
    headwise = lax.all_to_all(packed, "seq", split_axis=1, concat_axis=0, tiled=True)
    query_block = headwise[:, :, : repeat * HD].reshape(block_rows, groups, repeat, HD)
    key_values = headwise[:, :, repeat * HD :]
    query_index = block_start + jnp.arange(block_rows, dtype=jnp.int32)
    query_ids = lax.dynamic_slice_in_dim(segments, block_start, block_rows)

    def score_block(kv_piece, piece_start):
        count = kv_piece.shape[0]
        key_part = kv_piece[:, :, :HD]
        value_part = kv_piece[:, :, HD:]
        scores = (
            jnp.einsum("sgrd,pgd->grsp", query_block, key_part, preferred_element_type=jnp.float32)
            * scale
        )
        key_index = piece_start + jnp.arange(count, dtype=jnp.int32)
        key_ids = lax.dynamic_slice_in_dim(segments, piece_start, count)
        allowed = (key_index[None, :] <= query_index[:, None]) & (
            key_ids[None, :] == query_ids[:, None]
        )
        return (jnp.where(allowed, jnp.exp(scores - bound), 0.0), key_part, value_part)

    def forward_block(carry, kv_piece, piece_start):

        def forward_compute(state):
            exps, key_part, value_part = score_block(kv_piece, piece_start)
            totals = state[0] + jnp.sum(exps, axis=-1)
            sums = state[1] + jnp.einsum(
                "grsp,pgd->sgrd",
                exps.astype(jnp.bfloat16),
                value_part,
                preferred_element_type=jnp.float32,
            )
            return (totals, sums)

        def unchanged(state):
            return state

        return lax.cond(piece_start > block_last, unchanged, forward_compute, carry)

    empty = (
        jnp.zeros((groups, repeat, block_rows), jnp.float32),
        jnp.zeros((block_rows, groups, repeat, HD), jnp.float32),
    )
    kv_piece = lax.all_gather(key_values, "fsdp", axis=0, tiled=True)
    count = kv_piece.shape[0]
    pieces = kv_piece.reshape(count // key_block, key_block, groups, 2 * HD)
    starts = key_block * jnp.arange(count // key_block, dtype=jnp.int32)

    def scan_step(state, item):
        return (forward_block(state, item[0], item[1]), None)

    result, _ = lax.scan(scan_step, empty, (pieces, starts))
    totals, sums = result
    totals_rows = jnp.transpose(totals, (2, 0, 1))
    attended = sums / totals_rows[..., None]
    outgoing = attended.astype(jnp.bfloat16).reshape(block_rows, groups, repeat * HD)
    tokenwise = lax.all_to_all(outgoing, "seq", split_axis=0, concat_axis=1, tiled=True).reshape(
        rows, H * HD
    )
    hidden_state = inputs + jnp.dot(tokenwise, full_out, preferred_element_type=jnp.float32)
    inverse_two = rms_scale(hidden_state)
    normed_two = (hidden_state * inverse_two * gain_two).astype(jnp.bfloat16)
    gate_pre = jnp.dot(normed_two, full_gate, preferred_element_type=jnp.float32)
    up_pre = jnp.dot(normed_two, full_up, preferred_element_type=jnp.float32)
    activated = (jax.nn.silu(gate_pre) * up_pre).astype(jnp.bfloat16)
    ffn_branch = jnp.dot(activated, full_down, preferred_element_type=jnp.float32)
    layer_out = (hidden_state + ffn_branch).astype(jnp.bfloat16)
    down_term = jnp.einsum("tf,td->fd", activated, cotangent, preferred_element_type=jnp.float32)
    grad_act = jnp.einsum("td,fd->tf", cotangent, full_down, preferred_element_type=jnp.float32)
    sigmoid_gate = jax.nn.sigmoid(gate_pre)
    grad_gate = (grad_act * up_pre * sigmoid_gate * (1.0 + gate_pre * (1.0 - sigmoid_gate))).astype(
        jnp.bfloat16
    )
    grad_up = (grad_act * gate_pre * sigmoid_gate).astype(jnp.bfloat16)
    gate_term = jnp.einsum("td,tf->df", normed_two, grad_gate, preferred_element_type=jnp.float32)
    up_term = jnp.einsum("td,tf->df", normed_two, grad_up, preferred_element_type=jnp.float32)
    grad_normed_two = jnp.einsum(
        "tf,df->td", grad_gate, full_gate, preferred_element_type=jnp.float32
    ) + jnp.einsum("tf,df->td", grad_up, full_up, preferred_element_type=jnp.float32)
    gain_two_term, grad_hidden_norm = norm_back(
        hidden_state, inverse_two, gain_two, grad_normed_two, (0,)
    )
    grad_hidden = cotangent.astype(jnp.float32) + grad_hidden_norm
    ffn_shards = (
        lax.psum_scatter(
            gain_two_term.astype(jnp.bfloat16), "fsdp", scatter_dimension=0, tiled=True
        ).astype(jnp.float32),
        lax.psum_scatter(
            gate_term.astype(jnp.bfloat16), "fsdp", scatter_dimension=0, tiled=True
        ).astype(jnp.float32),
        lax.psum_scatter(
            up_term.astype(jnp.bfloat16), "fsdp", scatter_dimension=0, tiled=True
        ).astype(jnp.float32),
        lax.psum_scatter(
            down_term.astype(jnp.bfloat16), "fsdp", scatter_dimension=0, tiled=True
        ).astype(jnp.float32),
    )
    grad_branch = grad_hidden.astype(jnp.bfloat16)
    out_term = jnp.einsum("ti,td->id", tokenwise, grad_branch, preferred_element_type=jnp.float32)
    grad_tokenwise = jnp.einsum(
        "td,id->ti", grad_branch, full_out, preferred_element_type=jnp.float32
    ).astype(jnp.bfloat16)
    grad_heads = lax.all_to_all(
        grad_tokenwise.reshape(rows, KVH, repeat * HD),
        "seq",
        split_axis=1,
        concat_axis=0,
        tiled=True,
    )
    grad_heads = grad_heads.reshape(block_rows, groups, repeat, HD).astype(jnp.float32)
    grad_numer = (grad_heads / totals_rows[..., None]).astype(jnp.bfloat16)
    row_terms = jnp.transpose(jnp.sum(grad_heads * attended, axis=-1) / totals_rows, (1, 2, 0))
    full_kv = lax.all_gather(key_values, "fsdp", axis=0, tiled=True)

    def backward_block(grad_query, item):
        kv_piece, piece_start = item

        def backward_compute(grad_query):
            exps, key_part, value_part = score_block(kv_piece, piece_start)
            grad_probs = jnp.einsum(
                "sgrd,pgd->grsp", grad_numer, value_part, preferred_element_type=jnp.float32
            )
            grad_scores = (exps * (grad_probs - row_terms[..., None])).astype(jnp.bfloat16)
            grad_query = (
                grad_query
                + jnp.einsum(
                    "grsp,pgd->sgrd", grad_scores, key_part, preferred_element_type=jnp.float32
                )
                * scale
            )
            grad_key = (
                jnp.einsum(
                    "grsp,sgrd->pgd", grad_scores, query_block, preferred_element_type=jnp.float32
                )
                * scale
            )
            grad_value = jnp.einsum(
                "grsp,sgrd->pgd",
                exps.astype(jnp.bfloat16),
                grad_numer,
                preferred_element_type=jnp.float32,
            )
            return (grad_query, jnp.concatenate([grad_key, grad_value], axis=-1))

        def skipped(grad_query):
            return (grad_query, jnp.zeros((key_block, groups, 2 * HD), jnp.float32))

        return lax.cond(piece_start > block_last, skipped, backward_compute, grad_query)

    kv_pieces = full_kv.reshape(total_rows // key_block, key_block, groups, 2 * HD)
    kv_starts = key_block * jnp.arange(total_rows // key_block, dtype=jnp.int32)
    grad_query, kv_terms = lax.scan(
        backward_block,
        jnp.zeros((block_rows, groups, repeat, HD), jnp.float32),
        (kv_pieces, kv_starts),
    )
    kv_grads = lax.psum_scatter(
        kv_terms.reshape(total_rows, groups, 2 * HD).astype(jnp.bfloat16),
        "fsdp",
        scatter_dimension=0,
        tiled=True,
    )
    grad_pack = jnp.concatenate(
        [grad_query.reshape(block_rows, groups, repeat * HD).astype(jnp.bfloat16), kv_grads],
        axis=-1,
    )
    grad_tokens = lax.all_to_all(grad_pack, "seq", split_axis=0, concat_axis=1, tiled=True)
    grad_query_rot = grad_tokens[:, :, : repeat * HD].reshape(rows, H, HD).astype(jnp.float32)
    grad_key_rot = grad_tokens[:, :, repeat * HD : (repeat + 1) * HD].astype(jnp.float32)
    grad_value = grad_tokens[:, :, (repeat + 1) * HD :].reshape(rows, KVH * HD)
    query_gain_term, grad_query_heads = norm_back(
        query_heads, inverse_query, query_scale, rotate(grad_query_rot, cosine, -sine), (0, 1)
    )
    key_gain_term, grad_key_heads = norm_back(
        key_heads, inverse_key, key_scale, rotate(grad_key_rot, cosine, -sine), (0, 1)
    )
    grad_query_pre = grad_query_heads.reshape(rows, H * HD).astype(jnp.bfloat16)
    grad_key_pre = grad_key_heads.reshape(rows, KVH * HD).astype(jnp.bfloat16)
    query_term = jnp.einsum(
        "td,tq->dq", normed_one, grad_query_pre, preferred_element_type=jnp.float32
    )
    key_term = jnp.einsum("td,tq->dq", normed_one, grad_key_pre, preferred_element_type=jnp.float32)
    value_term = jnp.einsum("td,tq->dq", normed_one, grad_value, preferred_element_type=jnp.float32)
    grad_normed_one = jnp.einsum(
        "tq,dq->td", grad_query_pre, full_query, preferred_element_type=jnp.float32
    )
    grad_normed_one = grad_normed_one + jnp.einsum(
        "tq,dq->td", grad_key_pre, full_key, preferred_element_type=jnp.float32
    )
    grad_normed_one = grad_normed_one + jnp.einsum(
        "tq,dq->td", grad_value, full_value, preferred_element_type=jnp.float32
    )
    gain_one_term, grad_input_norm = norm_back(inputs, inverse_one, gain_one, grad_normed_one, (0,))
    input_grad = grad_hidden + grad_input_norm
    attn_shards = (
        lax.psum_scatter(
            gain_one_term.astype(jnp.bfloat16), "fsdp", scatter_dimension=0, tiled=True
        ).astype(jnp.float32),
        lax.psum_scatter(
            query_gain_term.astype(jnp.bfloat16), "fsdp", scatter_dimension=0, tiled=True
        ).astype(jnp.float32),
        lax.psum_scatter(
            key_gain_term.astype(jnp.bfloat16), "fsdp", scatter_dimension=0, tiled=True
        ).astype(jnp.float32),
        lax.psum_scatter(
            query_term.astype(jnp.bfloat16), "fsdp", scatter_dimension=0, tiled=True
        ).astype(jnp.float32),
        lax.psum_scatter(
            key_term.astype(jnp.bfloat16), "fsdp", scatter_dimension=0, tiled=True
        ).astype(jnp.float32),
        lax.psum_scatter(
            value_term.astype(jnp.bfloat16), "fsdp", scatter_dimension=0, tiled=True
        ).astype(jnp.float32),
        lax.psum_scatter(
            out_term.astype(jnp.bfloat16), "fsdp", scatter_dimension=0, tiled=True
        ).astype(jnp.float32),
    )
    summed = (
        lax.psum(attn_shards[0].astype(jnp.bfloat16), "seq").astype(jnp.float32),
        lax.psum(attn_shards[1].astype(jnp.bfloat16), "seq").astype(jnp.float32),
        lax.psum(attn_shards[2].astype(jnp.bfloat16), "seq").astype(jnp.float32),
        lax.psum(attn_shards[3].astype(jnp.bfloat16), "seq").astype(jnp.float32),
        lax.psum(attn_shards[4].astype(jnp.bfloat16), "seq").astype(jnp.float32),
        lax.psum(attn_shards[5].astype(jnp.bfloat16), "seq").astype(jnp.float32),
        lax.psum(attn_shards[6].astype(jnp.bfloat16), "seq").astype(jnp.float32),
        lax.psum(ffn_shards[0].astype(jnp.bfloat16), "seq").astype(jnp.float32),
        lax.psum(ffn_shards[1].astype(jnp.bfloat16), "seq").astype(jnp.float32),
        lax.psum(ffn_shards[2].astype(jnp.bfloat16), "seq").astype(jnp.float32),
        lax.psum(ffn_shards[3].astype(jnp.bfloat16), "seq").astype(jnp.float32),
    )
    return (
        layer_out,
        input_grad,
        summed[0],
        summed[1],
        summed[2],
        summed[3],
        summed[4],
        summed[5],
        summed[6],
        summed[7],
        summed[8],
        summed[9],
        summed[10],
    )


def solution(mesh):
    in_specs = (
        P(("fsdp", "seq"), None),
        P(),
        P(("fsdp", "seq"), None),
        P("fsdp"),
        P("fsdp"),
        P("fsdp"),
        P("fsdp", None),
        P("fsdp", None),
        P("fsdp", None),
        P("fsdp", None),
        P("fsdp"),
        P("fsdp", None),
        P("fsdp", None),
        P("fsdp", None),
    )
    out_specs = (
        P(("fsdp", "seq"), None),
        P(("fsdp", "seq"), None),
        P("fsdp"),
        P("fsdp"),
        P("fsdp"),
        P("fsdp", None),
        P("fsdp", None),
        P("fsdp", None),
        P("fsdp", None),
        P("fsdp"),
        P("fsdp", None),
        P("fsdp", None),
        P("fsdp", None),
    )
    return jax.shard_map(local, mesh=mesh, in_specs=in_specs, out_specs=out_specs, check_vma=False)
```

profile of v0, /device:TPU:8, one launch (start us, length us, event | category | flops | bytes accessed | tf_op | source)
XLA Modules:
  0.0 1408.9 jit_solution(16593659195963830307)
XLA Ops:
  15.5 27.1 %all-reduce.9 = (bf16[1024]{0:T(1024)(128)(2,1)S(1)}, bf16[64]{0:T(256)(128)(2,1)S(1)}, bf16[64]{0:T(256)(128)(2,1)S(1)}, bf16[1024]{0:T(1024)(128)(2,1)S(1)}) all-reduce(bf16[1024]{0:T(1024)(128)(2,1)S(1)} %dynamic-update-slice, bf16[64]{0:T(256)(128)(2,1)S(1)} %dynamic-update-slice.2, ...), channel_id=1, replica_groups=mesh['seq'=8,'fsdp'=16] {'fsdp'}, use_global_device_ids=true, to_apply=%add | all-reduce | flops 2176 | bytes 8704
  48.5 29.9 %all-gather.13.cloned.1.call-done = bf16[1024,512]{1,0:T(8,128)(2,1)} async-done(((bf16[64,512]{1,0:T(8,128)(2,1)}), bf16[1024,512]{1,0:T(8,128)(2,1)}) %all-gather.13.cloned.1.call-update) | async-done | bytes 1048592 | tf_op jit(solution)/shard_map/all_gather | solution.py:112
  80.9 33.3 %all-gather.9.cloned.1.call-done = bf16[1024,1024]{1,0:T(8,128)(2,1)} async-done(((bf16[64,1024]{1,0:T(8,128)(2,1)}), bf16[1024,1024]{1,0:T(8,128)(2,1)}) %all-gather.9.cloned.1.call-update) | async-done | bytes 2097168 | tf_op jit(solution)/shard_map/all_gather | solution.py:110
  117.5 18.3 %all_to_all.60 = bf16[128,8,256]{0,2,1:T(8,128)(2,1)S(1)} all-to-all(bf16[128,8,256]{0,2,1:T(8,128)(2,1)S(1)} %pad_maximum_fusion), channel_id=1, replica_groups=mesh['seq'=8,'fsdp'=16] {'seq'}, dimensions={1} | all-to-all | bytes 1048576 | tf_op jit(solution)/shard_map/all_to_all | solution.py:147
  142.9 27.7 %all-gather.15.cloned.1.call-done = bf16[16384,1,128]{2,0,1:T(8,128)(2,1)} async-done(((bf16[1024,1,128]{2,0,1:T(8,128)(2,1)}), bf16[16384,1,128]{2,0,1:T(8,128)(2,1)}) %all-gather.15.cloned.1.call-update) | async-done | bytes 4194320 | tf_op jit(solution)/shard_map/all_gather | solution.py:190
  170.6 6.4 copy.152
  177.1 51.9 %while.29 = (s32[]{:T(128)}, f32[1,2,1024]{2,1,0:T(2,128)S(1)}, f32[1024,1,2,64]{0,3,2,1:T(8,128)S(1)}, s32[16]{0:T(128)S(1)}, s32[]{:T(128)}, /*index=5*/s32[16...) while((s32[]{:T(128)}, f32[1,2,1024]{2,1,0:T(2,128)S(1)}, ...), condition=%wide.region_12.13_spmd.clone, body=%wide.region_8.12_spmd.clone.sunk | while | flops 556926976 | bytes 22094152 | solution.py:198
  178.3 10.5 conditional.6
  190.1 10.5 conditional.6
  201.8 10.5 conditional.6
  231.3 6.7 all-to-all-start.1
  238.0 8.7 all-to-all-done.1
  249.7 15.5 %all-gather.19.cloned.1.call-done = bf16[1024,4608]{1,0:T(8,128)(2,1)} async-done(((bf16[64,4608]{1,0:T(8,128)(2,1)}), bf16[1024,4608]{1,0:T(8,128)(2,1)}) %all-gather.19.cloned.1.call-update) | async-done | bytes 9437200 | tf_op jit(solution)/shard_map/all_gather | solution.py:115
  265.1 6.5 fusion.70
  271.6 53.2 %all-gather.21.cloned.1.call-done = bf16[1024,4608]{1,0:T(8,128)(2,1)} async-done(((bf16[64,4608]{1,0:T(8,128)(2,1)}), bf16[1024,4608]{1,0:T(8,128)(2,1)}) %all-gather.21.cloned.1.call-update) | async-done | bytes 9437200 | tf_op jit(solution)/shard_map/all_gather | solution.py:116
  324.8 6.5 fusion.71
  331.4 55.0 %all-gather.23.cloned.1.call-done = bf16[4608,1024]{1,0:T(8,128)(2,1)} async-done(((bf16[288,1024]{1,0:T(8,128)(2,1)}), bf16[4608,1024]{1,0:T(8,128)(2,1)}) %all-gather.23.cloned.1.call-update) | async-done | bytes 9437200 | tf_op jit(solution)/shard_map/all_gather | solution.py:117
  386.4 8.9 multiply_convert_fusion
  395.3 7.6 fusion.72
  403.0 3.7 multiply_reduce_fusion
  408.6 6.8 all-to-all-start.2
  415.7 9.0 all-to-all-done.2
  433.0 80.6 %while.30 = (s32[]{:T(128)}, f32[1024,1,2,64]{0,3,2,1:T(8,128)S(1)}, bf16[16,1024,1,128]{3,1,0,2:T(8,128)(2,1)}, s32[16]{0:T(128)S(1)}, s32[]{:T(128)}, /*index=...) while((s32[]{:T(128)}, ...), condition=%wide.region_19.20_spmd.clone, body=%wide.region_16.19_spmd.clone.sunk | while | flops 1367214080 | bytes 46842728 | solution.py:298
  434.3 15.2 %conditional.7 = (f32[1024,1,2,64]{0,3,2,1:T(8,128)S(1)}, bf16[1,1024,1,128]{1,3,2,0:T(8,128)(2,1)S(1)}) conditional(s32[]{:T(128)} %convert_element_type.398, (bf16[16,1024,1,128]{1,3,2,0:T(8,128)(2,1)}, s32[]{:T(128)}, s32[]{:T(128)}, s32[]{:T(128)}, s32[16384]{0:T(1024)}, /*index=5*/s32[1024]{0:T(1024)S(1)}, ...), branch_computations={%region_17.17_spmd, %region_18.18_spmd} | conditional | flops 1367214080 | bytes 45789288 | solution.py:294
  441.1 3.7 fusion.24
  451.6 15.2 %conditional.7 = (f32[1024,1,2,64]{0,3,2,1:T(8,128)S(1)}, bf16[1,1024,1,128]{1,3,2,0:T(8,128)(2,1)S(1)}) conditional(s32[]{:T(128)} %convert_element_type.398, (bf16[16,1024,1,128]{1,3,2,0:T(8,128)(2,1)}, s32[]{:T(128)}, s32[]{:T(128)}, s32[]{:T(128)}, s32[16384]{0:T(1024)}, /*index=5*/s32[1024]{0:T(1024)S(1)}, ...), branch_computations={%region_17.17_spmd, %region_18.18_spmd} | conditional | flops 1367214080 | bytes 45789288 | solution.py:294
  458.5 3.7 fusion.24
  468.9 15.2 %conditional.7 = (f32[1024,1,2,64]{0,3,2,1:T(8,128)S(1)}, bf16[1,1024,1,128]{1,3,2,0:T(8,128)(2,1)S(1)}) conditional(s32[]{:T(128)} %convert_element_type.398, (bf16[16,1024,1,128]{1,3,2,0:T(8,128)(2,1)}, s32[]{:T(128)}, s32[]{:T(128)}, s32[]{:T(128)}, s32[16384]{0:T(1024)}, /*index=5*/s32[1024]{0:T(1024)S(1)}, ...), branch_computations={%region_17.17_spmd, %region_18.18_spmd} | conditional | flops 1367214080 | bytes 45789288 | solution.py:294
  475.8 3.7 fusion.24
  513.6 6.4 copy.159
  524.0 260.5 %reduce-scatter.9.cloned.1.call-done = bf16[1024,1,128]{0,2,1:T(8,128)(2,1)} async-done(((bf16[16384,1,128]{0,2,1:T(8,128)(2,1)}), bf16[1024,1,128]{0,2,1:T(8,128)(2,1)}) %reduce-scatter.9.cloned.1.call-update) | async-done | bytes 262160 | tf_op jit(solution)/shard_map/reduce_scatter | solution.py:303
  789.4 6.5 all-to-all-start.3
  798.8 7.4 all-to-all-done.3
  806.2 3.5 reshape.446
  837.9 2.9 convolution_convert_fusion.4
  840.8 6.3 convolution_convert_fusion.2
  847.3 6.4 convolution_convert_fusion.1
  854.6 5.1 convolution_convert_fusion
  859.8 53.4 %reduce-scatter.13.cloned.1.call-done = bf16[64,512]{1,0:T(8,128)(2,1)} async-done(((bf16[1024,512]{1,0:T(8,128)(2,1)}), bf16[64,512]{1,0:T(8,128)(2,1)}) %reduce-scatter.13.cloned.1.call-update) | async-done | bytes 65552 | tf_op jit(solution)/shard_map/reduce_scatter | solution.py:354
  913.2 62.4 %reduce-scatter.15.cloned.1.call-done = bf16[64,512]{1,0:T(8,128)(2,1)} async-done(((bf16[1024,512]{1,0:T(8,128)(2,1)}), bf16[64,512]{1,0:T(8,128)(2,1)}) %reduce-scatter.15.cloned.1.call-update) | async-done | bytes 65552 | tf_op jit(solution)/shard_map/reduce_scatter | solution.py:357
  975.6 64.3 %reduce-scatter.11.cloned.1.call-done = bf16[64,1024]{1,0:T(8,128)(2,1)} async-done(((bf16[1024,1024]{1,0:T(8,128)(2,1)}), bf16[64,1024]{1,0:T(8,128)(2,1)}) %reduce-scatter.11.cloned.1.call-update) | async-done | bytes 131088 | tf_op jit(solution)/shard_map/reduce_scatter | solution.py:351
  1039.9 76.9 %reduce-scatter.19.cloned.1.call-done = bf16[64,4608]{1,0:T(8,128)(2,1)} async-done(((bf16[1024,4608]{1,0:T(8,128)(2,1)}), bf16[64,4608]{1,0:T(8,128)(2,1)}) %reduce-scatter.19.cloned.1.call-update) | async-done | bytes 589840 | tf_op jit(solution)/shard_map/reduce_scatter | solution.py:234
  1116.8 77.9 %reduce-scatter.21.cloned.1.call-done = bf16[64,4608]{1,0:T(8,128)(2,1)} async-done(((bf16[1024,4608]{1,0:T(8,128)(2,1)}), bf16[64,4608]{1,0:T(8,128)(2,1)}) %reduce-scatter.21.cloned.1.call-update) | async-done | bytes 589840 | tf_op jit(solution)/shard_map/reduce_scatter | solution.py:237
  1194.7 77.6 %reduce-scatter.23.cloned.1.call-done = bf16[288,1024]{1,0:T(8,128)(2,1)} async-done(((bf16[4608,1024]{1,0:T(8,128)(2,1)}), bf16[288,1024]{1,0:T(8,128)(2,1)}) %reduce-scatter.23.cloned.1.call-update) | async-done | bytes 589840 | tf_op jit(solution)/shard_map/reduce_scatter | solution.py:240
  1273.5 5.8 fusion.42
  1284.4 30.1 %all-reduce.8 = (bf16[1024]{0:T(1024)(128)(2,1)S(1)}, bf16[64]{0:T(256)(128)(2,1)S(1)}, bf16[64]{0:T(256)(128)(2,1)S(1)}, bf16[1024]{0:T(1024)(128)(2,1)S(1)}) all-reduce(bf16[1024]{0:T(1024)(128)(2,1)S(1)} %get-tuple-element.450, bf16[64]{0:T(256)(128)(2,1)S(1)} %reduce_sum.180, ...), channel_id=3, replica_groups=mesh['seq'=8,'fsdp'=16] {'fsdp'}, use_global_device_ids=true, to_apply=%region_25.26.clone | all-reduce | flops 2176 | bytes 8704
  1314.8 26.7 %all-reduce.10 = (bf16[64]{0:T(256)(128)(2,1)S(1)}, bf16[4]{0:T(256)(128)(2,1)S(1)}, bf16[4]{0:T(256)(128)(2,1)S(1)}, bf16[64]{0:T(256)(128)(2,1)S(1)}) all-reduce(bf16[64]{0:T(256)(128)(2,1)S(1)} %dynamic-slice.5, bf16[4]{0:T(256)(128)(2,1)S(1)} %dynamic-slice.7, ...), channel_id=1, replica_groups=mesh['seq'=8,'fsdp'=16] {'seq'}, use_global_device_ids=true, to_apply=%region_26.27 | all-reduce | flops 136 | bytes 544 | tf_op jit(solution)/shard_map/psum | solution.py:365
  1344.6 48.0 %all-reduce.14.cloned.1.call-done = (bf16[64,1024]{1,0:T(8,128)(2,1)}, bf16[64,512]{1,0:T(8,128)(2,1)}, bf16[64,512]{1,0:T(8,128)(2,1)}, bf16[64,1024]{1,0:T(8,1...) async-done(((bf16[64,1024]{1,0:T(8,128)(2,1)}, bf16[64,512]{1,0:T(8,128)(2,1)}, bf16[64,512]{1,0:T(8,128)(2,1)}, ...) | async-done | bytes 2162704 | tf_op jit(solution)/shard_map/psum | solution.py:368
  (449 shorter events, 186.3 us)
Async XLA Ops:
  7.2 107.0 %copy-start.1 = (bf16[128,1024]{1,0:T(8,128)(2,1)S(1)}, bf16[128,1024]{1,0:T(8,128)(2,1)}, u32[]{:S(2)}) copy-start(bf16[128,1024]{1,0:T(8,128)(2,1)} %param.22) | copy-start | bytes 786436
  7.2 39.5 %all-gather.11.cloned.1.call-start = ((), (), s32[]{:S(2)}) async-start(), calls=%async_computation.13 | async-start | bytes 1114112 | tf_op jit(solution)/shard_map/all_gather | solution.py:111
  7.9 70.5 %all-gather.13.cloned.1.call-start = ((), (), s32[]{:S(2)}) async-start(), calls=%async_computation.14 | async-start | bytes 1114112 | tf_op jit(solution)/shard_map/all_gather | solution.py:112
  8.7 105.5 %all-gather.9.cloned.1.call-start = ((), (), s32[]{:S(2)}) async-start(), calls=%async_computation.12 | async-start | bytes 2228224 | tf_op jit(solution)/shard_map/all_gather | solution.py:110
  9.4 161.2 %all-gather.15.cloned.1.call-start = ((), (), s32[]{:S(2)}) async-start(), calls=%async_computation.15 | async-start | bytes 4456448 | tf_op jit(solution)/shard_map/all_gather | solution.py:190
  42.6 97.6 %copy-start.44 = (bf16[64]{0:T(256)(128)(2,1)}, bf16[64]{0:T(256)(128)(2,1)S(1)}, u32[]{:S(2)}) copy-start(bf16[64]{0:T(256)(128)(2,1)S(1)} %get-tuple-element.506) | copy-start | bytes 388
  42.6 98.8 %copy-start.45 = (bf16[64]{0:T(256)(128)(2,1)}, bf16[64]{0:T(256)(128)(2,1)S(1)}, u32[]{:S(2)}) copy-start(bf16[64]{0:T(256)(128)(2,1)S(1)} %get-tuple-element.505) | copy-start | bytes 388
  42.6 73.8 %copy-start.26 = (f32[1024]{0:T(1024)}, f32[1024]{0:T(1024)S(1)}, u32[]{:S(2)}) copy-start(f32[1024]{0:T(1024)S(1)} %convert_element_type.250) | copy-start | bytes 12292
  42.6 73.9 %copy-start.42 = (f32[64]{0:T(128)}, f32[64]{0:T(128)S(1)}, u32[]{:S(2)}) copy-start(f32[64]{0:T(128)S(1)} %convert_element_type.252) | copy-start | bytes 772
  44.7 35.7 %copy-start.43 = (f32[64]{0:T(128)}, f32[64]{0:T(128)S(1)}, u32[]{:S(2)}) copy-start(f32[64]{0:T(128)S(1)} %convert_element_type.256) | copy-start | bytes 772
  45.9 70.6 %copy-start.35 = (f32[128]{0:T(128)}, f32[128]{0:T(128)S(1)}, u32[]{:S(2)}) copy-start(f32[128]{0:T(128)S(1)} %add_rsqrt_fusion.3) | copy-start | bytes 1540
  46.6 70.7 %copy-start.24 = (f32[128,32]{0,1:T(8,128)}, f32[128,32]{0,1:T(8,128)S(1)}, u32[]{:S(2)}) copy-start(f32[128,32]{0,1:T(8,128)S(1)} %get-tuple-element.552) | copy-start | bytes 49156
  48.3 65.8 %copy-start.13 = (f32[128,512]{1,0:T(8,128)}, f32[128,512]{1,0:T(8,128)S(1)}, u32[]{:S(2)}) copy-start(f32[128,512]{1,0:T(8,128)S(1)} %fusion.63) | copy-start | bytes 786436
  48.5 65.7 %copy-start.11 = (f32[128,512]{0,1:T(8,128)}, f32[128,512]{0,1:T(8,128)S(1)}, u32[]{:S(2)}) copy-start(f32[128,512]{0,1:T(8,128)S(1)} %copy.148) | copy-start | bytes 786436
  116.2 20.6 %copy-start.9 = (f32[128,1024]{1,0:T(8,128)}, f32[128,1024]{1,0:T(8,128)S(1)}, u32[]{:S(2)}) copy-start(f32[128,1024]{1,0:T(8,128)S(1)} %fusion.65) | copy-start | bytes 1572868
  116.5 22.3 %copy-start.3 = (f32[128,1024]{0,1:T(8,128)}, f32[128,1024]{0,1:T(8,128)S(1)}, u32[]{:S(2)}) copy-start(f32[128,1024]{0,1:T(8,128)S(1)} %copy.147) | copy-start | bytes 1572868
  136.8 110.5 %all-gather.17.cloned.1.call-start = ((), (), s32[]{:S(2)}) async-start(), calls=%async_computation.16 | async-start | bytes 2228224 | tf_op jit(solution)/shard_map/all_gather | solution.py:113
  137.4 127.7 %all-gather.19.cloned.1.call-start = ((), (), s32[]{:S(2)}) async-start(), calls=%async_computation.17 | async-start | bytes 10027008 | tf_op jit(solution)/shard_map/all_gather | solution.py:115
  138.0 186.9 %all-gather.21.cloned.1.call-start = ((), (), s32[]{:S(2)}) async-start(), calls=%async_computation.18 | async-start | bytes 10027008 | tf_op jit(solution)/shard_map/all_gather | solution.py:116
  138.7 247.7 %all-gather.23.cloned.1.call-start = ((), (), s32[]{:S(2)}) async-start(), calls=%async_computation.19 | async-start | bytes 10027008 | tf_op jit(solution)/shard_map/all_gather | solution.py:117
  229.0 20.6 %copy-start.46 = (s32[16]{0:T(128)}, s32[16]{0:T(128)S(1)}, u32[]{:S(2)}) copy-start(s32[16]{0:T(128)S(1)} %get-tuple-element.903) | copy-start | bytes 196
  231.3 15.5 %all-to-all-start.1 = ((bf16[8,2,8192]{2,1,0:T(2,128)(2,1)}), bf16[8,2,8192]{2,1,0:T(2,128)(2,1)S(1)}, u32[]{:S(2)}, u32[]{:S(2)}) async-start(bf16[8,2,8192]{2,1,0:T(2,128)(2,1)} %reshape.443), calls=%async_computation.1 | async-start | bytes 524288 | tf_op jit(solution)/shard_map/all_to_all | solution.py:203
  247.2 24.3 %copy-start.15 = (bf16[128,8,1,128]{0,3,1,2:T(8,128)(2,1)}, bf16[128,8,1,128]{0,3,1,2:T(8,128)(2,1)S(1)}, u32[]{:S(2)}) copy-start(bf16[128,8,1,128]{0,3,1,2:T(8,128)(2,1)S(1)} %copy.154) | copy-start | bytes 786436
  249.5 15.6 %copy-start.40 = (f32[128]{0:T(128)}, f32[128]{0:T(128)S(1)}, u32[]{:S(2)}) copy-start(f32[128]{0:T(128)S(1)} %add_rsqrt_fusion.2) | copy-start | bytes 1540
  271.6 114.8 %copy-start.21 = (bf16[128,1024]{1,0:T(8,128)(2,1)S(1)}, bf16[128,1024]{1,0:T(8,128)(2,1)}, u32[]{:S(2)}) copy-start(bf16[128,1024]{1,0:T(8,128)(2,1)} %param.24) | copy-start | bytes 786436
  395.3 7.7 copy-start.8
  407.0 26.0 %copy-start.5 = (f32[128,1024]{1,0:T(8,128)}, f32[128,1024]{1,0:T(8,128)S(1)}, u32[]{:S(2)}) copy-start(f32[128,1024]{1,0:T(8,128)S(1)} %multiply_add_fusion) | copy-start | bytes 1572868
  407.0 26.0 %copy-start.47 = (s32[16]{0:T(128)S(1)}, s32[16]{0:T(128)}, u32[]{:S(2)}) copy-start(s32[16]{0:T(128)} %copy-done.46) | copy-start | bytes 196
  408.6 16.1 %all-to-all-start.2 = ((bf16[128,8,128]{2,0,1:T(8,128)(2,1)}), bf16[128,8,128]{2,0,1:T(8,128)(2,1)}, u32[]{:S(2)}, u32[]{:S(2)}) async-start(bf16[128,8,128]{2,0,1:T(8,128)(2,1)} %bitcast.252), calls=%async_computation.2 | async-start | bytes 524288 | tf_op jit(solution)/shard_map/all_to_all | solution.py:249
  415.4 369.1 %reduce-scatter.9.cloned.1.call-start = ((), (), s32[]{:S(2)}) async-start(), calls=%async_computation.20 | async-start | bytes 4456448 | tf_op jit(solution)/shard_map/reduce_scatter | solution.py:303
  520.1 339.7 %reduce-scatter.17.cloned.1.call-start = ((), (), s32[]{:S(2)}) async-start(), calls=%async_computation.24 | async-start | bytes 2228224 | tf_op jit(solution)/shard_map/reduce_scatter | solution.py:360
  787.2 27.7 %copy-start.25 = (f32[128,32]{0,1:T(8,128)S(1)}, f32[128,32]{0,1:T(8,128)}, u32[]{:S(2)}) copy-start(f32[128,32]{0,1:T(8,128)} %copy-done.24) | copy-start | bytes 49156
  788.5 27.2 %copy-start.12 = (f32[128,512]{0,1:T(8,128)S(1)}, f32[128,512]{0,1:T(8,128)}, u32[]{:S(2)}) copy-start(f32[128,512]{0,1:T(8,128)} %copy-done.11) | copy-start | bytes 786436
  789.4 16.8 %all-to-all-start.3 = ((bf16[8,2,16384]{2,1,0:T(2,128)(2,1)}), bf16[8,2,16384]{2,1,0:T(2,128)(2,1)}, u32[]{:S(2)}, u32[]{:S(2)}) async-start(bf16[8,2,16384]{2,1,0:T(2,128)(2,1)} %reshape.445), calls=%async_computation.4 | async-start | bytes 1048576 | tf_op jit(solution)/shard_map/all_to_all | solution.py:313
  795.9 23.1 %copy-start.14 = (f32[128,512]{1,0:T(8,128)S(1)}, f32[128,512]{1,0:T(8,128)}, u32[]{:S(2)}) copy-start(f32[128,512]{1,0:T(8,128)} %copy-done.13) | copy-start | bytes 786436
  795.9 117.2 %reduce-scatter.13.cloned.1.call-start = ((), (), s32[]{:S(2)}) async-start(), calls=%async_computation.22 | async-start | bytes 1114112 | tf_op jit(solution)/shard_map/reduce_scatter | solution.py:354
  814.9 10.5 copy-start.19
  820.8 11.6 copy-start.17
  820.8 11.6 copy-start.4
  823.0 152.5 %reduce-scatter.15.cloned.1.call-start = ((), (), s32[]{:S(2)}) async-start(), calls=%async_computation.23 | async-start | bytes 1114112 | tf_op jit(solution)/shard_map/reduce_scatter | solution.py:357
  825.4 214.5 %reduce-scatter.11.cloned.1.call-start = ((), (), s32[]{:S(2)}) async-start(), calls=%async_computation.21 | async-start | bytes 2228224 | tf_op jit(solution)/shard_map/reduce_scatter | solution.py:351
  840.8 276.0 %reduce-scatter.19.cloned.1.call-start = ((), (), s32[]{:S(2)}) async-start(), calls=%async_computation.25 | async-start | bytes 10027008 | tf_op jit(solution)/shard_map/reduce_scatter | solution.py:234
  847.2 347.5 %reduce-scatter.21.cloned.1.call-start = ((), (), s32[]{:S(2)}) async-start(), calls=%async_computation.26 | async-start | bytes 10027008 | tf_op jit(solution)/shard_map/reduce_scatter | solution.py:237
  853.7 418.6 %reduce-scatter.23.cloned.1.call-start = ((), (), s32[]{:S(2)}) async-start(), calls=%async_computation.27 | async-start | bytes 10027008 | tf_op jit(solution)/shard_map/reduce_scatter | solution.py:240
  859.7 532.9 %all-reduce.14.cloned.1.call-start = ((), (), s32[]{:S(2)}) async-start(), calls=%async_computation.28 | async-start | bytes 4325376 | tf_op jit(solution)/shard_map/psum | solution.py:368
  1273.5 8.6 copy-start.18
  1392.6 8.0 copy-start.34
  1392.6 8.7 copy-start.33
  (22 other events, 85.6 us)
Sparse Core Ops, SparseCore 0:
  9.7 34.3 all-gather.10
  45.9 32.4 all-gather.12
  80.1 33.9 all-gather.8
  136.9 33.6 all-gather.14
  172.2 33.9 all-gather.16
  207.7 57.3 all-gather.18
  266.8 57.9 all-gather.20
  326.5 59.8 all-gather.22
  520.2 264.2 reduce-scatter.8
  786.7 63.2 reduce-scatter.16
  853.0 60.1 reduce-scatter.12
  915.5 60.0 reduce-scatter.14
  978.0 61.8 reduce-scatter.10
  1042.1 74.5 reduce-scatter.18
  1119.0 75.6 reduce-scatter.20
  1197.0 75.2 reduce-scatter.22
  1275.3 117.2 all-reduce.13
where the time goes:
time: 1420 us; the launch traced here: 1410 us
  waiting for transfers between devices  966 us (68%)
  matrix products  123 us (9%)
  blocking collectives  102 us (7%)
  local copies, waits for them, and re-layouts  97.7 us (7%)
  other arithmetic  46.3 us (3%)
  loops' own time  34.1 us (2%)
  starting transfers between devices  21.2 us (1%)
  between operations  19.1 us (1%)
    reduce_scatter x1, waiting for transfers between devices, local(): lax.psum_scatter(kv_terms.reshape(total_rows, groups, 2 * HD).astype(jnp....  261 us
    reduce_scatter x1, waiting for transfers between devices, local(): lax.psum_scatter(up_term.astype(jnp.bfloat16), 'fsdp', scatter_dimension=...  77.9 us
    reduce_scatter x1, waiting for transfers between devices, local(): lax.psum_scatter(down_term.astype(jnp.bfloat16), 'fsdp', scatter_dimensio...  77.6 us
    reduce_scatter x1, waiting for transfers between devices, local(): lax.psum_scatter(gate_term.astype(jnp.bfloat16), 'fsdp', scatter_dimensio...  76.9 us
    reduce_scatter x1, waiting for transfers between devices, local(): lax.psum_scatter(query_term.astype(jnp.bfloat16), 'fsdp', scatter_dimensi...  64.3 us
    reduce_scatter x1, waiting for transfers between devices, local(): lax.psum_scatter(value_term.astype(jnp.bfloat16), 'fsdp', scatter_dimensi...  62.4 us
    unnamed x2, blocking collectives  57.2 us
    all_gather x1, waiting for transfers between devices, local(): lax.all_gather(down_weight, 'fsdp', axis=0, tiled=True)  55 us
  transfers between devices with their start and end apart: 20, of which 17 were waited for; matrix products, arithmetic and copies ran while one was open for 11% of the time, Pallas kernels for 0%

commit v1 on v0

v1 whole, which is shorter than its diff:
```python
import functools
import math

import jax
import jax.numpy as jnp
from jax import lax
from jax.experimental import pallas as pl
from jax.experimental.pallas import tpu as pltpu
from jax.sharding import PartitionSpec as P

H = 16
KVH = 8
HD = 64
DOCS = 4
EPSILON = 1e-06
THETA = 1000000.0
LOG2E = math.log2(math.e)
F32 = jnp.float32
BF16 = jnp.bfloat16
TILE = 512
KEYS = 512
VMEM = 56 * 1024 * 1024
PIECE = 48


def rms_scale(values):
    return lax.rsqrt(jnp.mean(values * values, axis=-1, keepdims=True) + EPSILON)


def norm_back(values, inverse, gain, grad):
    normalized = values * inverse
    gain_term = jnp.sum(grad * normalized, axis=tuple(range(grad.ndim - 1)))
    weighted = grad * gain
    inner = jnp.mean(weighted * normalized, axis=-1, keepdims=True)
    return (gain_term, inverse * (weighted - normalized * inner))


def doc_starts(segments):
    labels = jnp.arange(DOCS, dtype=jnp.int32)
    member = (segments[None, :] == labels[:, None]).astype(jnp.int32)
    lengths = jnp.sum(member, axis=1)
    return jnp.cumsum(lengths) - lengths


def rotate(values, cosine, sine):
    half = values.shape[-1] // 2
    first, second = values[..., :half], values[..., half:]
    return jnp.concatenate(
        [first * cosine - second * sine, second * cosine + first * sine], axis=-1
    )


def dot_nt(a, b):
    return lax.dot_general(a, b, (((1,), (1,)), ((), ())), preferred_element_type=F32)


def dot_tn(a, b):
    return lax.dot_general(a, b, (((0,), (0,)), ((), ())), preferred_element_type=F32)


def dot_nn(a, b):
    return jnp.dot(a, b, preferred_element_type=F32)


def key_loops(ranges_ref, tile, step):
    low, inner_low, inner_high, high = [ranges_ref[i, tile] for i in range(4)]

    def masked(block, _):
        step(block, True)
        return 0

    def plain(block, _):
        step(block, False)
        return 0

    lax.fori_loop(low, inner_low, masked, 0)
    lax.fori_loop(inner_low, inner_high, plain, 0)
    lax.fori_loop(inner_high, high, masked, 0)


def forward_kernel(ranges_ref, shift_ref, query_ref, first_ref, kv_ref, sums_ref, totals_ref, total):
    tile = pl.program_id(0)
    rows = query_ref.shape[1]
    query = query_ref[...].reshape(2 * rows, 2 * HD)
    first = jnp.concatenate([first_ref[...]] * 2, axis=0)
    index = ranges_ref[4, tile] + lax.broadcasted_iota(jnp.int32, (rows, 1), 0)
    index = jnp.concatenate([index, index], axis=0)
    shift = shift_ref[0]
    ones = jnp.ones((KEYS, 2 * HD), BF16)
    total[...] = jnp.zeros_like(total)

    def step(block, masked):
        start = pl.multiple_of(block * KEYS, KEYS)
        kv = kv_ref[pl.ds(start, KEYS), :]
        exps = jnp.exp2(dot_nt(query, kv) * (LOG2E * HD**-0.5) - shift)
        if masked:
            keys = start + lax.broadcasted_iota(jnp.int32, (2 * rows, KEYS), 1)
            exps = jnp.where((keys >= first) & (keys <= index), exps, 0.0)
        total[...] += dot_nn(exps.astype(BF16), jnp.concatenate([kv, ones], axis=1))

    key_loops(ranges_ref, tile, step)
    sums_ref[...] = total[:, : 2 * HD].reshape(2, rows, 2 * HD)
    totals_ref[...] = total[:, 2 * HD :].reshape(2, rows, 2 * HD)


def forward_attention(ranges, shift, query, first, kv):
    rows = query.shape[1]
    tiles = rows // TILE
    whole = lambda t, *_: (0, 0)
    part = lambda t, *_: (0, t, 0)
    return pl.pallas_call(
        forward_kernel,
        grid_spec=pltpu.PrefetchScalarGridSpec(
            num_scalar_prefetch=2,
            grid=(tiles,),
            in_specs=[
                pl.BlockSpec((2, TILE, 2 * HD), part),
                pl.BlockSpec((TILE, 1), lambda t, *_: (t, 0)),
                pl.BlockSpec(kv.shape, whole),
            ],
            out_specs=[
                pl.BlockSpec((2, TILE, 2 * HD), part),
                pl.BlockSpec((2, TILE, 2 * HD), part),
            ],
            scratch_shapes=[pltpu.VMEM((2 * TILE, 4 * HD), F32)],
        ),
        out_shape=[jax.ShapeDtypeStruct(query.shape, F32)] * 2,
        compiler_params=pltpu.CompilerParams(vmem_limit_bytes=VMEM),
        cost_estimate=pl.CostEstimate(
            flops=8 * 10**9, bytes_accessed=8 * 10**6, transcendentals=16 * 10**6
        ),
        name="attention_forward",
    )(ranges, shift, query, first, kv)


def backward_kernel(
    ranges_ref, shift_ref, query_ref, grad_ref, delta_ref, first_ref, kv_ref, gq_ref, gkv_ref, total
):
    tile = pl.program_id(0)
    rows = query_ref.shape[1]
    query = query_ref[...].reshape(2 * rows, 2 * HD)
    grad = grad_ref[...].reshape(2 * rows, 2 * HD)
    delta = delta_ref[...].reshape(1, 2 * rows)
    first = first_ref[...].reshape(1, 2 * rows)
    index = ranges_ref[4, tile] + lax.broadcasted_iota(jnp.int32, (1, rows), 1)
    index = jnp.concatenate([index, index], axis=1)
    shift = shift_ref[0]

    @pl.when(tile == 0)
    def _():
        total[...] = jnp.zeros_like(total)

    gq_ref[...] = jnp.zeros_like(gq_ref)

    def step(block, masked):
        start = pl.multiple_of(block * KEYS, KEYS)
        kv = kv_ref[pl.ds(start, KEYS), :]
        exps = jnp.exp2(dot_nt(kv, query) * (LOG2E * HD**-0.5) - shift)
        if masked:
            keys = start + lax.broadcasted_iota(jnp.int32, (KEYS, 2 * rows), 0)
            exps = jnp.where((keys >= first) & (keys <= index), exps, 0.0)
        scores = (exps * (dot_nt(kv, grad) - delta)).astype(BF16)
        gq_ref[...] += dot_tn(scores, kv).reshape(gq_ref.shape)
        total[pl.ds(start, KEYS), :] += dot_nn(scores, query) * HD**-0.5 + dot_nn(
            exps.astype(BF16), grad
        )

    key_loops(ranges_ref, tile, step)

    @pl.when(tile == pl.num_programs(0) - 1)
    def _():
        gkv_ref[...] = total[...].astype(BF16)


def backward_attention(ranges, shift, query, grad, delta, first, kv):
    rows = query.shape[1]
    tiles = rows // TILE
    whole = lambda t, *_: (0, 0)
    part = lambda t, *_: (0, t, 0)
    row = lambda t, *_: (t, 0, 0)
    return pl.pallas_call(
        backward_kernel,
        grid_spec=pltpu.PrefetchScalarGridSpec(
            num_scalar_prefetch=2,
            grid=(tiles,),
            in_specs=[
                pl.BlockSpec((2, TILE, 2 * HD), part),
                pl.BlockSpec((2, TILE, 2 * HD), part),
                pl.BlockSpec((1, 1, 2 * TILE), row),
                pl.BlockSpec((1, 1, 2 * TILE), row),
                pl.BlockSpec(kv.shape, whole),
            ],
            out_specs=[
                pl.BlockSpec((2, TILE, 2 * HD), part),
                pl.BlockSpec(kv.shape, whole),
            ],
            scratch_shapes=[pltpu.VMEM(kv.shape, F32)],
        ),
        out_shape=[
            jax.ShapeDtypeStruct(query.shape, F32),
            jax.ShapeDtypeStruct(kv.shape, BF16),
        ],
        compiler_params=pltpu.CompilerParams(vmem_limit_bytes=VMEM),
        cost_estimate=pl.CostEstimate(
            flops=20 * 10**9, bytes_accessed=16 * 10**6, transcendentals=16 * 10**6
        ),
        name="attention_backward",
    )(ranges, shift, query, grad, delta, first, kv)


MESH = pl.DeviceIdType.MESH
HBM = pl.BlockSpec(memory_space=pl.ANY)
IN_VMEM = pl.BlockSpec(memory_space=pltpu.VMEM)
RING = 8


def pair_of(value):
    return value + 1 - 2 * lax.rem(value, 2)


def ring_step(index, steps):
    return lax.div(index, RING) * RING + lax.rem(lax.rem(index, RING) + 2 * steps, RING)


class Copies:
    def __init__(self, send, recv, local):
        self.send, self.recv, self.local = send, recv, local
        self.started, self.locals = [], []

    def remote(self, src, dst, peer):
        i = len(self.started)
        copy = pltpu.make_async_remote_copy(
            src_ref=src,
            dst_ref=dst,
            send_sem=self.send.at[i],
            recv_sem=self.recv.at[i],
            device_id=peer,
            device_id_type=MESH,
        )
        copy.start()
        self.started.append(copy)
        return copy

    def here(self, src, dst):
        copy = pltpu.make_async_copy(src, dst, self.local.at[len(self.locals)])
        copy.start()
        self.locals.append(copy)
        return copy

    def finish(self):
        for copy in self.started:
            copy.wait_send()


def greet(peers):
    barrier = pltpu.get_barrier_semaphore()
    for peer in peers:
        pl.semaphore_signal(barrier, inc=1, device_id=peer, device_id_type=MESH)
    pl.semaphore_wait(barrier, len(peers))


def slot(ref, axis, size, index, split=None, half=0):
    start = index * size
    where = [pl.ds(0, n) for n in ref.shape]
    where[axis] = pl.ds(pl.multiple_of(start, 16), size)
    if split is not None:
        along, cut = split
        whole = size if along == axis else ref.shape[along]
        base = start if along == axis else 0
        begin, count = (0, cut) if half == 0 else (cut, whole - cut)
        offset = base + begin
        where[along] = pl.ds(pl.multiple_of(offset, 16) if along == axis else offset, count)
    return ref.at[tuple(where)]


def gather_stages(copies, src, out, axis, size, split, me, pair, device, sibling):
    plus, minus = ring_step(me, 1), ring_step(me, 3)
    at = functools.partial(slot, out, axis, size)
    halves = lambda index, half: at(index, split, half)
    to_sibling = []

    def pass_on(index):
        if sibling is not None:
            to_sibling.append(copies.remote(at(index), at(index), device(sibling)))

    kept = copies.here(src, at(me))
    first = copies.remote(src, at(me), device(pair))
    up = copies.remote(src, at(me), device(plus))
    down = copies.remote(src, at(me), device(minus))
    if sibling is not None:
        to_sibling.append(copies.remote(src, at(me), device(sibling)))
    yield
    up.wait_recv()
    far = [copies.remote(halves(minus, 0), halves(minus, 0), device(plus))]
    pass_on(minus)
    down.wait_recv()
    far.append(copies.remote(halves(plus, 1), halves(plus, 1), device(minus)))
    pass_on(plus)
    yield
    first.wait_recv()
    up = copies.remote(at(pair), at(pair), device(plus))
    down = copies.remote(at(pair), at(pair), device(minus))
    pass_on(pair)
    yield
    shift = pair - me
    up.wait_recv()
    last = [copies.remote(halves(minus + shift, 0), halves(minus + shift, 0), device(plus))]
    pass_on(minus + shift)
    down.wait_recv()
    last.append(copies.remote(halves(plus + shift, 1), halves(plus + shift, 1), device(minus)))
    pass_on(plus + shift)
    yield
    opposite = ring_step(me, 2)
    for copy in far:
        copy.wait_recv()
    pass_on(opposite)
    yield
    for copy in last:
        copy.wait_recv()
    pass_on(opposite + shift)
    yield
    for copy in to_sibling:
        copy.wait_recv()
    kept.wait()


def run_stages(stages):
    live = list(stages)
    while live:
        live = [stage for stage in live if next(stage, stage) is not stage]


class Places:
    def __init__(self):
        self.seq, self.fsdp = lax.axis_index("seq"), lax.axis_index("fsdp")
        self.core = lax.rem(self.fsdp, 2)
        self.chip = lax.div(self.fsdp, 2)
        self.row = lax.div(self.chip, 4)
        self.col = lax.rem(self.chip, 4)
        self.sibling = pair_of(self.fsdp)
        self.across = lax.rem(self.fsdp + 8, 16)

    def on_seq(self, index):
        return (index, self.fsdp)

    def on_fsdp(self, index):
        return (self.seq, index)

    def other_seq(self, step):
        return lax.rem(self.seq + step, 8)

    def other_chip(self, step):
        return lax.rem(self.row + step // 4, 2) * 4 + lax.rem(self.col + step % 4, 4)

    def gather_peers(self):
        seq = [pair_of(self.seq), ring_step(self.seq, 1), ring_step(self.seq, 3)]
        fsdp = [self.across, ring_step(self.fsdp, 1), ring_step(self.fsdp, 3), self.sibling]
        return [self.on_seq(i) for i in seq] + [self.on_fsdp(i) for i in fsdp]

    def scatter_peers(self):
        seq = [self.on_seq(self.other_seq(d)) for d in range(1, 8)]
        fsdp = [self.on_fsdp(self.other_chip(d) * 2 + self.core) for d in range(1, 8)]
        return seq + fsdp + [self.on_fsdp(self.sibling)]


def params(name_id):
    return pltpu.CompilerParams(
        collective_id=name_id, has_side_effects=True, vmem_limit_bytes=VMEM
    )


def semaphores(remote, local):
    return [
        pltpu.SemaphoreType.DMA((remote,)),
        pltpu.SemaphoreType.DMA((remote,)),
        pltpu.SemaphoreType.DMA((local,)),
    ]


def seq_gather(copies, places, src, out, axis, split):
    size = src.shape[axis]
    return gather_stages(
        copies, src, out, axis, size, split, places.seq, pair_of(places.seq), places.on_seq, None
    )


def fsdp_gather(copies, places, src, out, axis, split):
    size = src.shape[axis]
    return gather_stages(
        copies, src, out, axis, size, split, places.fsdp, places.across, places.on_fsdp, places.sibling
    )


def gather(name, name_id, seq_items, fsdp_items):
    items = seq_items + fsdp_items
    count = len(items)

    def kernel(*refs):
        srcs, outs = refs[:count], refs[count : 2 * count]
        copies, places = Copies(*refs[2 * count :]), Places()
        greet(places.gather_peers())
        stages = []
        for i, (_, axis, split) in enumerate(items):
            make = seq_gather if i < len(seq_items) else fsdp_gather
            stages.append(make(copies, places, srcs[i], outs[i], axis, split))
        run_stages(stages)
        copies.finish()

    shapes = []
    for i, (array, axis, _) in enumerate(items):
        shape = list(array.shape)
        shape[axis] *= 8 if i < len(seq_items) else 16
        shapes.append(jax.ShapeDtypeStruct(tuple(shape), array.dtype))
    return pl.pallas_call(
        kernel,
        out_shape=shapes,
        in_specs=[HBM] * count,
        out_specs=[HBM] * count,
        scratch_shapes=semaphores(9 * len(seq_items) + 17 * len(fsdp_items), count),
        compiler_params=params(name_id),
        name=name,
    )(*[item[0] for item in items])


class SeqSum:
    def __init__(self, copies, places, part, held):
        self.held = held
        self.kept = copies.here(part.at[places.seq], held.at[0])
        self.copies = []
        for d in (4, 3, 5, 2, 6, 1, 7):
            peer = places.other_seq(d)
            self.copies.append(copies.remote(part.at[peer], held.at[d], places.on_seq(peer)))

    def total(self):
        self.kept.wait()
        for copy in self.copies:
            copy.wait_recv()
        total = self.held[0].astype(F32)
        for d in range(1, 8):
            total += self.held[d].astype(F32)
        return total


class FsdpSum:
    def __init__(self, copies, places, part, mine, theirs, held):
        self.remote, self.places = copies.remote, places
        self.mine, self.theirs, self.held = mine, theirs, held
        self.other = copies.remote(
            part.at[:, 1 - places.core], theirs, places.on_fsdp(places.sibling)
        )
        self.kept = copies.here(part.at[:, places.core], mine)

    def send(self):
        self.kept.wait()
        self.other.wait_recv()
        self.copies = []
        for d in (2, 6, 4, 5, 7, 1, 3):
            chip = self.places.other_chip(d)
            self.mine[chip] = (
                self.mine[chip].astype(F32) + self.theirs[chip].astype(F32)
            ).astype(BF16)
            peer = self.places.on_fsdp(chip * 2 + self.places.core)
            self.copies.append(self.remote(self.mine.at[chip], self.held.at[d], peer))

    def total(self):
        chip = self.places.chip
        total = self.mine[chip].astype(F32) + self.theirs[chip].astype(F32)
        for copy in self.copies:
            copy.wait_recv()
        for d in range(1, 8):
            total += self.held[d].astype(F32)
        return total


def fsdp_buffers(shape):
    return [pltpu.VMEM((8,) + shape, BF16)] * 3


def unit_rows(values):
    return lax.rsqrt(jnp.mean(values * values, axis=-1, keepdims=True) + EPSILON)


def hidden_kernel(
    part, h1, dy, gain, wo, gate, up, down,
    gh1_ref, gb_ref, term_ref, go_ref, gate_out, up_out, down_out,
    held, go_own, b0, b1, b2, b3, b4, b5, b6, b7, b8, send, recv, local_sem,
):
    copies, places = Copies(send, recv, local_sem), Places()
    greet(places.scatter_peers())
    hidden = SeqSum(copies, places, part, held)
    sums = [
        FsdpSum(copies, places, gate, b0, b1, b2),
        FsdpSum(copies, places, up, b3, b4, b5),
        FsdpSum(copies, places, down, b6, b7, b8),
    ]
    for item in sums:
        item.send()
    gn2 = hidden.total()
    value = h1[...]
    inverse = unit_rows(value)
    normed = value * inverse
    term_ref[...] = jnp.sum(gn2 * normed, axis=0, keepdims=True)
    weighted = gn2 * gain[...]
    inner = jnp.mean(weighted * normed, axis=-1, keepdims=True)
    gh1 = dy[...].astype(F32) + inverse * (weighted - normed * inner)
    gh1_ref[...] = gh1
    gb_ref[...] = gh1.astype(BF16)

    def columns(j, _):
        begin = pl.multiple_of(j * 256, 256)
        go_own[:, pl.ds(begin, 256)] = dot_nt(gb_ref[...], wo[pl.ds(begin, 256), :]).astype(BF16)
        return 0

    lax.fori_loop(0, 4, columns, 0)
    rows = go_own.shape[0]
    mine = go_ref.at[pl.ds(pl.multiple_of(places.seq * rows, 16), rows), :]
    head = lambda index: go_own.at[:, pl.ds(pl.multiple_of(index * 128, 128), 128)]
    kept = copies.here(head(places.seq), mine)
    heads = []
    for d in (4, 3, 5, 2, 6, 1, 7):
        peer = places.other_seq(d)
        heads.append(copies.remote(head(peer), mine, places.on_seq(peer)))
    for item, out in zip(sums, (gate_out, up_out, down_out)):
        out[...] = item.total().astype(BF16)
    kept.wait()
    for copy in heads:
        copy.wait_recv()
    copies.finish()


def scatter_hidden(part, h1, dy, gain, wo, gate, up, down):
    rows, width = h1.shape
    shapes = [a.shape[2:] for a in (gate, up, down)]
    scratch = [pltpu.VMEM((8, rows, width), BF16), pltpu.VMEM((rows, width), BF16)]
    for shape in shapes:
        scratch += fsdp_buffers(shape)
    return pl.pallas_call(
        hidden_kernel,
        out_shape=[
            jax.ShapeDtypeStruct((rows, width), F32),
            jax.ShapeDtypeStruct((rows, width), BF16),
            jax.ShapeDtypeStruct((1, width), F32),
            jax.ShapeDtypeStruct((8 * rows, 128), BF16),
        ]
        + [jax.ShapeDtypeStruct(shape, BF16) for shape in shapes],
        in_specs=[HBM] + [IN_VMEM] * 4 + [HBM] * 3,
        out_specs=[IN_VMEM] * 3 + [HBM] + [IN_VMEM] * 3,
        scratch_shapes=scratch + semaphores(7 + 7 + 3 * 8, 5),
        compiler_params=params(4),
        name="scatter_hidden",
    )(part, h1, dy, gain, wo, gate, up, down)


def keys_kernel(
    branch, h1, gkv, gout, gate, up, down,
    layer_ref, gkv_out, gout_out, gate_all, up_all, down_all,
    held, b0, b1, b2, b3, b4, b5, send, recv, local_sem,
):
    copies, places = Copies(send, recv, local_sem), Places()
    greet(places.scatter_peers())
    sums = [FsdpSum(copies, places, gkv, b0, b1, b2), FsdpSum(copies, places, gout, b3, b4, b5)]
    hidden = SeqSum(copies, places, branch, held)
    stages = [
        seq_gather(copies, places, gate, gate_all, 0, (0, 32)),
        seq_gather(copies, places, up, up_all, 0, (0, 32)),
        seq_gather(copies, places, down, down_all, 0, (0, 16)),
    ]
    for stage in stages:
        next(stage)
    for item in sums:
        item.send()
    run_stages(stages)
    for item, out in zip(sums, (gkv_out, gout_out)):
        out[...] = item.total().astype(BF16)
    layer_ref[...] = (h1[...] + hidden.total()).astype(BF16)
    copies.finish()


def scatter_keys(branch, h1, gkv, gout, gate, up, down):
    rows, width = h1.shape
    shapes = [a.shape[2:] for a in (gkv, gout)]
    scratch = [pltpu.VMEM((8, rows, width), BF16)]
    for shape in shapes:
        scratch += fsdp_buffers(shape)
    wide = [jax.ShapeDtypeStruct((8 * a.shape[0],) + a.shape[1:], BF16) for a in (gate, up, down)]
    return pl.pallas_call(
        keys_kernel,
        out_shape=[jax.ShapeDtypeStruct((rows, width), BF16)]
        + [jax.ShapeDtypeStruct(shape, BF16) for shape in shapes]
        + wide,
        in_specs=[HBM, IN_VMEM] + [HBM] * 5,
        out_specs=[IN_VMEM] * 3 + [HBM] * 3,
        scratch_shapes=scratch + semaphores(7 + 2 * 8 + 27, 6),
        compiler_params=params(5),
        name="scatter_keys",
    )(branch, h1, gkv, gout, gate, up, down)


def input_kernel(
    part, tokens, gain, gh1, pack, gout,
    grad_ref, pack_all, gout_all,
    held, b0, b1, b2, small, send, recv, local_sem,
):
    copies, places = Copies(send, recv, local_sem), Places()
    greet(places.scatter_peers())
    packs = FsdpSum(copies, places, pack, b0, b1, b2)
    hidden = SeqSum(copies, places, part, held)
    packs.send()
    stages = [seq_gather(copies, places, gout, gout_all, 0, (0, 32))]
    next(stages[0])
    small[...] = packs.total().astype(BF16)
    stages.append(seq_gather(copies, places, small, pack_all, 0, (0, 48)))
    run_stages(stages)
    gn1 = hidden.total()
    value = tokens[...].astype(F32)
    inverse = unit_rows(value)
    normed = value * inverse
    weighted = gn1 * gain[...]
    inner = jnp.mean(weighted * normed, axis=-1, keepdims=True)
    grad_ref[...] = gh1[...] + inverse * (weighted - normed * inner)
    copies.finish()


def scatter_input(part, tokens, gain, gh1, pack, gout):
    rows, width = gh1.shape
    shape = pack.shape[2:]
    return pl.pallas_call(
        input_kernel,
        out_shape=[
            jax.ShapeDtypeStruct((rows, width), F32),
            jax.ShapeDtypeStruct((8 * shape[0], shape[1]), BF16),
            jax.ShapeDtypeStruct((8 * gout.shape[0], width), BF16),
        ],
        in_specs=[HBM] + [IN_VMEM] * 3 + [HBM] * 2,
        out_specs=[IN_VMEM] + [HBM] * 2,
        scratch_shapes=[pltpu.VMEM((8, rows, width), BF16)]
        + fsdp_buffers(shape)
        + [pltpu.VMEM(shape, BF16)]
        + semaphores(7 + 8 + 18, 4),
        compiler_params=params(6),
        name="scatter_input",
    )(part, tokens, gain, gh1, pack, gout)


def local(
    tokens,
    segments,
    cotangent,
    attention_gain,
    query_gain,
    key_gain,
    query_weight,
    key_weight,
    value_weight,
    out_weight,
    feedforward_gain,
    gate_weight,
    up_weight,
    down_weight,
):
    seq_count = lax.axis_size("seq")
    fsdp_count = lax.axis_size("fsdp")
    fsdp = lax.axis_index("fsdp")
    seq = lax.axis_index("seq")
    rows, width = tokens.shape
    block = rows * seq_count
    hidden = gate_weight.shape[1]
    part = hidden // seq_count
    per_head = (H // KVH) * HD
    block_start = fsdp * block
    take = lax.dynamic_slice_in_dim

    ratio = fsdp_count // seq_count
    pairs = [
        (
            f % seq_count * fsdp_count + ratio * s + f // (fsdp_count // ratio),
            s * fsdp_count + f,
        )
        for f in range(fsdp_count)
        for s in range(seq_count)
    ]
    back_pairs = [(b, a) for a, b in pairs]
    both = ("seq", "fsdp")

    gains = jnp.concatenate([attention_gain, feedforward_gain, query_gain, key_gain])
    heads_weight = jnp.concatenate(
        [
            take(query_weight, seq * per_head, per_head, 1),
            take(key_weight, seq * HD, HD, 1),
            take(value_weight, seq * HD, HD, 1),
        ],
        axis=1,
    )
    gains = jnp.pad(gains[None, :], ((0, 15), (0, heads_weight.shape[1] - gains.shape[0])))
    pieces = down_weight.shape[0] // seq_count
    down_piece = lax.ppermute(take(down_weight, seq * pieces, pieces, 0), both, pairs)
    down_piece = jnp.pad(down_piece, ((0, PIECE - pieces), (0, 0)))
    gate_up = jnp.stack(
        [take(gate_weight, seq * part, part, 1), take(up_weight, seq * part, part, 1)]
    )
    x_block, packs, wo = gather(
        "gather_inputs",
        1,
        [(tokens, 0, (0, 64))],
        [(jnp.concatenate([heads_weight, gains]), 0, (0, 48)), (out_weight, 0, (0, 32))],
    )
    packs = packs.reshape(fsdp_count, -1, packs.shape[1])
    heads_weight = packs[:, : width // fsdp_count].reshape(width, -1)
    gains = packs[:, width // fsdp_count].astype(F32)

    shard = width // fsdp_count
    gain_one = gains[:, :shard].reshape(width)
    gain_two = gains[:, shard : 2 * shard].reshape(width)
    qshard = HD // fsdp_count
    gain_q = gains[:, 2 * shard : 2 * shard + qshard].reshape(HD)
    gain_k = gains[:, 2 * shard + qshard : 2 * shard + 2 * qshard].reshape(HD)

    starts = doc_starts(segments)
    ids = take(segments, block_start, block)
    picked = (ids[:, None] == jnp.arange(DOCS, dtype=jnp.int32)[None, :]).astype(jnp.int32)
    first = jnp.sum(picked * starts[None, :], axis=1)
    index = block_start + jnp.arange(block, dtype=jnp.int32)
    freqs = THETA ** (-2.0 * jnp.arange(HD // 2, dtype=F32) / HD)
    angles = (index - first).astype(F32)[:, None] * freqs[None, :]
    cosine, sine = jnp.cos(angles), jnp.sin(angles)
    shift = (HD**0.5 * LOG2E) * jnp.max(jnp.abs(gain_q)) * jnp.max(jnp.abs(gain_k))
    shift = shift.reshape(1)

    tiles = block // TILE
    q_first = block_start + TILE * jnp.arange(tiles, dtype=jnp.int32)
    tile_first = first.reshape(tiles, TILE)
    low = tile_first[:, 0] // KEYS
    high = (q_first + TILE - 1) // KEYS + 1
    inner_low = jnp.minimum((tile_first[:, TILE - 1] + KEYS - 1) // KEYS, high)
    inner_high = jnp.maximum((q_first + 1) // KEYS, inner_low)
    ranges = jnp.stack([low, inner_low, inner_high, high, q_first])

    x = x_block.astype(F32)
    inverse_one = rms_scale(x)
    n1 = (x * inverse_one * gain_one).astype(BF16)
    pre = dot_nn(n1, heads_weight)
    qp = pre[:, :per_head].reshape(block, H // KVH, HD)
    kp = pre[:, per_head : per_head + HD]
    value = pre[:, per_head + HD :].astype(BF16)
    inverse_q = rms_scale(qp)
    inverse_k = rms_scale(kp)
    q = rotate(qp * inverse_q * gain_q, cosine[:, None, :], sine[:, None, :]).astype(BF16)
    k = rotate(kp * inverse_k * gain_k, cosine, sine).astype(BF16)
    q = jnp.transpose(q, (1, 0, 2))
    empty = jnp.zeros_like(q)
    q_pad = jnp.concatenate([q, empty], axis=2)
    dy_block, kv = gather(
        "gather_keys",
        2,
        [(cotangent, 0, (0, 64))],
        [(jnp.concatenate([k, value], axis=1), 0, (0, 512))],
    )

    sums, totals = forward_attention(ranges, shift, q_pad, first[:, None], kv)
    totals = totals[:, :, :1]
    o = sums[:, :, HD:] / totals
    ob = jnp.transpose(o.astype(BF16), (1, 0, 2)).reshape(block, per_head)
    ob_block, gate_up, down_w = gather(
        "gather_attended",
        3,
        [(ob, 1, (0, 512))],
        [(gate_up, 1, (1, 32)), (down_piece, 0, (0, 32))],
    )
    gate_w, up_w = gate_up[0], gate_up[1]
    down_w = down_w.reshape(fsdp_count, PIECE, width)[:, :pieces].reshape(part, width)

    h1 = x + dot_nn(ob_block, wo)
    inverse_two = rms_scale(h1)
    n2 = (h1 * inverse_two * gain_two).astype(BF16)
    gate = dot_nn(n2, gate_w)
    up = dot_nn(n2, up_w)
    sig = jax.nn.sigmoid(gate)
    act = (gate * sig * up).astype(BF16)
    gact = dot_nt(dy_block, down_w)
    ggate = (gact * up * sig * (1.0 + gate * (1.0 - sig))).astype(BF16)
    gup = (gact * gate * sig).astype(BF16)
    gn2_part = (dot_nt(ggate, gate_w) + dot_nt(gup, up_w)).astype(BF16)
    branch = dot_nn(act, down_w).astype(BF16)
    own = lambda array: take(array, seq * rows, rows)
    h1_own = own(h1)
    by_core = lambda array: array.reshape(8, 2, -1, array.shape[-1])
    g_down = dot_tn(act, dy_block).astype(BF16).reshape(fsdp_count, pieces, width)
    g_down = jnp.pad(g_down, ((0, 0), (0, PIECE - pieces), (0, 0)))
    gh1, gb, gain_two_term, go, g_gate, g_up, g_down = scatter_hidden(
        gn2_part.reshape(seq_count, rows, width),
        h1_own,
        cotangent,
        gain_two[None, :],
        wo,
        by_core(dot_tn(n2, ggate).astype(BF16)),
        by_core(dot_tn(n2, gup).astype(BF16)),
        by_core(g_down.reshape(-1, width)),
    )
    g_down = lax.ppermute(g_down, both, back_pairs)
    g_out = dot_tn(own(ob_block), gb).astype(BF16)
    go = jnp.transpose(go.reshape(block, H // KVH, HD), (1, 0, 2)).astype(F32)
    ga = (go / totals).astype(BF16)
    ga_pad = jnp.concatenate([empty, ga], axis=2)
    delta = jnp.sum(go * o, axis=2) / totals[:, :, 0]

    tiled = lambda a: jnp.transpose(a.reshape(2, tiles, TILE), (1, 0, 2)).reshape(tiles, 1, 2 * TILE)
    gq, gkv = backward_attention(
        ranges,
        shift,
        q_pad,
        ga_pad,
        tiled(delta),
        tiled(jnp.stack([first, first])),
        kv,
    )
    layer_out, gkv, g_out, g_gate, g_up, g_down = scatter_keys(
        branch.reshape(seq_count, rows, width),
        h1_own,
        by_core(gkv),
        by_core(g_out),
        g_gate,
        g_up,
        g_down,
    )
    gq = jnp.transpose((gq[:, :, :HD] * HD**-0.5).astype(BF16), (1, 0, 2)).astype(F32)
    gk = gkv[:, :HD].astype(F32)
    gv = gkv[:, HD:]
    gain_q_term, gqp = norm_back(
        qp, inverse_q, gain_q, rotate(gq, cosine[:, None, :], -sine[:, None, :])
    )
    gain_k_term, gkp = norm_back(kp, inverse_k, gain_k, rotate(gk, cosine, -sine))
    gpre = jnp.concatenate(
        [gqp.reshape(block, per_head).astype(BF16), gkp.astype(BF16), gv], axis=1
    )
    gn1_partial = dot_nt(gpre, heads_weight)
    gain_one_term = jnp.sum(gn1_partial * (x * inverse_one), axis=0)
    g_heads = dot_tn(n1, gpre).astype(BF16).reshape(fsdp_count, shard, -1)
    terms = jnp.concatenate(
        [
            gain_one_term.reshape(fsdp_count, shard),
            gain_two_term.reshape(fsdp_count, shard),
            gain_q_term.reshape(fsdp_count, qshard),
            gain_k_term.reshape(fsdp_count, qshard),
        ],
        axis=1,
    ).astype(BF16)
    terms = jnp.pad(terms[:, None, :], ((0, 0), (0, 15), (0, g_heads.shape[2] - terms.shape[1])))
    pack = jnp.concatenate([g_heads, terms], axis=1)
    input_grad, packs, g_out = scatter_input(
        gn1_partial.astype(BF16).reshape(seq_count, rows, width),
        tokens,
        gain_one[None, :],
        gh1,
        pack.reshape((8, 2) + pack.shape[1:]),
        g_out,
    )
    packs = packs.reshape((seq_count,) + pack.shape[1:])
    g_heads = packs[:, :shard]
    terms = jnp.sum(packs[:, shard].astype(F32), axis=0)
    g_out = jnp.sum(g_out.reshape(seq_count, shard, width).astype(F32), axis=0)
    g_down = g_down.reshape(seq_count, PIECE, width)[:, :pieces].reshape(-1, width)
    columns = lambda a: jnp.transpose(a.reshape(seq_count, shard, part), (1, 0, 2)).reshape(shard, hidden)

    g_query = jnp.transpose(g_heads[:, :, :per_head], (1, 0, 2)).reshape(shard, H * HD)
    g_key = jnp.transpose(g_heads[:, :, per_head : per_head + HD], (1, 0, 2)).reshape(shard, KVH * HD)
    g_value = jnp.transpose(g_heads[:, :, per_head + HD :], (1, 0, 2)).reshape(shard, KVH * HD)

    return (
        layer_out,
        input_grad,
        terms[:shard],
        terms[2 * shard : 2 * shard + qshard],
        terms[2 * shard + qshard : 2 * shard + 2 * qshard],
        g_query.astype(F32),
        g_key.astype(F32),
        g_value.astype(F32),
        g_out,
        terms[shard : 2 * shard],
        columns(g_gate).astype(F32),
        columns(g_up).astype(F32),
        g_down.astype(F32),
    )


def solution(mesh):
    rows = P(("fsdp", "seq"), None)
    matrix = P("fsdp", None)
    vector = P("fsdp")
    in_specs = (rows, P(), rows) + (vector,) * 3 + (matrix,) * 4 + (vector,) + (matrix,) * 3
    out_specs = (rows, rows) + (vector,) * 3 + (matrix,) * 4 + (vector,) + (matrix,) * 3
    return jax.shard_map(local, mesh=mesh, in_specs=in_specs, out_specs=out_specs, check_vma=False)
```

time: 1420 us -> 502 us (0.35)
  the two profiles are of different devices: /device:TPU:8 before, /device:TPU:50 now
where the time goes in v1:
time: 502 us; the launch traced here: 493 us
  Pallas kernels  360 us (72%)
  local copies, waits for them, and re-layouts  48 us (10%)
  matrix products  42.2 us (8%)
  other arithmetic  31.6 us (6%)
  starting transfers between devices  7.75 us (2%)
    pallas_call x3, Pallas kernels, gather(): pl.pallas_call(kernel, out_shape=shapes, in_specs=[HBM] * count, out_spec...  92.8 us
    pallas_call x1, Pallas kernels, scatter_keys(): pl.pallas_call(keys_kernel, out_shape=[jax.ShapeDtypeStruct((rows, width)...  88 us
    pallas_call x1, Pallas kernels, scatter_hidden(): pl.pallas_call(hidden_kernel, out_shape=[jax.ShapeDtypeStruct((rows, widt...  62 us
    pallas_call x1, Pallas kernels, scatter_input(): pl.pallas_call(input_kernel, out_shape=[jax.ShapeDtypeStruct((rows, width...  56.1 us
    pallas_call x1, Pallas kernels, backward_attention(): pl.pallas_call(backward_kernel, grid_spec=pltpu.PrefetchScalarGridSpec(nu...  40.9 us
    pallas_call x1, Pallas kernels, forward_attention(): pl.pallas_call(forward_kernel, grid_spec=pltpu.PrefetchScalarGridSpec(num...  20.4 us
    dot_general x5, matrix products, dot_nn(): return jnp.dot(a, b, preferred_element_type=F32)  14.6 us
    dot_general x5, matrix products, dot_tn(): lax.dot_general(a, b, (((0,), (0,)), ((), ())), preferred_element_type=F32)  13.9 us
  transfers between devices with their start and end apart: 2, of which 0 were waited for; matrix products, arithmetic and copies ran while one was open for 9% of the time, Pallas kernels for 24%

profile of v1, /device:TPU:50, one launch (start us, length us, event | category | flops | bytes accessed | tf_op | source)
XLA Modules:
  0.0 492.9 jit_solution(16500538911037342127)
XLA Ops:
  1.7 4.7 collective-permute-start
  6.5 1.1 convert_reduce_fusion.1
  11.6 28.1 %gather_inputs.1 = (bf16[1024,1024]{1,0:T(8,128)(2,1)}, bf16[1280,256]{1,0:T(8,128)(2,1)}, bf16[1024,1024]{1,0:T(8,128)(2,1)}) custom-call(bf16[128,1024]{1,0:T(8,128)(2,1)} %tokens.1, bf16[80,256]{1,0:T(8,128)(2,1)} %fusion.40.refs_1_, bf16[64,1024]{1,0:T(8,128)(2,1)} %refs_2_.1), custom_call_target="tpu_custom_call" | custom-call | tf_op jit(solution)/shard_map/gather_inputs/pallas_call | solution.py:414
  40.8 1.1 slice.155
  44.1 2.1 fusion.4
  53.2 3.1 fusion.25
  58.9 29.7 %gather_keys.1 = (bf16[1024,1024]{1,0:T(8,128)(2,1)}, bf16[16384,128]{1,0:T(8,128)(2,1)}) custom-call(bf16[128,1024]{1,0:T(8,128)(2,1)} %dy.1, bf16[1024,128]{1,0:T(8,128)(2,1)} %pad_maximum_fusion.4.refs_1_), custom_call_target="tpu_custom_call" | custom-call | tf_op jit(solution)/shard_map/gather_keys/pallas_call | solution.py:414
  89.3 20.4 %attention_forward.1 = (f32[2,1024,128]{2,1,0:T(8,128)}, f32[2,1024,128]{2,1,0:T(8,128)}) custom-call(s32[5,2]{1,0:T(8,128)} %stack.24.ranges_ref, f32[1]{0:T(128)} %bitcast.5.shift_ref, bf16[2,1024,128]{2,1,0:T(8,128)(2,1)} %concatenate.68.query_ref, s32[1024,1]{1,0:T(8,128)} %copy.148.first_ref, bf16[16384,128]{1,0:T(8,128)(2,1)} %get-tuple-element.43.kv_ref), custom_call_target="tpu_custom_call" | custom-call | flops 8000000000 | bytes 8000000 | tf_op jit(solution)/shard_map/attention_forward/pallas_call | solution.py:111
  109.6 1.6 slice_reduce_fusion
  111.2 1.8 convert_bitcast_fusion.3
  116.5 35.0 %gather_attended.1 = (bf16[1024,1024]{1,0:T(8,128)(2,1)}, bf16[2,1024,576]{2,1,0:T(8,128)(2,1)}, bf16[768,1024]{1,0:T(8,128)(2,1)}) custom-call(bf16[1024,128]{1,0:T(8,128)(2,1)} %copy.150.refs_0_, bf16[2,64,576]{2,1,0:T(8,128)(2,1)} %pad_maximum_fusion.7.refs_1_, bf16[48,1024]{1,0:T(8,128)(2,1)} %pad.19.refs_2_), custom_call_target="tpu_custom_call" | custom-call | tf_op jit(solution)/shard_map/gather_attended/pallas_call | solution.py:414
  151.5 1.4 slice.164
  152.9 1.6 reshape.627
  154.5 5.5 %multiply_reduce_fusion = (f32[1024]{0:T(1024)S(1)}, f32[1024,1024]{1,0:T(8,128)S(1)}) fusion(bf16[1024,1024]{1,0:T(8,128)(2,1)} %get-tuple-element.46, bf16[1024,1024]{1,0:T(8,128)(2,1)} %get-tuple-element.47.wo, bf16[1024,1024]{1,0:T(8,128)(2,1)} %get-tuple-element.41), kind=kOutput, calls=%fused_computation.10 | convolution fusion | flops 2151676928 | bytes 10489856 | tf_op jit(solution)/shard_map/dot_general | solution.py:62
  160.9 1.4 fusion.53
  162.7 2.1 copy-done.23
  164.8 1.5 fusion.6
  166.3 3.6 multiply_convert_fusion.1
  169.8 2.4 convolution_convert_fusion.4
  172.2 3.1 convolution_convert_fusion.1
  175.4 2.4 convolution_convert_fusion.3
  177.8 4.0 fusion.8
  181.8 1.4 reshape.632
  183.2 1.4 pad.20
  185.4 3.8 convolution_convert_fusion.2
  189.2 1.4 copy.152
  190.6 2.6 copy.153
  193.2 5.8 %add_convert_fusion = bf16[1024,1024]{1,0:T(8,128)(2,1)} fusion(f32[1024,1024]{1,0:T(8,128)} %fusion.8, bf16[1024,576]{0,1:T(8,128)(2,1)S(1)} %copy-done.25, bf16[2,1024,576]{2,1,0:T(8,128)(2,1)} %get-tuple-element.48), kind=kOutput, calls=%fused_computation.8 | convolution fusion | flops 1210056704 | bytes 8781824 | tf_op jit(solution)/shard_map/dot_general | solution.py:54
  198.9 62.0 %scatter_hidden.1 = (f32[128,1024]{1,0:T(8,128)}, bf16[128,1024]{1,0:T(8,128)(2,1)}, f32[1,1024]{1,0:T(1,128)}, bf16[1024,128]{1,0:T(8,128)(2,1)}, bf16[64,576]{...) custom-call(bf16[8,128,1024]{2,1,0:T(8,128)(2,1)} %bitcast.153, ...), custom_call_target="tpu_custom_call" | custom-call | tf_op jit(solution)/shard_map/scatter_hidden/pallas_call | solution.py:537
  260.9 3.2 convolution_convert_fusion
  264.1 3.0 collective-permute-start.1
  268.1 2.4 copy.155
  270.4 2.6 fusion.17
  273.7 2.1 concatenate.70.grad_ref
  275.8 40.9 %attention_backward.1 = (f32[2,1024,128]{2,1,0:T(8,128)}, bf16[16384,128]{1,0:T(8,128)(2,1)}) custom-call(s32[5,2]{1,0:T(8,128)} %stack.24.ranges_ref, f32[1]{0:T(128)} %bitcast.5.shift_ref, bf16[2,1024,128]{2,1,0:T(8,128)(2,1)} %concatenate.68.query_ref, bf16[2,1024,128]{2,1,0:T(8,128)(2,1)} %concatenate.70.grad_ref, f32[2,1,1024]{2,1,0:T(1,128)} %reshape.633.delta_ref, ...), custom_call_target="tpu_custom_call" | custom-call | flops 20000000000 | bytes 16000000 | tf_op jit(solution)/shard_map/attention_backward/pallas_call | solution.py:181
  316.7 1.4 convert_bitcast_fusion.2
  319.9 1.3 fusion.36
  321.4 88.0 %scatter_keys.1 = (bf16[128,1024]{1,0:T(8,128)(2,1)}, bf16[1024,128]{1,0:T(8,128)(2,1)}, bf16[64,1024]{1,0:T(8,128)(2,1)}, bf16[512,576]{1,0:T(8,128)(2,1)}, bf1...) custom-call(bf16[8,128,1024]{2,1,0:T(8,128)(2,1)} %bitcast.152, f32[128,1024]{1,0:T(8,128)} %constant_dynamic-slice_fusion.h1, ...), custom_call_target="tpu_custom_call" | custom-call | tf_op jit(solution)/shard_map/scatter_keys/pallas_call | solution.py:586
  409.4 1.2 slice_convert_fusion.1
  411.4 2.5 fusion.32
  415.7 2.0 convolution_convert_fusion.5
  417.8 2.5 fusion.3
  421.5 56.1 %scatter_input.1 = (f32[128,1024]{1,0:T(8,128)}, bf16[640,256]{1,0:T(8,128)(2,1)}, bf16[512,1024]{1,0:T(8,128)(2,1)}) custom-call(bf16[8,128,1024]{2,1,0:T(8,128)(2,1)} %bitcast.151, bf16[128,1024]{1,0:T(8,128)(2,1)} %tokens.1, f32[1,1024]{1,0:T(1,128)} %broadcast_in_dim_reshape.5.gain, f32[128,1024]{1,0:T(8,128)} %get-tuple-element.60.gh1, ...), custom_call_target="tpu_custom_call" | custom-call | tf_op jit(solution)/shard_map/scatter_input/pallas_call | solution.py:627
  479.7 1.7 copy_bitcast_fusion
  481.4 1.1 convert_bitcast_fusion.4
  486.1 1.3 reshape.645
  488.3 1.3 reshape.646
  489.8 1.1 reshape.647
  (152 shorter events, 38.1 us)
Async XLA Ops:
  0.6 1.1 copy-start
  1.7 114.1 %collective-permute-start = (bf16[36,1024]{1,0:T(8,128)(2,1)S(1)}, bf16[36,1024]{1,0:T(8,128)(2,1)S(1)}, u32[]{:S(2)}, u32[]{:S(2)}) collective-permute-start(bf16[36,1024]{1,0:T(8,128)(2,1)S(1)} %constant_dynamic-slice_fusion.1), channel_id=1, source_target_pairs={{0,0},{2,16},{4,32},{6,48},{8,64},{10,80},{12,96},{14,112},{16,1},... | collective-permute-start | bytes 221192 | tf_op jit(solution)/shard_map/ppermute | solution.py:696
  39.8 6.4 %copy-start.4 = (bf16[1024,1024]{1,0:T(8,128)(2,1)S(1)}, bf16[1024,1024]{1,0:T(8,128)(2,1)}, u32[]{:S(2)}) copy-start(bf16[1024,1024]{1,0:T(8,128)(2,1)} %get-tuple-element.41) | copy-start | bytes 6291460
  41.9 5.3 %copy-start.15 = (bf16[16,64,256]{2,1,0:T(8,128)(2,1)}, bf16[16,64,256]{2,1,0:T(8,128)(2,1)S(1)}, u32[]{:S(2)}) copy-start(bf16[16,64,256]{2,1,0:T(8,128)(2,1)S(1)} %slice.155) | copy-start | bytes 1572868
  47.2 1.0 copy-start.3
  154.5 6.3 %copy-start.9 = (bf16[576,1024]{1,0:T(8,128)(2,1)S(1)}, bf16[576,1024]{1,0:T(8,128)(2,1)}, u32[]{:S(2)}) copy-start(bf16[576,1024]{1,0:T(8,128)(2,1)} %reshape.627) | copy-start | bytes 3538948
  154.5 6.3 %copy-start.24 = (bf16[1024,1024]{1,0:T(8,128)(2,1)S(1)}, bf16[1024,1024]{1,0:T(8,128)(2,1)}, u32[]{:S(2)}) copy-start(bf16[1024,1024]{1,0:T(8,128)(2,1)} %get-tuple-element.50) | copy-start | bytes 6291460
  162.3 2.5 copy-start.23
  162.7 12.7 %copy-start.6 = (bf16[1024,1024]{1,0:T(8,128)(2,1)}, bf16[1024,1024]{1,0:T(8,128)(2,1)S(1)}, u32[]{:S(2)}) copy-start(bf16[1024,1024]{1,0:T(8,128)(2,1)S(1)} %multiply_convert_fusion) | copy-start | bytes 6291460
  183.2 2.2 copy-start.7
  185.4 3.8 copy-start.10
  190.6 2.6 copy-start.25
  260.9 6.2 %copy-start.18 = (bf16[1024,128]{1,0:T(8,128)(2,1)S(1)}, bf16[1024,128]{1,0:T(8,128)(2,1)}, u32[]{:S(2)}) copy-start(bf16[1024,128]{1,0:T(8,128)(2,1)} %get-tuple-element.51) | copy-start | bytes 786436
  260.9 9.5 %copy-start.2 = (f32[2,1024,128]{2,1,0:T(8,128)S(1)}, f32[2,1024,128]{2,1,0:T(8,128)}, u32[]{:S(2)}) copy-start(f32[2,1024,128]{2,1,0:T(8,128)} %get-tuple-element.44) | copy-start | bytes 3145732
  264.1 57.3 %collective-permute-start.1 = (bf16[48,1024]{1,0:T(8,128)(2,1)}, bf16[48,1024]{1,0:T(8,128)(2,1)}, u32[]{:S(2)}, u32[]{:S(2)}) collective-permute-start(bf16[48,1024]{1,0:T(8,128)(2,1)} %get-tuple-element.56), channel_id=1, source_target_pairs={{0,0},{16,2},{32,4},{48,6},{64,8},{80,10},{96,12},{112,14},{1,16},... | collective-permute-start | bytes 294920 | tf_op jit(solution)/shard_map/ppermute | solution.py:799
  316.7 1.4 copy-start.8
  318.6 0.9 copy-start.22
  413.9 1.8 copy-start.5
  415.7 2.1 copy-start.16
  415.7 2.1 copy-start.20
  415.7 2.1 copy-start.21
  477.7 6.7 %copy-start.11 = (bf16[512,1024]{1,0:T(8,128)(2,1)S(1)}, bf16[512,1024]{1,0:T(8,128)(2,1)}, u32[]{:S(2)}) copy-start(bf16[512,1024]{1,0:T(8,128)(2,1)} %get-tuple-element.65) | copy-start | bytes 3145732
  479.7 5.5 %copy-start.13 = (bf16[512,576]{1,0:T(8,128)(2,1)S(1)}, bf16[512,576]{1,0:T(8,128)(2,1)}, u32[]{:S(2)}) copy-start(bf16[512,576]{1,0:T(8,128)(2,1)} %get-tuple-element.66) | copy-start | bytes 1769476
  485.3 2.1 copy-start.12
  487.5 2.1 copy-start.14
  489.6 1.3 copy-start.19
  489.6 2.0 copy-start.17
  489.6 2.8 copy-start.1

commit v2 on v1

--- a/solution.py
+++ b/solution.py
@@ -17,8 +17,9 @@
 LOG2E = math.log2(math.e)
 F32 = jnp.float32
 BF16 = jnp.bfloat16
-TILE = 512
-KEYS = 512
+STRIP = 128
+FEED = 256
+KEYS = 1024
 VMEM = 56 * 1024 * 1024
 PIECE = 48
 
@@ -78,10 +79,33 @@
     lax.fori_loop(inner_high, high, masked, 0)
 
 
-def forward_kernel(ranges_ref, shift_ref, query_ref, first_ref, kv_ref, sums_ref, totals_ref, total):
+def lanes_low(shape):
+    return lax.broadcasted_iota(jnp.int32, shape, 1) < HD
+
+
+def two_heads(packed, low):
+    other = pltpu.roll(packed, HD, 1)
+    heads = (packed, other) if low else (other, packed)
+    keep = lanes_low(packed.shape) if low else ~lanes_low(packed.shape)
+    return jnp.concatenate([jnp.where(keep, head, 0.0) for head in heads], axis=0)
+
+
+def one_row(heads, low):
+    rows = heads.shape[0] // 2
+    first, second = heads[:rows], heads[rows:]
+    if low:
+        second = pltpu.roll(second, HD, 1)
+    else:
+        first = pltpu.roll(first, HD, 1)
+    return jnp.where(lanes_low(first.shape), first, second)
+
+
+def forward_kernel(
+    ranges_ref, shift_ref, query_ref, first_ref, kv_ref, ob_ref, o_ref, totals_ref, total
+):
     tile = pl.program_id(0)
-    rows = query_ref.shape[1]
-    query = query_ref[...].reshape(2 * rows, 2 * HD)
+    rows = query_ref.shape[0]
+    query = two_heads(query_ref[...].astype(F32) * HD**-0.5, True).astype(BF16)
     first = jnp.concatenate([first_ref[...]] * 2, axis=0)
     index = ranges_ref[4, tile] + lax.broadcasted_iota(jnp.int32, (rows, 1), 0)
     index = jnp.concatenate([index, index], axis=0)
@@ -92,39 +116,47 @@
     def step(block, masked):
         start = pl.multiple_of(block * KEYS, KEYS)
         kv = kv_ref[pl.ds(start, KEYS), :]
-        exps = jnp.exp2(dot_nt(query, kv) * (LOG2E * HD**-0.5) - shift)
+        exps = jnp.exp2(dot_nt(query, kv) * LOG2E - shift)
         if masked:
             keys = start + lax.broadcasted_iota(jnp.int32, (2 * rows, KEYS), 1)
             exps = jnp.where((keys >= first) & (keys <= index), exps, 0.0)
         total[...] += dot_nn(exps.astype(BF16), jnp.concatenate([kv, ones], axis=1))
 
     key_loops(ranges_ref, tile, step)
-    sums_ref[...] = total[:, : 2 * HD].reshape(2, rows, 2 * HD)
-    totals_ref[...] = total[:, 2 * HD :].reshape(2, rows, 2 * HD)
+    totals = total[:, 2 * HD :]
+    o = total[:, : 2 * HD] / totals
+    o_ref[0] = o
+    totals_ref[0] = totals
+    ob_ref[...] = one_row(o, False).astype(BF16)
 
 
 def forward_attention(ranges, shift, query, first, kv):
-    rows = query.shape[1]
-    tiles = rows // TILE
+    tiles = query.shape[0] // STRIP
     whole = lambda t, *_: (0, 0)
-    part = lambda t, *_: (0, t, 0)
+    part = lambda t, *_: (t, 0)
+    wide = lambda t, *_: (t, 0, 0)
     return pl.pallas_call(
         forward_kernel,
         grid_spec=pltpu.PrefetchScalarGridSpec(
             num_scalar_prefetch=2,
             grid=(tiles,),
             in_specs=[
-                pl.BlockSpec((2, TILE, 2 * HD), part),
-                pl.BlockSpec((TILE, 1), lambda t, *_: (t, 0)),
+                pl.BlockSpec((STRIP, 2 * HD), part),
+                pl.BlockSpec((STRIP, 1), part),
                 pl.BlockSpec(kv.shape, whole),
             ],
             out_specs=[
-                pl.BlockSpec((2, TILE, 2 * HD), part),
-                pl.BlockSpec((2, TILE, 2 * HD), part),
+                pl.BlockSpec((STRIP, 2 * HD), part),
+                pl.BlockSpec((1, 2 * STRIP, 2 * HD), wide),
+                pl.BlockSpec((1, 2 * STRIP, 2 * HD), wide),
             ],
-            scratch_shapes=[pltpu.VMEM((2 * TILE, 4 * HD), F32)],
+            scratch_shapes=[pltpu.VMEM((2 * STRIP, 4 * HD), F32)],
         ),
-        out_shape=[jax.ShapeDtypeStruct(query.shape, F32)] * 2,
+        out_shape=[
+            jax.ShapeDtypeStruct(query.shape, BF16),
+            jax.ShapeDtypeStruct((tiles, 2 * STRIP, 2 * HD), F32),
+            jax.ShapeDtypeStruct((tiles, 2 * STRIP, 2 * HD), F32),
+        ],
         compiler_params=pltpu.CompilerParams(vmem_limit_bytes=VMEM),
         cost_estimate=pl.CostEstimate(
             flops=8 * 10**9, bytes_accessed=8 * 10**6, transcendentals=16 * 10**6
@@ -134,14 +166,19 @@
 
 
 def backward_kernel(
-    ranges_ref, shift_ref, query_ref, grad_ref, delta_ref, first_ref, kv_ref, gq_ref, gkv_ref, total
+    ranges_ref, shift_ref, query_ref, grad_ref, o_ref, totals_ref, first_ref, kv_ref,
+    gq_ref, gkv_ref, total, gq,
 ):
     tile = pl.program_id(0)
-    rows = query_ref.shape[1]
-    query = query_ref[...].reshape(2 * rows, 2 * HD)
-    grad = grad_ref[...].reshape(2 * rows, 2 * HD)
-    delta = delta_ref[...].reshape(1, 2 * rows)
-    first = first_ref[...].reshape(1, 2 * rows)
+    rows = query_ref.shape[0]
+    query = two_heads(query_ref[...].astype(F32) * HD**-0.5, True).astype(BF16)
+    go = two_heads(grad_ref[...].astype(F32), False)
+    totals = totals_ref[0]
+    grad = (go / totals).astype(BF16)
+    delta = jnp.sum(go * o_ref[0], axis=1, keepdims=True) / totals
+    delta = jnp.transpose(delta)[:1]
+    both = jnp.concatenate([query, grad], axis=0)
+    first = jnp.concatenate([first_ref[0]] * 2, axis=1)
     index = ranges_ref[4, tile] + lax.broadcasted_iota(jnp.int32, (1, rows), 1)
     index = jnp.concatenate([index, index], axis=1)
     shift = shift_ref[0]
@@ -150,54 +187,55 @@
     def _():
         total[...] = jnp.zeros_like(total)
 
-    gq_ref[...] = jnp.zeros_like(gq_ref)
+    gq[...] = jnp.zeros_like(gq)
 
     def step(block, masked):
         start = pl.multiple_of(block * KEYS, KEYS)
         kv = kv_ref[pl.ds(start, KEYS), :]
-        exps = jnp.exp2(dot_nt(kv, query) * (LOG2E * HD**-0.5) - shift)
+        exps = jnp.exp2(dot_nt(kv, query) * LOG2E - shift)
         if masked:
             keys = start + lax.broadcasted_iota(jnp.int32, (KEYS, 2 * rows), 0)
             exps = jnp.where((keys >= first) & (keys <= index), exps, 0.0)
         scores = (exps * (dot_nt(kv, grad) - delta)).astype(BF16)
-        gq_ref[...] += dot_tn(scores, kv).reshape(gq_ref.shape)
-        total[pl.ds(start, KEYS), :] += dot_nn(scores, query) * HD**-0.5 + dot_nn(
-            exps.astype(BF16), grad
+        gq[...] += dot_tn(scores, kv)
+        total[pl.ds(start, KEYS), :] += dot_nn(
+            jnp.concatenate([scores, exps.astype(BF16)], axis=1), both
         )
 
     key_loops(ranges_ref, tile, step)
+    gq_ref[...] = (one_row(gq[...], True) * HD**-0.5).astype(BF16)
 
     @pl.when(tile == pl.num_programs(0) - 1)
     def _():
         gkv_ref[...] = total[...].astype(BF16)
 
 
-def backward_attention(ranges, shift, query, grad, delta, first, kv):
-    rows = query.shape[1]
-    tiles = rows // TILE
+def backward_attention(ranges, shift, query, grad, o, totals, first, kv):
+    tiles = query.shape[0] // STRIP
     whole = lambda t, *_: (0, 0)
-    part = lambda t, *_: (0, t, 0)
-    row = lambda t, *_: (t, 0, 0)
+    part = lambda t, *_: (t, 0)
+    wide = lambda t, *_: (t, 0, 0)
     return pl.pallas_call(
         backward_kernel,
         grid_spec=pltpu.PrefetchScalarGridSpec(
             num_scalar_prefetch=2,
             grid=(tiles,),
             in_specs=[
-                pl.BlockSpec((2, TILE, 2 * HD), part),
-                pl.BlockSpec((2, TILE, 2 * HD), part),
-                pl.BlockSpec((1, 1, 2 * TILE), row),
-                pl.BlockSpec((1, 1, 2 * TILE), row),
+                pl.BlockSpec((STRIP, 2 * HD), part),
+                pl.BlockSpec((STRIP, 2 * HD), part),
+                pl.BlockSpec((1, 2 * STRIP, 2 * HD), wide),
+                pl.BlockSpec((1, 2 * STRIP, 2 * HD), wide),
+                pl.BlockSpec((1, 1, STRIP), wide),
                 pl.BlockSpec(kv.shape, whole),
             ],
             out_specs=[
-                pl.BlockSpec((2, TILE, 2 * HD), part),
+                pl.BlockSpec((STRIP, 2 * HD), part),
                 pl.BlockSpec(kv.shape, whole),
             ],
-            scratch_shapes=[pltpu.VMEM(kv.shape, F32)],
+            scratch_shapes=[pltpu.VMEM(kv.shape, F32), pltpu.VMEM((2 * STRIP, 2 * HD), F32)],
         ),
         out_shape=[
-            jax.ShapeDtypeStruct(query.shape, F32),
+            jax.ShapeDtypeStruct(query.shape, BF16),
             jax.ShapeDtypeStruct(kv.shape, BF16),
         ],
         compiler_params=pltpu.CompilerParams(vmem_limit_bytes=VMEM),
@@ -205,7 +243,65 @@
             flops=20 * 10**9, bytes_accessed=16 * 10**6, transcendentals=16 * 10**6
         ),
         name="attention_backward",
-    )(ranges, shift, query, grad, delta, first, kv)
+    )(ranges, shift, query, grad, o, totals, first, kv)
+
+
+def feed_kernel(
+    n2_ref, dy_ref, weights_ref, down_ref,
+    gn2_ref, branch_ref, gate_out, up_out, down_out,
+    act_ref, ggate_ref, gup_ref,
+):
+    count, width = n2_ref.shape
+
+    def tokens(t, _):
+        at = pl.ds(pl.multiple_of(t * FEED, FEED), FEED)
+        n2 = n2_ref[at, :]
+        gate = dot_nn(n2, weights_ref[0])
+        up = dot_nn(n2, weights_ref[1])
+        gact = dot_nt(dy_ref[at, :], down_ref[...])
+        sig = jax.nn.sigmoid(gate)
+        silu = gate * sig
+        act = (silu * up).astype(BF16)
+        ggate = (gact * up * sig * (1.0 + gate * (1.0 - sig))).astype(BF16)
+        gup = (gact * silu).astype(BF16)
+        act_ref[at, :] = act
+        ggate_ref[at, :] = ggate
+        gup_ref[at, :] = gup
+        gn2_ref[at, :] = (dot_nt(ggate, weights_ref[0]) + dot_nt(gup, weights_ref[1])).astype(BF16)
+        branch_ref[at, :] = dot_nn(act, down_ref[...]).astype(BF16)
+        return 0
+
+    lax.fori_loop(0, count // FEED, tokens, 0)
+
+    def columns(c, _):
+        at = pl.ds(pl.multiple_of(c * FEED, FEED), FEED)
+        n2 = n2_ref[:, at]
+        gate_out[at, :] = dot_tn(n2, ggate_ref[...]).astype(BF16)
+        up_out[at, :] = dot_tn(n2, gup_ref[...]).astype(BF16)
+        down_out[:, at] = dot_tn(act_ref[...], dy_ref[:, at]).astype(BF16)
+        return 0
+
+    lax.fori_loop(0, width // FEED, columns, 0)
+
+
+def feed_forward(n2, dy, weights, down):
+    part = down.shape[0]
+    count, width = n2.shape
+    return pl.pallas_call(
+        feed_kernel,
+        out_shape=[
+            jax.ShapeDtypeStruct(shape, BF16)
+            for shape in [(count, width)] * 2 + [(width, part)] * 2 + [(part, width)]
+        ],
+        in_specs=[IN_VMEM] * 4,
+        out_specs=[IN_VMEM] * 5,
+        scratch_shapes=[pltpu.VMEM((count, part), BF16)] * 3,
+        compiler_params=pltpu.CompilerParams(vmem_limit_bytes=VMEM),
+        cost_estimate=pl.CostEstimate(
+            flops=11 * 10**9, bytes_accessed=16 * 10**6, transcendentals=10**6
+        ),
+        name="feed_forward",
+    )(n2, dy, weights, down)
 
 
 MESH = pl.DeviceIdType.MESH
@@ -227,13 +323,13 @@
         self.send, self.recv, self.local = send, recv, local
         self.started, self.locals = [], []
 
-    def remote(self, src, dst, peer):
+    def remote(self, src, dst, peer, recv=None):
         i = len(self.started)
         copy = pltpu.make_async_remote_copy(
             src_ref=src,
             dst_ref=dst,
             send_sem=self.send.at[i],
-            recv_sem=self.recv.at[i],
+            recv_sem=self.recv.at[i] if recv is None else recv,
             device_id=peer,
             device_id_type=MESH,
         )
@@ -330,6 +426,78 @@
         live = [stage for stage in live if next(stage, stage) is not stage]
 
 
+class Swap:
+    def __init__(self, copies, recv, sem, tag, stays, sends):
+        self.copies, self.recv, self.tag, self.stays = copies, recv, tag, stays
+        (src, dst, peer), rest = sends[0], sends[1:]
+        self.own = pltpu.make_async_remote_copy(
+            src_ref=src,
+            dst_ref=dst,
+            send_sem=sem.at[0],
+            recv_sem=recv.at[tag],
+            device_id=peer,
+            device_id_type=MESH,
+        )
+        self.kept = pltpu.make_async_copy(src, dst, sem.at[1])
+
+        @pl.when(stays)
+        def _():
+            self.kept.start()
+
+        @pl.when(jnp.logical_not(stays))
+        def _():
+            self.own.start()
+
+        self.sample = (src, dst, peer, sem)
+        for src, dst, peer in rest:
+            copies.remote(src, dst, peer, recv.at[tag])
+
+    def wait(self, landing):
+        src, _, peer, sem = self.sample
+        for step in range(1, 8):
+            sender = lax.rem(self.tag + step, 8)
+            pltpu.make_async_remote_copy(
+                src_ref=src,
+                dst_ref=landing(sender),
+                send_sem=sem.at[0],
+                recv_sem=self.recv.at[sender],
+                device_id=peer,
+                device_id_type=MESH,
+            ).wait_recv()
+
+        @pl.when(self.stays)
+        def _():
+            self.kept.wait()
+
+        @pl.when(jnp.logical_not(self.stays))
+        def _():
+            self.own.wait()
+
+
+def greet_for_swap(places, peers, senders):
+    barrier = pltpu.get_barrier_semaphore()
+    peers = peers + senders[1:]
+    for peer in peers:
+        pl.semaphore_signal(barrier, inc=1, device_id=peer, device_id_type=MESH)
+
+    @pl.when(places.stays)
+    def _():
+        pl.semaphore_wait(barrier, len(peers))
+
+    @pl.when(jnp.logical_not(places.stays))
+    def _():
+        pl.semaphore_signal(barrier, inc=1, device_id=senders[0], device_id_type=MESH)
+        pl.semaphore_wait(barrier, len(peers) + 1)
+
+
+def strips_at(ref, index):
+    return ref.at[pl.ds(pl.multiple_of(index * STRIP, STRIP), STRIP), :]
+
+
+def heads_at(ref, index):
+    return ref.at[:, pl.ds(pl.multiple_of(index * 2 * HD, 2 * HD), 2 * HD)]
+
+
 class Places:
     def __init__(self):
         self.seq, self.fsdp = lax.axis_index("seq"), lax.axis_index("fsdp")
@@ -339,6 +507,7 @@
         self.col = lax.rem(self.chip, 4)
         self.sibling = pair_of(self.fsdp)
         self.across = lax.rem(self.fsdp + 8, 16)
+        self.stays = self.chip == self.seq
 
     def on_seq(self, index):
         return (index, self.fsdp)
@@ -357,10 +526,16 @@
         fsdp = [self.across, ring_step(self.fsdp, 1), ring_step(self.fsdp, 3), self.sibling]
         return [self.on_seq(i) for i in seq] + [self.on_fsdp(i) for i in fsdp]
 
-    def scatter_peers(self):
-        seq = [self.on_seq(self.other_seq(d)) for d in range(1, 8)]
-        fsdp = [self.on_fsdp(self.other_chip(d) * 2 + self.core) for d in range(1, 8)]
-        return seq + fsdp + [self.on_fsdp(self.sibling)]
+    def strip_peers(self):
+        return [self.on_fsdp(self.other_chip(d) * 2 + self.core) for d in range(1, 8)]
+
+    def owners(self):
+        strips = [lax.rem(self.chip + d, 8) for d in range(8)]
+        return strips, [(self.chip, strip * 2 + self.core) for strip in strips]
+
+    def heads(self):
+        heads = [lax.rem(self.seq + d, 8) for d in range(8)]
+        return heads, [(head, self.seq * 2 + self.core) for head in heads]
 
 
 def params(name_id):
@@ -391,19 +566,38 @@
     )
 
 
-def gather(name, name_id, seq_items, fsdp_items):
+class Strips:
+    def __init__(self, copies, places, src, out):
+        self.kept = copies.here(strips_at(src, places.chip), strips_at(out, places.chip))
+        self.copies = []
+        for d in range(1, 8):
+            chip = places.other_chip(d)
+            peer = places.on_fsdp(chip * 2 + places.core)
+            self.copies.append(copies.remote(strips_at(src, chip), strips_at(out, places.chip), peer))
+
+    def wait(self):
+        for copy in self.copies:
+            copy.wait_recv()
+        self.kept.wait()
+
+
+def gather(name, name_id, seq_items, fsdp_items, strips=()):
     items = seq_items + fsdp_items
     count = len(items)
+    every = count + len(strips)
 
     def kernel(*refs):
-        srcs, outs = refs[:count], refs[count : 2 * count]
-        copies, places = Copies(*refs[2 * count :]), Places()
-        greet(places.gather_peers())
+        srcs, outs = refs[:every], refs[every : 2 * every]
+        copies, places = Copies(*refs[2 * every :]), Places()
+        greet(places.gather_peers() + (places.strip_peers() if strips else []))
+        moved = [Strips(copies, places, srcs[i], outs[i]) for i in range(count, every)]
         stages = []
         for i, (_, axis, split) in enumerate(items):
             make = seq_gather if i < len(seq_items) else fsdp_gather
             stages.append(make(copies, places, srcs[i], outs[i], axis, split))
         run_stages(stages)
+        for item in moved:
+            item.wait()
         copies.finish()
 
     shapes = []
@@ -411,69 +605,206 @@
         shape = list(array.shape)
         shape[axis] *= 8 if i < len(seq_items) else 16
         shapes.append(jax.ShapeDtypeStruct(tuple(shape), array.dtype))
+    shapes += [jax.ShapeDtypeStruct(array.shape, array.dtype) for array in strips]
+    remote = 9 * len(seq_items) + 17 * len(fsdp_items) + 7 * len(strips)
     return pl.pallas_call(
         kernel,
         out_shape=shapes,
-        in_specs=[HBM] * count,
-        out_specs=[HBM] * count,
-        scratch_shapes=semaphores(9 * len(seq_items) + 17 * len(fsdp_items), count),
+        in_specs=[HBM] * every,
+        out_specs=[HBM] * every,
+        scratch_shapes=semaphores(remote, every),
         compiler_params=params(name_id),
         name=name,
-    )(*[item[0] for item in items])
-
-
-class SeqSum:
-    def __init__(self, copies, places, part, held):
-        self.held = held
-        self.kept = copies.here(part.at[places.seq], held.at[0])
-        self.copies = []
-        for d in (4, 3, 5, 2, 6, 1, 7):
-            peer = places.other_seq(d)
-            self.copies.append(copies.remote(part.at[peer], held.at[d], places.on_seq(peer)))
+    )(*[item[0] for item in items], *strips)
+
+
+def attended_kernel(
+    ob, wo, tokens, gain, gate_up, down,
+    own_ref, h1_ref, n2_all, gate_up_all, down_all,
+    own, n2, tags, ends, send, recv, local_sem,
+):
+    copies, places = Copies(send, recv, local_sem), Places()
+    strips, owners = places.owners()
+    _, senders = places.heads()
+    greet_for_swap(places, places.gather_peers(), senders)
+    landing = heads_at(own, places.seq)
+    sends = [(strips_at(ob, strip), landing, peer) for strip, peer in zip(strips, owners)]
+    swap = Swap(copies, tags, ends, places.seq, places.stays, sends)
+    stages = [
+        fsdp_gather(copies, places, gate_up, gate_up_all, 1, (1, 32)),
+        fsdp_gather(copies, places, down, down_all, 0, (0, 32)),
+    ]
+    for stage in stages:
+        next(stage)
+    swap.wait(lambda sender: heads_at(own, sender))
+    own_ref[...] = own[...]
+
+    def columns(j, _):
+        at = pl.ds(pl.multiple_of(j * 256, 256), 256)
+        h1_ref[:, at] = tokens[:, at].astype(F32) + dot_nn(own[...], wo[:, at])
+        return 0
+
+    lax.fori_loop(0, 4, columns, 0)
+    value = h1_ref[...]
+    n2[...] = (value * unit_rows(value) * gain[...]).astype(BF16)
+    stages.insert(0, seq_gather(copies, places, n2, n2_all, 0, (0, 64)))
+    run_stages(stages)
+    copies.finish()
+
+
+def gather_attended(ob, wo, tokens, gain, gate_up, down):
+    rows, width = tokens.shape
+    return pl.pallas_call(
+        attended_kernel,
+        out_shape=[
+            jax.ShapeDtypeStruct((rows, width), BF16),
+            jax.ShapeDtypeStruct((rows, width), F32),
+            jax.ShapeDtypeStruct((8 * rows, width), BF16),
+            jax.ShapeDtypeStruct((2, 16 * gate_up.shape[1], gate_up.shape[2]), BF16),
+            jax.ShapeDtypeStruct((16 * down.shape[0], width), BF16),
+        ],
+        in_specs=[HBM] + [IN_VMEM] * 3 + [HBM] * 2,
+        out_specs=[IN_VMEM] * 2 + [HBM] * 3,
+        scratch_shapes=[
+            pltpu.VMEM((rows, width), BF16),
+            pltpu.VMEM((rows, width), BF16),
+            pltpu.SemaphoreType.DMA((8,)),
+            pltpu.SemaphoreType.DMA((2,)),
+        ]
+        + semaphores(7 + 9 + 2 * 17, 3),
+        compiler_params=params(3),
+        name="gather_attended",
+    )(ob, wo, tokens, gain, gate_up, down)
+
+
+class RingSum:
+    def __init__(self, copies, near, mine, held, cut, index, device):
+        self.remote, self.mine, self.device = copies.remote, mine, device
+        self.half, self.ring, self.other = held
+        self.cut, self.index = cut, index
+        self.plus, self.minus, self.pair = near
+
+    def parts(self):
+        rows = self.mine.shape[1]
+        return pl.ds(0, self.cut), pl.ds(self.cut, rows - self.cut)
+
+    def send(self):
+        low, high = self.parts()
+        self.first, self.second = [], []
+        for flip in (1, 0):
+            far, up, down = [self.mine.at[self.index(flip, step)] for step in (2, 1, 3)]
+            self.first.append(
+                (
+                    self.remote(far.at[low], self.half.at[flip, low], self.plus),
+                    self.remote(far.at[high], self.half.at[flip, high], self.minus),
+                )
+            )
+            self.second.append(
+                [
+                    self.remote(up.at[high], self.ring.at[flip, 0, high], self.plus),
+                    self.remote(down.at[low], self.ring.at[flip, 1, low], self.minus),
+                ]
+            )
+
+    def relay(self):
+        low, high = self.parts()
+        for i, flip in enumerate((1, 0)):
+            for copy, step, part, way, peer in (
+                (self.first[i][0], 1, low, 0, self.plus),
+                (self.first[i][1], 3, high, 1, self.minus),
+            ):
+                copy.wait_recv()
+                at = self.index(flip, step)
+                self.mine[at, part] = (
+                    self.mine[at, part].astype(F32) + self.half[flip, part].astype(F32)
+                ).astype(BF16)
+                self.second[i].append(
+                    self.remote(self.mine.at[at, part], self.ring.at[flip, way, part], peer)
+                )
+
+    def gathered(self, i, flip):
+        for copy in self.second[i]:
+            copy.wait_recv()
+        return (
+            self.mine[self.index(flip, 0)].astype(F32)
+            + self.ring[flip, 0].astype(F32)
+            + self.ring[flip, 1].astype(F32)
+        )
+
+    def cross(self):
+        self.other[0] = self.gathered(0, 1).astype(BF16)
+        self.last = self.remote(self.other.at[0], self.other.at[1], self.pair)
 
     def total(self):
+        total = self.gathered(1, 0)
+        self.last.wait_recv()
+        return total + self.other[1].astype(F32)
+
+
+def ring_buffers(shape):
+    return [
+        pltpu.VMEM((2,) + shape, BF16),
+        pltpu.VMEM((2, 2) + shape, BF16),
+        pltpu.VMEM((2,) + shape, BF16),
+    ]
+
+
+RING_COPIES = 13
+
+
+class SeqSum(RingSum):
+    def __init__(self, copies, places, part, buffers, cut):
+        mine, held = buffers[0], buffers[1:]
+        seq = places.seq
+
+        def index(flip, step):
+            base = ring_step(seq, step)
+            return pair_of(base) if flip else base
+
+        near = [places.on_seq(i) for i in (ring_step(seq, 1), ring_step(seq, 3), pair_of(seq))]
+        super().__init__(copies, near, mine, held, cut, index, places.on_seq)
+        self.kept = copies.here(part, mine)
+
+    def ready(self):
         self.kept.wait()
-        for copy in self.copies:
+
+
+class FsdpSum(RingSum):
+    def __init__(self, copies, places, part, buffers, cut):
+        mine, self.theirs, held = buffers[0], buffers[1], buffers[2:]
+        fsdp = places.fsdp
+
+        def index(flip, step):
+            return lax.rem(places.row + flip, 2) * 4 + lax.rem(places.col + step, 4)
+
+        near = [places.on_fsdp(i) for i in (ring_step(fsdp, 1), ring_step(fsdp, 3), places.across)]
+        super().__init__(copies, near, mine, held, cut, index, places.on_fsdp)
+        self.order = [index(flip, step) for flip in (1, 0) for step in (2, 1, 3, 0)]
+        self.others = [
+            copies.remote(
+                part.at[at, 1 - places.core], self.theirs.at[at], places.on_fsdp(places.sibling)
+            )
+            for at in self.order
+        ]
+        self.kept = copies.here(part.at[:, places.core], mine)
+
+    def ready(self):
+        self.kept.wait()
+        for at, copy in zip(self.order, self.others):
             copy.wait_recv()
-        total = self.held[0].astype(F32)
-        for d in range(1, 8):
-            total += self.held[d].astype(F32)
-        return total
-
-
-class FsdpSum:
-    def __init__(self, copies, places, part, mine, theirs, held):
-        self.remote, self.places = copies.remote, places
-        self.mine, self.theirs, self.held = mine, theirs, held
-        self.other = copies.remote(
-            part.at[:, 1 - places.core], theirs, places.on_fsdp(places.sibling)
-        )
-        self.kept = copies.here(part.at[:, places.core], mine)
-
-    def send(self):
-        self.kept.wait()
-        self.other.wait_recv()
-        self.copies = []
-        for d in (2, 6, 4, 5, 7, 1, 3):
-            chip = self.places.other_chip(d)
-            self.mine[chip] = (
-                self.mine[chip].astype(F32) + self.theirs[chip].astype(F32)
-            ).astype(BF16)
-            peer = self.places.on_fsdp(chip * 2 + self.places.core)
-            self.copies.append(self.remote(self.mine.at[chip], self.held.at[d], peer))
-
-    def total(self):
-        chip = self.places.chip
-        total = self.mine[chip].astype(F32) + self.theirs[chip].astype(F32)
-        for copy in self.copies:
-            copy.wait_recv()
-        for d in range(1, 8):
-            total += self.held[d].astype(F32)
-        return total
+            self.mine[at] = (self.mine[at].astype(F32) + self.theirs[at].astype(F32)).astype(BF16)
+
+
+def seq_buffers(shape):
+    return [pltpu.VMEM((8,) + shape, BF16)] + ring_buffers(shape)
 
 
 def fsdp_buffers(shape):
-    return [pltpu.VMEM((8,) + shape, BF16)] * 3
+    return [pltpu.VMEM((8,) + shape, BF16)] * 2 + ring_buffers(shape)
+
+
+SEQ_COPIES = RING_COPIES
+FSDP_COPIES = RING_COPIES + 8
 
 
 def unit_rows(values):
@@ -483,18 +814,25 @@
 def hidden_kernel(
     part, h1, dy, gain, wo, gate, up, down,
     gh1_ref, gb_ref, term_ref, go_ref, gate_out, up_out, down_out,
-    held, go_own, b0, b1, b2, b3, b4, b5, b6, b7, b8, send, recv, local_sem,
+    go_own, tags, ends, *scratch,
 ):
-    copies, places = Copies(send, recv, local_sem), Places()
-    greet(places.scatter_peers())
-    hidden = SeqSum(copies, places, part, held)
+    copies, places = Copies(*scratch[19:]), Places()
+    heads, workers = places.heads()
+    _, senders = places.owners()
+    greet_for_swap(places, places.gather_peers(), senders)
+    hidden = SeqSum(copies, places, part, scratch[:4], 64)
     sums = [
-        FsdpSum(copies, places, gate, b0, b1, b2),
-        FsdpSum(copies, places, up, b3, b4, b5),
-        FsdpSum(copies, places, down, b6, b7, b8),
+        FsdpSum(copies, places, gate, scratch[4:9], 32),
+        FsdpSum(copies, places, up, scratch[9:14], 32),
+        FsdpSum(copies, places, down, scratch[14:19], 32),
     ]
-    for item in sums:
+    for item in [hidden] + sums:
+        item.ready()
         item.send()
+    for item in [hidden] + sums:
+        item.relay()
+    for item in [hidden] + sums:
+        item.cross()
     gn2 = hidden.total()
     value = h1[...]
     inverse = unit_rows(value)
@@ -512,26 +850,23 @@
         return 0
 
     lax.fori_loop(0, 4, columns, 0)
-    rows = go_own.shape[0]
-    mine = go_ref.at[pl.ds(pl.multiple_of(places.seq * rows, 16), rows), :]
-    head = lambda index: go_own.at[:, pl.ds(pl.multiple_of(index * 128, 128), 128)]
-    kept = copies.here(head(places.seq), mine)
-    heads = []
-    for d in (4, 3, 5, 2, 6, 1, 7):
-        peer = places.other_seq(d)
-        heads.append(copies.remote(head(peer), mine, places.on_seq(peer)))
+    landing = strips_at(go_ref, places.chip)
+    sends = [(heads_at(go_own, head), landing, peer) for head, peer in zip(heads, workers)]
+    swap = Swap(copies, tags, ends, places.chip, places.stays, sends)
     for item, out in zip(sums, (gate_out, up_out, down_out)):
         out[...] = item.total().astype(BF16)
-    kept.wait()
-    for copy in heads:
-        copy.wait_recv()
+    swap.wait(lambda sender: strips_at(go_ref, sender))
     copies.finish()
 
 
 def scatter_hidden(part, h1, dy, gain, wo, gate, up, down):
     rows, width = h1.shape
     shapes = [a.shape[2:] for a in (gate, up, down)]
-    scratch = [pltpu.VMEM((8, rows, width), BF16), pltpu.VMEM((rows, width), BF16)]
+    scratch = [
+        pltpu.VMEM((rows, width), BF16),
+        pltpu.SemaphoreType.DMA((8,)),
+        pltpu.SemaphoreType.DMA((2,)),
+    ] + seq_buffers((rows, width))
     for shape in shapes:
         scratch += fsdp_buffers(shape)
     return pl.pallas_call(
@@ -545,41 +880,56 @@
         + [jax.ShapeDtypeStruct(shape, BF16) for shape in shapes],
         in_specs=[HBM] + [IN_VMEM] * 4 + [HBM] * 3,
         out_specs=[IN_VMEM] * 3 + [HBM] + [IN_VMEM] * 3,
-        scratch_shapes=scratch + semaphores(7 + 7 + 3 * 8, 5),
+        scratch_shapes=scratch + semaphores(SEQ_COPIES + 7 + 3 * FSDP_COPIES, 4),
         compiler_params=params(4),
         name="scatter_hidden",
     )(part, h1, dy, gain, wo, gate, up, down)
 
 
 def keys_kernel(
-    branch, h1, gkv, gout, gate, up, down,
-    layer_ref, gkv_out, gout_out, gate_all, up_all, down_all,
-    held, b0, b1, b2, b3, b4, b5, send, recv, local_sem,
+    branch, h1, gkv, gout, gate, up, down, gq,
+    layer_ref, gkv_out, gout_out, gate_all, up_all, down_all, gq_out,
+    *scratch,
 ):
-    copies, places = Copies(send, recv, local_sem), Places()
-    greet(places.scatter_peers())
-    sums = [FsdpSum(copies, places, gkv, b0, b1, b2), FsdpSum(copies, places, gout, b3, b4, b5)]
-    hidden = SeqSum(copies, places, branch, held)
+    copies, places = Copies(*scratch[14:]), Places()
+    greet(places.gather_peers() + places.strip_peers())
+    moved = Strips(copies, places, gq, gq_out)
+    sums = [
+        FsdpSum(copies, places, gkv, scratch[4:9], 512),
+        FsdpSum(copies, places, gout, scratch[9:14], 32),
+    ]
+    hidden = SeqSum(copies, places, branch, scratch[:4], 64)
     stages = [
         seq_gather(copies, places, gate, gate_all, 0, (0, 32)),
         seq_gather(copies, places, up, up_all, 0, (0, 32)),
         seq_gather(copies, places, down, down_all, 0, (0, 16)),
     ]
+    items = [hidden] + sums
+    hidden.ready()
+    hidden.send()
     for stage in stages:
         next(stage)
     for item in sums:
+        item.ready()
         item.send()
+    for item in items:
+        item.relay()
+    for stage in stages:
+        next(stage)
+    for item in items:
+        item.cross()
     run_stages(stages)
     for item, out in zip(sums, (gkv_out, gout_out)):
         out[...] = item.total().astype(BF16)
     layer_ref[...] = (h1[...] + hidden.total()).astype(BF16)
+    moved.wait()
     copies.finish()
 
 
-def scatter_keys(branch, h1, gkv, gout, gate, up, down):
+def scatter_keys(branch, h1, gkv, gout, gate, up, down, gq):
     rows, width = h1.shape
     shapes = [a.shape[2:] for a in (gkv, gout)]
-    scratch = [pltpu.VMEM((8, rows, width), BF16)]
+    scratch = seq_buffers((rows, width))
     for shape in shapes:
         scratch += fsdp_buffers(shape)
     wide = [jax.ShapeDtypeStruct((8 * a.shape[0],) + a.shape[1:], BF16) for a in (gate, up, down)]
@@ -587,27 +937,34 @@
         keys_kernel,
         out_shape=[jax.ShapeDtypeStruct((rows, width), BF16)]
         + [jax.ShapeDtypeStruct(shape, BF16) for shape in shapes]
-        + wide,
-        in_specs=[HBM, IN_VMEM] + [HBM] * 5,
-        out_specs=[IN_VMEM] * 3 + [HBM] * 3,
-        scratch_shapes=scratch + semaphores(7 + 2 * 8 + 27, 6),
+        + wide
+        + [jax.ShapeDtypeStruct(gq.shape, BF16)],
+        in_specs=[HBM, IN_VMEM] + [HBM] * 6,
+        out_specs=[IN_VMEM] * 3 + [HBM] * 4,
+        scratch_shapes=scratch + semaphores(SEQ_COPIES + 2 * FSDP_COPIES + 27 + 7, 7),
         compiler_params=params(5),
         name="scatter_keys",
-    )(branch, h1, gkv, gout, gate, up, down)
+    )(branch, h1, gkv, gout, gate, up, down, gq)
 
 
 def input_kernel(
     part, tokens, gain, gh1, pack, gout,
     grad_ref, pack_all, gout_all,
-    held, b0, b1, b2, small, send, recv, local_sem,
+    small, *scratch,
 ):
-    copies, places = Copies(send, recv, local_sem), Places()
-    greet(places.scatter_peers())
-    packs = FsdpSum(copies, places, pack, b0, b1, b2)
-    hidden = SeqSum(copies, places, part, held)
-    packs.send()
+    copies, places = Copies(*scratch[9:]), Places()
+    greet(places.gather_peers())
+    packs = FsdpSum(copies, places, pack, scratch[4:9], 48)
+    hidden = SeqSum(copies, places, part, scratch[:4], 64)
+    for item in (hidden, packs):
+        item.ready()
+        item.send()
     stages = [seq_gather(copies, places, gout, gout_all, 0, (0, 32))]
     next(stages[0])
+    for item in (packs, hidden):
+        item.relay()
+    for item in (packs, hidden):
+        item.cross()
     small[...] = packs.total().astype(BF16)
     stages.append(seq_gather(copies, places, small, pack_all, 0, (0, 48)))
     run_stages(stages)
@@ -633,10 +990,10 @@
         ],
         in_specs=[HBM] + [IN_VMEM] * 3 + [HBM] * 2,
         out_specs=[IN_VMEM] + [HBM] * 2,
-        scratch_shapes=[pltpu.VMEM((8, rows, width), BF16)]
+        scratch_shapes=[pltpu.VMEM(shape, BF16)]
+        + seq_buffers((rows, width))
         + fsdp_buffers(shape)
-        + [pltpu.VMEM(shape, BF16)]
-        + semaphores(7 + 8 + 18, 4),
+        + semaphores(SEQ_COPIES + FSDP_COPIES + 18, 4),
         compiler_params=params(6),
         name="scatter_input",
     )(part, tokens, gain, gh1, pack, gout)
@@ -716,22 +1073,30 @@
     gain_k = gains[:, 2 * shard + qshard : 2 * shard + 2 * qshard].reshape(HD)
 
     starts = doc_starts(segments)
-    ids = take(segments, block_start, block)
-    picked = (ids[:, None] == jnp.arange(DOCS, dtype=jnp.int32)[None, :]).astype(jnp.int32)
-    first = jnp.sum(picked * starts[None, :], axis=1)
+    labels = jnp.arange(DOCS, dtype=jnp.int32)
+
+    def firsts(ids):
+        picked = (ids[:, None] == labels[None, :]).astype(jnp.int32)
+        return jnp.sum(picked * starts[None, :], axis=1)
+
     index = block_start + jnp.arange(block, dtype=jnp.int32)
+    positions = index - firsts(take(segments, block_start, block))
     freqs = THETA ** (-2.0 * jnp.arange(HD // 2, dtype=F32) / HD)
-    angles = (index - first).astype(F32)[:, None] * freqs[None, :]
+    angles = positions.astype(F32)[:, None] * freqs[None, :]
     cosine, sine = jnp.cos(angles), jnp.sin(angles)
     shift = (HD**0.5 * LOG2E) * jnp.max(jnp.abs(gain_q)) * jnp.max(jnp.abs(gain_k))
     shift = shift.reshape(1)
 
-    tiles = block // TILE
-    q_first = block_start + TILE * jnp.arange(tiles, dtype=jnp.int32)
-    tile_first = first.reshape(tiles, TILE)
-    low = tile_first[:, 0] // KEYS
-    high = (q_first + TILE - 1) // KEYS + 1
-    inner_low = jnp.minimum((tile_first[:, TILE - 1] + KEYS - 1) // KEYS, high)
+    core, chip = fsdp % 2, fsdp // 2
+    strip_ids = segments.reshape(fsdp_count // 2, 2, block // STRIP, STRIP)
+    strip_ids = lax.dynamic_index_in_dim(strip_ids, core, 1, keepdims=False)
+    strip_ids = lax.dynamic_index_in_dim(strip_ids, chip, 1, keepdims=False)
+    first = firsts(strip_ids.reshape(-1))
+    strip_first = first.reshape(-1, STRIP)
+    q_first = (2 * jnp.arange(fsdp_count // 2, dtype=jnp.int32) + core) * block + chip * STRIP
+    low = strip_first[:, 0] // KEYS
+    high = (q_first + STRIP - 1) // KEYS + 1
+    inner_low = jnp.minimum((strip_first[:, STRIP - 1] + KEYS - 1) // KEYS, high)
     inner_high = jnp.maximum((q_first + 1) // KEYS, inner_low)
     ranges = jnp.stack([low, inner_low, inner_high, high, q_first])
 
@@ -746,45 +1111,23 @@
     inverse_k = rms_scale(kp)
     q = rotate(qp * inverse_q * gain_q, cosine[:, None, :], sine[:, None, :]).astype(BF16)
     k = rotate(kp * inverse_k * gain_k, cosine, sine).astype(BF16)
-    q = jnp.transpose(q, (1, 0, 2))
-    empty = jnp.zeros_like(q)
-    q_pad = jnp.concatenate([q, empty], axis=2)
-    dy_block, kv = gather(
+    dy_block, kv, q = gather(
         "gather_keys",
         2,
         [(cotangent, 0, (0, 64))],
         [(jnp.concatenate([k, value], axis=1), 0, (0, 512))],
-    )
-
-    sums, totals = forward_attention(ranges, shift, q_pad, first[:, None], kv)
-    totals = totals[:, :, :1]
-    o = sums[:, :, HD:] / totals
-    ob = jnp.transpose(o.astype(BF16), (1, 0, 2)).reshape(block, per_head)
-    ob_block, gate_up, down_w = gather(
-        "gather_attended",
-        3,
-        [(ob, 1, (0, 512))],
-        [(gate_up, 1, (1, 32)), (down_piece, 0, (0, 32))],
-    )
-    gate_w, up_w = gate_up[0], gate_up[1]
+        [q.reshape(block, per_head)],
+    )
+
+    ob, o, totals = forward_attention(ranges, shift, q, first[:, None], kv)
+    ob_own, h1_own, n2, gate_up, down_w = gather_attended(
+        ob, wo, tokens, gain_two[None, :], gate_up, down_piece
+    )
     down_w = down_w.reshape(fsdp_count, PIECE, width)[:, :pieces].reshape(part, width)
 
-    h1 = x + dot_nn(ob_block, wo)
-    inverse_two = rms_scale(h1)
-    n2 = (h1 * inverse_two * gain_two).astype(BF16)
-    gate = dot_nn(n2, gate_w)
-    up = dot_nn(n2, up_w)
-    sig = jax.nn.sigmoid(gate)
-    act = (gate * sig * up).astype(BF16)
-    gact = dot_nt(dy_block, down_w)
-    ggate = (gact * up * sig * (1.0 + gate * (1.0 - sig))).astype(BF16)
-    gup = (gact * gate * sig).astype(BF16)
-    gn2_part = (dot_nt(ggate, gate_w) + dot_nt(gup, up_w)).astype(BF16)
-    branch = dot_nn(act, down_w).astype(BF16)
-    own = lambda array: take(array, seq * rows, rows)
-    h1_own = own(h1)
+    gn2_part, branch, g_gate, g_up, g_down = feed_forward(n2, dy_block, gate_up, down_w)
     by_core = lambda array: array.reshape(8, 2, -1, array.shape[-1])
-    g_down = dot_tn(act, dy_block).astype(BF16).reshape(fsdp_count, pieces, width)
+    g_down = g_down.reshape(fsdp_count, pieces, width)
     g_down = jnp.pad(g_down, ((0, 0), (0, PIECE - pieces), (0, 0)))
     gh1, gb, gain_two_term, go, g_gate, g_up, g_down = scatter_hidden(
         gn2_part.reshape(seq_count, rows, width),
@@ -792,28 +1135,16 @@
         cotangent,
         gain_two[None, :],
         wo,
-        by_core(dot_tn(n2, ggate).astype(BF16)),
-        by_core(dot_tn(n2, gup).astype(BF16)),
+        by_core(g_gate),
+        by_core(g_up),
         by_core(g_down.reshape(-1, width)),
     )
     g_down = lax.ppermute(g_down, both, back_pairs)
-    g_out = dot_tn(own(ob_block), gb).astype(BF16)
-    go = jnp.transpose(go.reshape(block, H // KVH, HD), (1, 0, 2)).astype(F32)
-    ga = (go / totals).astype(BF16)
-    ga_pad = jnp.concatenate([empty, ga], axis=2)
-    delta = jnp.sum(go * o, axis=2) / totals[:, :, 0]
-
-    tiled = lambda a: jnp.transpose(a.reshape(2, tiles, TILE), (1, 0, 2)).reshape(tiles, 1, 2 * TILE)
+    g_out = dot_tn(ob_own, gb).astype(BF16)
     gq, gkv = backward_attention(
-        ranges,
-        shift,
-        q_pad,
-        ga_pad,
-        tiled(delta),
-        tiled(jnp.stack([first, first])),
-        kv,
-    )
-    layer_out, gkv, g_out, g_gate, g_up, g_down = scatter_keys(
+        ranges, shift, q, go, o, totals, strip_first[:, None, :], kv
+    )
+    layer_out, gkv, g_out, g_gate, g_up, g_down, gq = scatter_keys(
         branch.reshape(seq_count, rows, width),
         h1_own,
         by_core(gkv),
@@ -821,8 +1152,9 @@
         g_gate,
         g_up,
         g_down,
-    )
-    gq = jnp.transpose((gq[:, :, :HD] * HD**-0.5).astype(BF16), (1, 0, 2)).astype(F32)
+        gq,
+    )
+    gq = gq.astype(F32).reshape(block, H // KVH, HD)
     gk = gkv[:, :HD].astype(F32)
     gv = gkv[:, HD:]
     gain_q_term, gqp = norm_back(

time: 502 us -> 414 us (0.82)
  the two profiles are of different devices: /device:TPU:50 before, /device:TPU:8 now
where the time goes in v2:
time: 414 us; the launch traced here: 409 us
  Pallas kernels  336 us (81%)
  local copies, waits for them, and re-layouts  31.8 us (8%)
  other arithmetic  21.7 us (5%)
  matrix products  9.36 us (2%)
  starting transfers between devices  8.05 us (2%)
    pallas_call x2, Pallas kernels, gather(): pl.pallas_call(kernel, out_shape=shapes, in_specs=[HBM] * every, out_spec...  64.2 us
    pallas_call x1, Pallas kernels, scatter_keys(): pl.pallas_call(keys_kernel, out_shape=[jax.ShapeDtypeStruct((rows, width)...  59 us
    pallas_call x1, Pallas kernels, scatter_hidden(): pl.pallas_call(hidden_kernel, out_shape=[jax.ShapeDtypeStruct((rows, widt...  48.2 us
    pallas_call x1, Pallas kernels, gather_attended(): pl.pallas_call(attended_kernel, out_shape=[jax.ShapeDtypeStruct((rows, wi...  42.6 us
    pallas_call x1, Pallas kernels, scatter_input(): pl.pallas_call(input_kernel, out_shape=[jax.ShapeDtypeStruct((rows, width...  41.5 us
    pallas_call x1, Pallas kernels, backward_attention(): pl.pallas_call(backward_kernel, grid_spec=pltpu.PrefetchScalarGridSpec(nu...  36.7 us
    pallas_call x1, Pallas kernels, feed_forward(): pl.pallas_call(feed_kernel, out_shape=[jax.ShapeDtypeStruct(shape, BF16)...  22.4 us
    pallas_call x1, Pallas kernels, forward_attention(): pl.pallas_call(forward_kernel, grid_spec=pltpu.PrefetchScalarGridSpec(num...  21 us
  transfers between devices with their start and end apart: 2, of which 0 were waited for; matrix products, arithmetic and copies ran while one was open for 7% of the time, Pallas kernels for 30%

profile of v2, /device:TPU:8, one launch (start us, length us, event | category | flops | bytes accessed | tf_op | source)
XLA Modules:
  0.0 409.1 jit_solution(13635117725328306564)
XLA Ops:
  0.7 1.0 copy-done
  1.7 4.8 %collective-permute-start = (bf16[36,1024]{1,0:T(8,128)(2,1)S(1)}, bf16[36,1024]{1,0:T(8,128)(2,1)}, u32[]{:S(2)}, u32[]{:S(2)}) collective-permute-start(bf16[36,1024]{1,0:T(8,128)(2,1)S(1)} %constant_dynamic-slice_fusion), channel_id=1, source_target_pairs={{0,0},{2,16},{4,32},{6,48},{8,64},{10,80},{12,96},{14,112},{16,1},... | collective-permute-start | bytes 221192 | tf_op jit(solution)/shard_map/ppermute | solution.py:1053
  6.6 0.8 pad_maximum_fusion.10
  8.1 0.8 constant_dynamic-slice_fusion.1
  9.7 30.7 %gather_inputs.1 = (bf16[1024,1024]{1,0:T(8,128)(2,1)}, bf16[1280,256]{1,0:T(8,128)(2,1)}, bf16[1024,1024]{1,0:T(8,128)(2,1)}) custom-call(bf16[128,1024]{1,0:T(8,128)(2,1)} %tokens.3, bf16[80,256]{1,0:T(8,128)(2,1)} %fusion.26.refs_1_, bf16[64,1024]{1,0:T(8,128)(2,1)} %refs_2_.1), custom_call_target="tpu_custom_call" | custom-call | tf_op jit(solution)/shard_map/gather_inputs/pallas_call | solution.py:610
  40.3 0.9 slice.129
  41.2 1.1 slice.133
  43.8 2.2 fusion.4
  46.1 1.0 fusion.10
  48.0 1.0 copy.102.first_ref
  50.0 0.8 copy.116
  51.6 3.2 fusion.12
  54.8 1.2 copy.104
  56.4 0.8 copy.101.refs_2_
  58.6 1.1 dynamic-slice_bitcast_fusion
  59.7 2.1 pad_maximum_fusion.4.refs_1_
  61.7 33.5 %gather_keys.1 = (bf16[1024,1024]{1,0:T(8,128)(2,1)}, bf16[16384,128]{1,0:T(8,128)(2,1)}, bf16[1024,128]{1,0:T(8,128)(2,1)}) custom-call(bf16[128,1024]{1,0:T(8,128)(2,1)} %dy.1, bf16[1024,128]{1,0:T(8,128)(2,1)} %pad_maximum_fusion.4.refs_1_, bf16[1024,128]{1,0:T(8,128)(2,1)} %copy.101.refs_2_), custom_call_target="tpu_custom_call" | custom-call | tf_op jit(solution)/shard_map/gather_keys/pallas_call | solution.py:610
  95.8 21.0 %attention_forward.1 = (bf16[1024,128]{1,0:T(8,128)(2,1)}, f32[8,256,128]{2,1,0:T(8,128)}, f32[8,256,128]{2,1,0:T(8,128)}) custom-call(s32[5,8]{1,0:T(8,128)} %stack.8.ranges_ref, f32[1]{0:T(128)} %bitcast.8.shift_ref, bf16[1024,128]{1,0:T(8,128)(2,1)} %get-tuple-element.53.query_ref, s32[1024,1]{1,0:T(8,128)} %copy.102.first_ref, ...), custom_call_target="tpu_custom_call" | custom-call | flops 8000000000 | bytes 8000000 | tf_op jit(solution)/shard_map/attention_forward/pallas_call | solution.py:138
  117.5 1.5 pad.17.down
  119.0 42.6 %gather_attended.1 = (bf16[128,1024]{1,0:T(8,128)(2,1)}, f32[128,1024]{1,0:T(8,128)}, bf16[1024,1024]{1,0:T(8,128)(2,1)}, bf16[2,1024,576]{2,1,0:T(8,128)(2,1)}, bf16[768,1024]{1,0:T(8,128)(2,1)}) custom-call(bf16[1024,128]{1,0:T(8,128)(2,1)} %get-tuple-element.55.ob, bf16[1024,1024]{1,0:T(8,128)(2,1)} %get-tuple-element.56.wo, bf16[128,1024]{1,0:T(8,128)(2,1)} %tokens.3, ...), custom_call_target="tpu_custom_call" | custom-call | tf_op jit(solution)/shard_map/gather_attended/pallas_call | solution.py:657
  161.7 1.4 slice.142
  163.1 1.1 reshape.620.down_ref
  164.3 22.4 %feed_forward.1 = (bf16[1024,1024]{1,0:T(8,128)(2,1)}, bf16[1024,1024]{1,0:T(8,128)(2,1)}, bf16[1024,576]{1,0:T(8,128)(2,1)}, bf16[1024,576]{1,0:T(8,128)(2,1)}, bf16[576,1024]{1,0:T(8,128)(2,1)}) custom-call(bf16[1024,1024]{1,0:T(8,128)(2,1)} %get-tuple-element.57.n2_ref, bf16[1024,1024]{1,0:T(8,128)(2,1)} %get-tuple-element.58.dy_ref, ...), custom_call_target="tpu_custom_call" | custom-call | flops 11000000512 | bytes 16000000 | tf_op jit(solution)/shard_map/feed_forward/pallas_call | solution.py:290
  186.7 1.4 reshape.625
  188.1 1.4 pad.18
  189.5 48.2 %scatter_hidden.1 = (f32[128,1024]{1,0:T(8,128)}, bf16[128,1024]{1,0:T(8,128)(2,1)}, f32[1,1024]{1,0:T(1,128)}, bf16[1024,128]{1,0:T(8,128)(2,1)}, bf16[64,576]{...) custom-call(bf16[8,128,1024]{2,1,0:T(8,128)(2,1)} %bitcast.110, f32[128,1024]{1,0:T(8,128)} %get-tuple-element.62.h1, ...), custom_call_target="tpu_custom_call" | custom-call | tf_op jit(solution)/shard_map/scatter_hidden/pallas_call | solution.py:872
  237.7 3.2 collective-permute-start.1
  241.0 3.0 convolution_convert_fusion
  244.0 36.7 %attention_backward.1 = (bf16[1024,128]{1,0:T(8,128)(2,1)}, bf16[16384,128]{1,0:T(8,128)(2,1)}) custom-call(s32[5,8]{1,0:T(8,128)} %stack.8.ranges_ref, f32[1]{0:T(128)} %bitcast.8.shift_ref, bf16[1024,128]{1,0:T(8,128)(2,1)} %get-tuple-element.53.query_ref, bf16[1024,128]{1,0:T(8,128)(2,1)} %get-tuple-element.67.grad_ref, ...), custom_call_target="tpu_custom_call" | custom-call | flops 20000000000 | bytes 16000000 | tf_op jit(solution)/shard_map/attention_backward/pallas_call | solution.py:218
  281.5 59.0 %scatter_keys.1 = (bf16[128,1024]{1,0:T(8,128)(2,1)}, bf16[1024,128]{1,0:T(8,128)(2,1)}, bf16[64,1024]{1,0:T(8,128)(2,1)}, bf16[512,576]{1,0:T(8,128)(2,1)}, bf1...) custom-call(bf16[8,128,1024]{2,1,0:T(8,128)(2,1)} %bitcast.109, ...), custom_call_target="tpu_custom_call" | custom-call | tf_op jit(solution)/shard_map/scatter_keys/pallas_call | solution.py:936
  340.5 1.1 copy.103
  342.3 2.5 fusion.19
  346.1 2.8 convolution_convert_fusion.1
  348.9 2.6 fusion.3
  352.0 0.9 pad_maximum_fusion.pack
  352.9 41.5 %scatter_input.1 = (f32[128,1024]{1,0:T(8,128)}, bf16[640,256]{1,0:T(8,128)(2,1)}, bf16[512,1024]{1,0:T(8,128)(2,1)}) custom-call(bf16[8,128,1024]{2,1,0:T(8,128)(2,1)} %bitcast.107, bf16[128,1024]{1,0:T(8,128)(2,1)} %tokens.3, f32[1,1024]{1,0:T(1,128)} %broadcast_in_dim_reshape.8.gain, f32[128,1024]{1,0:T(8,128)} %get-tuple-element.80.gh1, ...), custom_call_target="tpu_custom_call" | custom-call | tf_op jit(solution)/shard_map/scatter_input/pallas_call | solution.py:984
  394.4 0.9 fusion.27
  396.4 1.7 copy_bitcast_fusion
  398.1 1.1 convert_bitcast_fusion.2
  399.4 0.8 reshape.638
  400.3 0.8 reshape.637
  401.1 0.9 convert_reduce_fusion
  402.0 0.8 copy.111
  402.8 1.3 reshape.640
  404.3 0.8 copy.112
  405.0 1.3 reshape.641
  406.5 1.1 reshape.642
  408.3 0.8 copy.125
  (117 shorter events, 12.9 us)
Async XLA Ops:
  0.6 1.1 copy-start
  1.7 115.8 %collective-permute-start = (bf16[36,1024]{1,0:T(8,128)(2,1)S(1)}, bf16[36,1024]{1,0:T(8,128)(2,1)}, u32[]{:S(2)}, u32[]{:S(2)}) collective-permute-start(bf16[36,1024]{1,0:T(8,128)(2,1)S(1)} %constant_dynamic-slice_fusion), channel_id=1, source_target_pairs={{0,0},{2,16},{4,32},{6,48},{8,64},{10,80},{12,96},{14,112},{16,1},... | collective-permute-start | bytes 221192 | tf_op jit(solution)/shard_map/ppermute | solution.py:1053
  6.6 44.9 %copy-start.22 = (f32[32]{0:T(128)}, f32[32]{0:T(128)S(1)}, u32[]{:S(2)}) copy-start(f32[32]{0:T(128)S(1)} %multiply_power_fusion) | copy-start | bytes 388
  42.3 4.8 %copy-start.9 = (bf16[16,64,256]{2,1,0:T(8,128)(2,1)}, bf16[16,64,256]{2,1,0:T(8,128)(2,1)S(1)}, u32[]{:S(2)}) copy-start(bf16[16,64,256]{2,1,0:T(8,128)(2,1)S(1)} %slice.133) | copy-start | bytes 1572868
  43.1 3.9 copy-start.17
  43.8 2.2 copy-start.2
  46.0 1.0 copy-start.20
  46.1 1.1 copy-start.15
  47.8 3.8 copy-start.16
  189.5 51.5 %copy-start.12 = (bf16[128,1024]{1,0:T(8,128)(2,1)S(1)}, bf16[128,1024]{1,0:T(8,128)(2,1)}, u32[]{:S(2)}) copy-start(bf16[128,1024]{1,0:T(8,128)(2,1)} %get-tuple-element.71) | copy-start | bytes 786436
  237.7 43.1 %collective-permute-start.1 = (bf16[48,1024]{1,0:T(8,128)(2,1)}, bf16[48,1024]{1,0:T(8,128)(2,1)S(1)}, u32[]{:S(2)}, u32[]{:S(2)}) collective-permute-start(bf16[48,1024]{1,0:T(8,128)(2,1)} %get-tuple-element.75), channel_id=1, source_target_pairs={{0,0},{16,2},{32,4},{48,6},{64,8},{80,10},{96,12},{112,14},{1,16},... | collective-permute-start | bytes 294920 | tf_op jit(solution)/shard_map/ppermute | solution.py:1142
  244.0 36.7 %copy-start.19 = (f32[1,1024]{1,0:T(1,128)S(1)}, f32[1,1024]{1,0:T(1,128)}, u32[]{:S(2)}) copy-start(f32[1,1024]{1,0:T(1,128)} %get-tuple-element.81) | copy-start | bytes 12292
  280.8 0.6 copy-start.14
  340.5 1.4 copy-start.5
  341.6 0.7 copy-start.23
  345.3 0.8 copy-start.18
  345.3 0.8 copy-start.21
  346.1 2.8 copy-start.3
  346.1 2.8 copy-start.10
  394.4 6.7 %copy-start.4 = (bf16[512,1024]{1,0:T(8,128)(2,1)S(1)}, bf16[512,1024]{1,0:T(8,128)(2,1)}, u32[]{:S(2)}) copy-start(bf16[512,1024]{1,0:T(8,128)(2,1)} %get-tuple-element.85) | copy-start | bytes 3145732
  396.4 5.5 %copy-start.7 = (bf16[512,576]{1,0:T(8,128)(2,1)S(1)}, bf16[512,576]{1,0:T(8,128)(2,1)}, u32[]{:S(2)}) copy-start(bf16[512,576]{1,0:T(8,128)(2,1)} %get-tuple-element.86) | copy-start | bytes 1769476
  402.0 2.1 copy-start.6
  404.2 2.1 copy-start.8
  406.3 1.3 copy-start.13
  406.4 2.0 copy-start.11
  406.4 2.8 copy-start.1

commit v3 on v2

--- a/solution.py
+++ b/solution.py
@@ -24,31 +24,11 @@
 PIECE = 48
 
 
-def rms_scale(values):
-    return lax.rsqrt(jnp.mean(values * values, axis=-1, keepdims=True) + EPSILON)
-
-
-def norm_back(values, inverse, gain, grad):
-    normalized = values * inverse
-    gain_term = jnp.sum(grad * normalized, axis=tuple(range(grad.ndim - 1)))
-    weighted = grad * gain
-    inner = jnp.mean(weighted * normalized, axis=-1, keepdims=True)
-    return (gain_term, inverse * (weighted - normalized * inner))
-
-
 def doc_starts(segments):
     labels = jnp.arange(DOCS, dtype=jnp.int32)
     member = (segments[None, :] == labels[:, None]).astype(jnp.int32)
     lengths = jnp.sum(member, axis=1)
     return jnp.cumsum(lengths) - lengths
-
-
-def rotate(values, cosine, sine):
-    half = values.shape[-1] // 2
-    first, second = values[..., :half], values[..., half:]
-    return jnp.concatenate(
-        [first * cosine - second * sine, second * cosine + first * sine], axis=-1
-    )
 
 
 def dot_nt(a, b):
@@ -244,64 +224,6 @@
         ),
         name="attention_backward",
     )(ranges, shift, query, grad, o, totals, first, kv)
-
-
-def feed_kernel(
-    n2_ref, dy_ref, weights_ref, down_ref,
-    gn2_ref, branch_ref, gate_out, up_out, down_out,
-    act_ref, ggate_ref, gup_ref,
-):
-    count, width = n2_ref.shape
-
-    def tokens(t, _):
-        at = pl.ds(pl.multiple_of(t * FEED, FEED), FEED)
-        n2 = n2_ref[at, :]
-        gate = dot_nn(n2, weights_ref[0])
-        up = dot_nn(n2, weights_ref[1])
-        gact = dot_nt(dy_ref[at, :], down_ref[...])
-        sig = jax.nn.sigmoid(gate)
-        silu = gate * sig
-        act = (silu * up).astype(BF16)
-        ggate = (gact * up * sig * (1.0 + gate * (1.0 - sig))).astype(BF16)
-        gup = (gact * silu).astype(BF16)
-        act_ref[at, :] = act
-        ggate_ref[at, :] = ggate
-        gup_ref[at, :] = gup
-        gn2_ref[at, :] = (dot_nt(ggate, weights_ref[0]) + dot_nt(gup, weights_ref[1])).astype(BF16)
-        branch_ref[at, :] = dot_nn(act, down_ref[...]).astype(BF16)
-        return 0
-
-    lax.fori_loop(0, count // FEED, tokens, 0)
-
-    def columns(c, _):
-        at = pl.ds(pl.multiple_of(c * FEED, FEED), FEED)
-        n2 = n2_ref[:, at]
-        gate_out[at, :] = dot_tn(n2, ggate_ref[...]).astype(BF16)
-        up_out[at, :] = dot_tn(n2, gup_ref[...]).astype(BF16)
-        down_out[:, at] = dot_tn(act_ref[...], dy_ref[:, at]).astype(BF16)
-        return 0
-
-    lax.fori_loop(0, width // FEED, columns, 0)
-
-
-def feed_forward(n2, dy, weights, down):
-    part = down.shape[0]
-    count, width = n2.shape
-    return pl.pallas_call(
-        feed_kernel,
-        out_shape=[
-            jax.ShapeDtypeStruct(shape, BF16)
-            for shape in [(count, width)] * 2 + [(width, part)] * 2 + [(part, width)]
-        ],
-        in_specs=[IN_VMEM] * 4,
-        out_specs=[IN_VMEM] * 5,
-        scratch_shapes=[pltpu.VMEM((count, part), BF16)] * 3,
-        compiler_params=pltpu.CompilerParams(vmem_limit_bytes=VMEM),
-        cost_estimate=pl.CostEstimate(
-            flops=11 * 10**9, bytes_accessed=16 * 10**6, transcendentals=10**6
-        ),
-        name="feed_forward",
-    )(n2, dy, weights, down)
 
 
 MESH = pl.DeviceIdType.MESH
@@ -474,9 +396,10 @@
             self.own.wait()
 
 
-def greet_for_swap(places, peers, senders):
+def greet_for_swaps(places, peers):
     barrier = pltpu.get_barrier_semaphore()
-    peers = peers + senders[1:]
+    senders, others = places.heads()[1], places.owners()[1]
+    peers = peers + senders[1:] + others[1:]
     for peer in peers:
         pl.semaphore_signal(barrier, inc=1, device_id=peer, device_id_type=MESH)
 
@@ -486,8 +409,9 @@
 
     @pl.when(jnp.logical_not(places.stays))
     def _():
-        pl.semaphore_signal(barrier, inc=1, device_id=senders[0], device_id_type=MESH)
-        pl.semaphore_wait(barrier, len(peers) + 1)
+        for peer in (senders[0], others[0]):
+            pl.semaphore_signal(barrier, inc=1, device_id=peer, device_id_type=MESH)
+        pl.semaphore_wait(barrier, len(peers) + 2)
 
 
 def strips_at(ref, index):
@@ -590,11 +514,14 @@
         srcs, outs = refs[:every], refs[every : 2 * every]
         copies, places = Copies(*refs[2 * every :]), Places()
         greet(places.gather_peers() + (places.strip_peers() if strips else []))
-        moved = [Strips(copies, places, srcs[i], outs[i]) for i in range(count, every)]
         stages = []
-        for i, (_, axis, split) in enumerate(items):
+        order = list(range(count))
+        for i in order[::-1] if strips else order:
+            _, axis, split = items[i]
             make = seq_gather if i < len(seq_items) else fsdp_gather
             stages.append(make(copies, places, srcs[i], outs[i], axis, split))
+            next(stages[-1])
+        moved = [Strips(copies, places, srcs[i], outs[i]) for i in range(count, every)]
         run_stages(stages)
         for item in moved:
             item.wait()
@@ -616,65 +543,6 @@
         compiler_params=params(name_id),
         name=name,
     )(*[item[0] for item in items], *strips)
-
-
-def attended_kernel(
-    ob, wo, tokens, gain, gate_up, down,
-    own_ref, h1_ref, n2_all, gate_up_all, down_all,
-    own, n2, tags, ends, send, recv, local_sem,
-):
-    copies, places = Copies(send, recv, local_sem), Places()
-    strips, owners = places.owners()
-    _, senders = places.heads()
-    greet_for_swap(places, places.gather_peers(), senders)
-    landing = heads_at(own, places.seq)
-    sends = [(strips_at(ob, strip), landing, peer) for strip, peer in zip(strips, owners)]
-    swap = Swap(copies, tags, ends, places.seq, places.stays, sends)
-    stages = [
-        fsdp_gather(copies, places, gate_up, gate_up_all, 1, (1, 32)),
-        fsdp_gather(copies, places, down, down_all, 0, (0, 32)),
-    ]
-    for stage in stages:
-        next(stage)
-    swap.wait(lambda sender: heads_at(own, sender))
-    own_ref[...] = own[...]
-
-    def columns(j, _):
-        at = pl.ds(pl.multiple_of(j * 256, 256), 256)
-        h1_ref[:, at] = tokens[:, at].astype(F32) + dot_nn(own[...], wo[:, at])
-        return 0
-
-    lax.fori_loop(0, 4, columns, 0)
-    value = h1_ref[...]
-    n2[...] = (value * unit_rows(value) * gain[...]).astype(BF16)
-    stages.insert(0, seq_gather(copies, places, n2, n2_all, 0, (0, 64)))
-    run_stages(stages)
-    copies.finish()
-
-
-def gather_attended(ob, wo, tokens, gain, gate_up, down):
-    rows, width = tokens.shape
-    return pl.pallas_call(
-        attended_kernel,
-        out_shape=[
-            jax.ShapeDtypeStruct((rows, width), BF16),
-            jax.ShapeDtypeStruct((rows, width), F32),
-            jax.ShapeDtypeStruct((8 * rows, width), BF16),
-            jax.ShapeDtypeStruct((2, 16 * gate_up.shape[1], gate_up.shape[2]), BF16),
-            jax.ShapeDtypeStruct((16 * down.shape[0], width), BF16),
-        ],
-        in_specs=[HBM] + [IN_VMEM] * 3 + [HBM] * 2,
-        out_specs=[IN_VMEM] * 2 + [HBM] * 3,
-        scratch_shapes=[
-            pltpu.VMEM((rows, width), BF16),
-            pltpu.VMEM((rows, width), BF16),
-            pltpu.SemaphoreType.DMA((8,)),
-            pltpu.SemaphoreType.DMA((2,)),
-        ]
-        + semaphores(7 + 9 + 2 * 17, 3),
-        compiler_params=params(3),
-        name="gather_attended",
-    )(ob, wo, tokens, gain, gate_up, down)
 
 
 class RingSum:
@@ -811,84 +679,202 @@
     return lax.rsqrt(jnp.mean(values * values, axis=-1, keepdims=True) + EPSILON)
 
 
+def spread(pieces, part):
+    shape = (pieces * PIECE, part)
+    row = lax.broadcasted_iota(jnp.int32, shape, 0)
+    column = lax.broadcasted_iota(jnp.int32, shape, 1)
+    size = part // pieces
+    inside = lax.rem(row, PIECE)
+    hit = (lax.div(row, PIECE) * size + inside == column) & (inside < size)
+    return jnp.where(hit, 1.0, 0.0).astype(BF16)
+
+
 def hidden_kernel(
-    part, h1, dy, gain, wo, gate, up, down,
-    gh1_ref, gb_ref, term_ref, go_ref, gate_out, up_out, down_out,
-    go_own, tags, ends, *scratch,
+    ob, wo, tokens, dy_own, gain, gate_up, down, dy,
+    own_ref, h1_ref, branch_ref, gh1_ref, gb_ref, term_ref, go_ref, gate_out, up_out, down_out,
+    own, n2, go_own, n2_all, weights, down_pad, down_all, act, ggate, gup, gn2_all, held,
+    gate_part, up_part, down_part, *scratch,
 ):
+    sums_at = scratch[:15]
+    tags, ends, tags_back, ends_back = scratch[15:19]
     copies, places = Copies(*scratch[19:]), Places()
+    others = [places.on_seq(places.other_seq(d)) for d in range(1, 8)]
+    greet_for_swaps(places, places.gather_peers() + others)
+    rows, width = own.shape
+    part = down_all.shape[0]
+    pieces = down_pad.shape[0] // PIECE
+
+    strips, owners = places.owners()
     heads, workers = places.heads()
-    _, senders = places.owners()
-    greet_for_swap(places, places.gather_peers(), senders)
-    hidden = SeqSum(copies, places, part, scratch[:4], 64)
+    landing = heads_at(own, places.seq)
+    sends = [(strips_at(ob, strip), landing, peer) for strip, peer in zip(strips, owners)]
+    swap = Swap(copies, tags, ends, places.seq, places.stays, sends)
+    gathers = [
+        fsdp_gather(copies, places, gate_up, weights, 1, (1, 32)),
+        fsdp_gather(copies, places, down, down_pad, 0, (0, 32)),
+    ]
+    for stage in gathers:
+        next(stage)
+    swap.wait(lambda sender: heads_at(own, sender))
+    own_ref[...] = own[...]
+
+    def project(j, _):
+        at = pl.ds(pl.multiple_of(j * 256, 256), 256)
+        h1_ref[:, at] = tokens[:, at].astype(F32) + dot_nn(own[...], wo[:, at])
+        return 0
+
+    lax.fori_loop(0, width // 256, project, 0)
+    value = h1_ref[...]
+    inverse = unit_rows(value)
+    n2[...] = (value * inverse * gain[...]).astype(BF16)
+    tokens_in = seq_gather(copies, places, n2, n2_all, 0, (0, 64))
+    next(tokens_in)
+    for _ in range(3):
+        for stage in gathers:
+            next(stage)
+        if _ < 2:
+            next(tokens_in)
+    run_stages(gathers)
+    matrix = spread(pieces, part)
+
+    def pack_down(j, _):
+        at = pl.ds(pl.multiple_of(j * 256, 256), 256)
+        down_all[:, at] = dot_tn(matrix, down_pad[:, at]).astype(BF16)
+        return 0
+
+    lax.fori_loop(0, width // 256, pack_down, 0)
+
+    arrivals = []
+
+    def feed(step):
+        base = lax.div(ring_step(places.seq, step), 2) * 2 * rows
+        at = pl.ds(pl.multiple_of(base, 2 * rows), 2 * rows)
+        values = n2_all[at, :]
+        gate = dot_nn(values, weights[0])
+        up = dot_nn(values, weights[1])
+        gact = dot_nt(dy[at, :], down_all[...])
+        sig = jax.nn.sigmoid(gate)
+        silu = gate * sig
+        act_here = (silu * up).astype(BF16)
+        gg = (gact * up * sig * (1.0 + gate * (1.0 - sig))).astype(BF16)
+        gu = (gact * silu).astype(BF16)
+        act[at, :] = act_here
+        ggate[at, :] = gg
+        gup[at, :] = gu
+        gn2_all[at, :] = (dot_nt(gg, weights[0]) + dot_nt(gu, weights[1])).astype(BF16)
+        for flip in (1, 0):
+            if step == 0 and flip == 0:
+                continue
+            peer = ring_step(places.seq, step)
+            peer = pair_of(peer) if flip else peer
+            arrivals.append(
+                copies.remote(
+                    gn2_all.at[pl.ds(pl.multiple_of(peer * rows, rows), rows), :],
+                    held.at[2 * step + flip],
+                    places.on_seq(peer),
+                )
+            )
+        branch_ref[at, :] = dot_nn(act_here, down_all[...]).astype(BF16)
+
+    tokens_in.send(None)
+    kept_first = copies.locals[-1]
+    kept_first.wait()
+    feed(0)
+    feed(1)
+    feed(3)
+    next(tokens_in)
+    next(tokens_in)
+    feed(2)
+
+    def columns(c, _):
+        at = pl.ds(pl.multiple_of(c * 256, 256), 256)
+        values = n2_all[:, at]
+        two = pl.ds(c * 2, 2)
+        shape = (2, 2) + gate_part.shape[2:]
+        gate_part[two] = dot_tn(values, ggate[...]).astype(BF16).reshape(shape)
+        up_part[two] = dot_tn(values, gup[...]).astype(BF16).reshape(shape)
+        g_down = dot_nn(matrix, dot_tn(act[...], dy[:, at]).astype(BF16)).astype(BF16)
+        down_part[:, :, :, at] = g_down.reshape((8, 2, PIECE, 256))
+        return 0
+
+    lax.fori_loop(0, width // 256, columns, 0)
     sums = [
-        FsdpSum(copies, places, gate, scratch[4:9], 32),
-        FsdpSum(copies, places, up, scratch[9:14], 32),
-        FsdpSum(copies, places, down, scratch[14:19], 32),
+        FsdpSum(copies, places, gate_part, sums_at[:5], 32),
+        FsdpSum(copies, places, up_part, sums_at[5:10], 32),
+        FsdpSum(copies, places, down_part, sums_at[10:15], 32),
     ]
-    for item in [hidden] + sums:
+    for item in sums:
         item.ready()
         item.send()
-    for item in [hidden] + sums:
-        item.relay()
-    for item in [hidden] + sums:
-        item.cross()
-    gn2 = hidden.total()
-    value = h1[...]
+    gn2 = gn2_all[pl.ds(pl.multiple_of(places.seq * rows, rows), rows), :].astype(F32)
+    for copy in arrivals:
+        copy.wait_recv()
+    for slot_index in range(1, 8):
+        gn2 += held[slot_index].astype(F32)
+    value = h1_ref[...]
     inverse = unit_rows(value)
     normed = value * inverse
     term_ref[...] = jnp.sum(gn2 * normed, axis=0, keepdims=True)
     weighted = gn2 * gain[...]
     inner = jnp.mean(weighted * normed, axis=-1, keepdims=True)
-    gh1 = dy[...].astype(F32) + inverse * (weighted - normed * inner)
+    gh1 = dy_own[...].astype(F32) + inverse * (weighted - normed * inner)
     gh1_ref[...] = gh1
     gb_ref[...] = gh1.astype(BF16)
 
-    def columns(j, _):
+    def project_back(j, _):
         begin = pl.multiple_of(j * 256, 256)
         go_own[:, pl.ds(begin, 256)] = dot_nt(gb_ref[...], wo[pl.ds(begin, 256), :]).astype(BF16)
         return 0
 
-    lax.fori_loop(0, 4, columns, 0)
+    lax.fori_loop(0, width // 256, project_back, 0)
     landing = strips_at(go_ref, places.chip)
     sends = [(heads_at(go_own, head), landing, peer) for head, peer in zip(heads, workers)]
-    swap = Swap(copies, tags, ends, places.chip, places.stays, sends)
+    swap_back = Swap(copies, tags_back, ends_back, places.chip, places.stays, sends)
+    for item in sums:
+        item.relay()
+    for item in sums:
+        item.cross()
     for item, out in zip(sums, (gate_out, up_out, down_out)):
         out[...] = item.total().astype(BF16)
-    swap.wait(lambda sender: strips_at(go_ref, sender))
+    swap_back.wait(lambda sender: strips_at(go_ref, sender))
     copies.finish()
 
 
-def scatter_hidden(part, h1, dy, gain, wo, gate, up, down):
-    rows, width = h1.shape
-    shapes = [a.shape[2:] for a in (gate, up, down)]
-    scratch = [
-        pltpu.VMEM((rows, width), BF16),
-        pltpu.SemaphoreType.DMA((8,)),
-        pltpu.SemaphoreType.DMA((2,)),
-    ] + seq_buffers((rows, width))
-    for shape in shapes:
+def hidden_block(ob, wo, tokens, dy_own, gain, gate_up, down, dy):
+    rows, width = tokens.shape
+    shard, part = gate_up.shape[1:]
+    slices = [(shard, part), (shard, part), (PIECE, width)]
+    block = (8 * rows, width)
+    vmem = [(rows, width)] * 3 + [block, (2, width, part), (16 * PIECE, width), (part, width)]
+    vmem += [(8 * rows, part)] * 3 + [block, (8, rows, width)]
+    vmem += [(8, 2) + shape for shape in slices]
+    scratch = [pltpu.VMEM(shape, BF16) for shape in vmem]
+    for shape in slices:
         scratch += fsdp_buffers(shape)
+    scratch += [pltpu.SemaphoreType.DMA((n,)) for n in (8, 2, 8, 2)]
     return pl.pallas_call(
         hidden_kernel,
         out_shape=[
+            jax.ShapeDtypeStruct((rows, width), BF16),
+            jax.ShapeDtypeStruct((rows, width), F32),
+            jax.ShapeDtypeStruct(block, BF16),
             jax.ShapeDtypeStruct((rows, width), F32),
             jax.ShapeDtypeStruct((rows, width), BF16),
             jax.ShapeDtypeStruct((1, width), F32),
             jax.ShapeDtypeStruct((8 * rows, 128), BF16),
         ]
-        + [jax.ShapeDtypeStruct(shape, BF16) for shape in shapes],
-        in_specs=[HBM] + [IN_VMEM] * 4 + [HBM] * 3,
-        out_specs=[IN_VMEM] * 3 + [HBM] + [IN_VMEM] * 3,
-        scratch_shapes=scratch + semaphores(SEQ_COPIES + 7 + 3 * FSDP_COPIES, 4),
+        + [jax.ShapeDtypeStruct(shape, BF16) for shape in slices],
+        in_specs=[HBM] + [IN_VMEM] * 4 + [HBM] * 2 + [IN_VMEM],
+        out_specs=[IN_VMEM] * 6 + [HBM] + [IN_VMEM] * 3,
+        scratch_shapes=scratch + semaphores(2 * 7 + 9 + 2 * 17 + 7 + 3 * FSDP_COPIES, 6),
         compiler_params=params(4),
-        name="scatter_hidden",
-    )(part, h1, dy, gain, wo, gate, up, down)
+        name="scatter_hidden_block",
+    )(ob, wo, tokens, dy_own, gain, gate_up, down, dy)
 
 
 def keys_kernel(
-    branch, h1, gkv, gout, gate, up, down, gq,
-    layer_ref, gkv_out, gout_out, gate_all, up_all, down_all, gq_out,
+    branch, h1, gkv, gout, gate, up, gq,
+    layer_ref, gkv_out, gout_out, gate_all, up_all, gq_out,
     *scratch,
 ):
     copies, places = Copies(*scratch[14:]), Places()
@@ -902,7 +888,6 @@
     stages = [
         seq_gather(copies, places, gate, gate_all, 0, (0, 32)),
         seq_gather(copies, places, up, up_all, 0, (0, 32)),
-        seq_gather(copies, places, down, down_all, 0, (0, 16)),
     ]
     items = [hidden] + sums
     hidden.ready()
@@ -926,47 +911,66 @@
     copies.finish()
 
 
-def scatter_keys(branch, h1, gkv, gout, gate, up, down, gq):
+def scatter_keys(branch, h1, gkv, gout, gate, up, gq):
     rows, width = h1.shape
     shapes = [a.shape[2:] for a in (gkv, gout)]
     scratch = seq_buffers((rows, width))
     for shape in shapes:
         scratch += fsdp_buffers(shape)
-    wide = [jax.ShapeDtypeStruct((8 * a.shape[0],) + a.shape[1:], BF16) for a in (gate, up, down)]
+    wide = [jax.ShapeDtypeStruct((8 * a.shape[0],) + a.shape[1:], BF16) for a in (gate, up)]
     return pl.pallas_call(
         keys_kernel,
         out_shape=[jax.ShapeDtypeStruct((rows, width), BF16)]
         + [jax.ShapeDtypeStruct(shape, BF16) for shape in shapes]
         + wide
         + [jax.ShapeDtypeStruct(gq.shape, BF16)],
-        in_specs=[HBM, IN_VMEM] + [HBM] * 6,
-        out_specs=[IN_VMEM] * 3 + [HBM] * 4,
-        scratch_shapes=scratch + semaphores(SEQ_COPIES + 2 * FSDP_COPIES + 27 + 7, 7),
+        in_specs=[HBM, IN_VMEM] + [HBM] * 5,
+        out_specs=[IN_VMEM] * 3 + [HBM] * 3,
+        scratch_shapes=scratch + semaphores(SEQ_COPIES + 2 * FSDP_COPIES + 18 + 7, 6),
         compiler_params=params(5),
         name="scatter_keys",
-    )(branch, h1, gkv, gout, gate, up, down, gq)
+    )(branch, h1, gkv, gout, gate, up, gq)
 
 
 def input_kernel(
-    part, tokens, gain, gh1, pack, gout,
-    grad_ref, pack_all, gout_all,
-    small, *scratch,
+    part, tokens, gain, gh1, pack, gout, down,
+    grad_ref, pack_all, down_all,
+    small, gathered, *scratch,
 ):
     copies, places = Copies(*scratch[9:]), Places()
-    greet(places.gather_peers())
+    steps = range(1, 8)
+    greet(places.gather_peers() + [places.on_seq(places.other_seq(d)) for d in steps])
+    hidden = SeqSum(copies, places, part, scratch[:4], 64)
+    hidden.ready()
+    hidden.send()
+    outs = [
+        copies.remote(
+            gout.at[places.other_seq(d)], gathered.at[d], places.on_seq(places.other_seq(d))
+        )
+        for d in steps
+    ]
+    own = copies.here(gout.at[places.seq], gathered.at[0])
     packs = FsdpSum(copies, places, pack, scratch[4:9], 48)
-    hidden = SeqSum(copies, places, part, scratch[:4], 64)
-    for item in (hidden, packs):
-        item.ready()
-        item.send()
-    stages = [seq_gather(copies, places, gout, gout_all, 0, (0, 32))]
+    packs.ready()
+    packs.send()
+    stages = [seq_gather(copies, places, down, down_all, 0, (0, 16))]
     next(stages[0])
-    for item in (packs, hidden):
-        item.relay()
-    for item in (packs, hidden):
-        item.cross()
-    small[...] = packs.total().astype(BF16)
-    stages.append(seq_gather(copies, places, small, pack_all, 0, (0, 48)))
+    packs.relay()
+    hidden.relay()
+    packs.cross()
+    next(stages[0])
+    hidden.cross()
+    own.wait()
+    for copy in outs:
+        copy.wait_recv()
+    rows = pack.shape[2]
+    total = gathered[0].astype(F32)
+    for d in steps:
+        total += gathered[d].astype(F32)
+    small[rows:] = total.astype(BF16)
+    small[:rows] = packs.total().astype(BF16)
+    stages.append(seq_gather(copies, places, small, pack_all, 0, (0, 64)))
+    next(stages[1])
     run_stages(stages)
     gn1 = hidden.total()
     value = tokens[...].astype(F32)
@@ -978,25 +982,136 @@
     copies.finish()
 
 
-def scatter_input(part, tokens, gain, gh1, pack, gout):
+def scatter_input(part, tokens, gain, gh1, pack, gout, down):
     rows, width = gh1.shape
     shape = pack.shape[2:]
+    small = (shape[0] + gout.shape[1], shape[1])
     return pl.pallas_call(
         input_kernel,
         out_shape=[
             jax.ShapeDtypeStruct((rows, width), F32),
-            jax.ShapeDtypeStruct((8 * shape[0], shape[1]), BF16),
-            jax.ShapeDtypeStruct((8 * gout.shape[0], width), BF16),
+            jax.ShapeDtypeStruct((8 * small[0], small[1]), BF16),
+            jax.ShapeDtypeStruct((8 * down.shape[0], width), BF16),
         ],
-        in_specs=[HBM] + [IN_VMEM] * 3 + [HBM] * 2,
+        in_specs=[HBM] + [IN_VMEM] * 3 + [HBM] * 3,
         out_specs=[IN_VMEM] + [HBM] * 2,
-        scratch_shapes=[pltpu.VMEM(shape, BF16)]
+        scratch_shapes=[pltpu.VMEM(small, BF16), pltpu.VMEM(gout.shape, BF16)]
         + seq_buffers((rows, width))
         + fsdp_buffers(shape)
-        + semaphores(SEQ_COPIES + FSDP_COPIES + 18, 4),
+        + semaphores(SEQ_COPIES + FSDP_COPIES + 18 + 7, 5),
         compiler_params=params(6),
         name="scatter_input",
-    )(part, tokens, gain, gh1, pack, gout)
+    )(part, tokens, gain, gh1, pack, gout, down)
+
+
+def swap_halves(values):
+    lane = lax.broadcasted_iota(jnp.int32, values.shape, 1)
+    ahead, behind = pltpu.roll(values, 2 * HD - HD // 2, 1), pltpu.roll(values, HD // 2, 1)
+    return jnp.where(lax.rem(lane, HD) < HD // 2, ahead, behind)
+
+
+def head_means(values):
+    low = lanes_low(values.shape)
+    first = jnp.sum(jnp.where(low, values, 0.0), axis=1, keepdims=True)
+    second = jnp.sum(jnp.where(low, 0.0, values), axis=1, keepdims=True)
+    return jnp.where(low, first, second) * (1.0 / HD)
+
+
+def heads_kernel(x_ref, weight_ref, gain_ref, gains_ref, cos_ref, sin_ref, n1_ref, pre_ref, q_ref, kv_ref):
+    def tokens(t, _):
+        at = pl.ds(pl.multiple_of(t * 256, 256), 256)
+        x = x_ref[at, :].astype(F32)
+        n1 = (x * unit_rows(x) * gain_ref[...]).astype(BF16)
+        n1_ref[at, :] = n1
+        pre = dot_nn(n1, weight_ref[...])
+        pre_ref[at, :] = pre
+        cosine, sine = cos_ref[at, :], sin_ref[at, :]
+        outs = []
+        for part in (0, 1):
+            values = pre[:, part * 2 * HD : (part + 1) * 2 * HD]
+            inverse = lax.rsqrt(head_means(values * values) + EPSILON)
+            normed = values * inverse * gains_ref[part : part + 1, :]
+            outs.append(normed * cosine + swap_halves(normed) * sine)
+        q_ref[at, :] = outs[0].astype(BF16)
+        kv_ref[at, :] = jnp.where(lanes_low(outs[1].shape), outs[1], pre[:, 2 * HD :]).astype(BF16)
+        return 0
+
+    lax.fori_loop(0, x_ref.shape[0] // 256, tokens, 0)
+
+
+def project_heads(x, weight, gain, gains, cosine, sine):
+    count, width = x.shape
+    return pl.pallas_call(
+        heads_kernel,
+        out_shape=[
+            jax.ShapeDtypeStruct((count, width), BF16),
+            jax.ShapeDtypeStruct((count, 4 * HD), F32),
+            jax.ShapeDtypeStruct((count, 2 * HD), BF16),
+            jax.ShapeDtypeStruct((count, 2 * HD), BF16),
+        ],
+        in_specs=[IN_VMEM] * 6,
+        out_specs=[IN_VMEM] * 4,
+        compiler_params=pltpu.CompilerParams(vmem_limit_bytes=VMEM),
+        name="project_heads",
+    )(x, weight, gain, gains, cosine, sine)
+
+
+def heads_back_kernel(
+    x_ref, n1_ref, pre_ref, weight_ref, gains_ref, cos_ref, sin_ref, gq_ref, gkv_ref,
+    gn1_ref, gheads_ref, gain_ref, terms_ref, gpre_ref,
+):
+    count, width = x_ref.shape
+    gain_ref[...] = jnp.zeros_like(gain_ref)
+    terms_ref[...] = jnp.zeros_like(terms_ref)
+
+    def tokens(t, _):
+        at = pl.ds(pl.multiple_of(t * 256, 256), 256)
+        cosine, sine = cos_ref[at, :], sin_ref[at, :]
+        for part, ref in ((0, gq_ref), (1, gkv_ref)):
+            columns = pl.ds(part * 2 * HD, 2 * HD)
+            grads = ref[at, :].astype(F32)
+            values = pre_ref[at, columns]
+            inverse = lax.rsqrt(head_means(values * values) + EPSILON)
+            normed = values * inverse
+            turned = grads * cosine - swap_halves(grads) * sine
+            terms_ref[part : part + 1, :] += jnp.sum(turned * normed, axis=0, keepdims=True)
+            weighted = turned * gains_ref[part : part + 1, :]
+            back = inverse * (weighted - normed * head_means(weighted * normed))
+            if part == 1:
+                back = jnp.where(lanes_low(back.shape), back, grads)
+            gpre_ref[at, columns] = back.astype(BF16)
+        gn1 = dot_nt(gpre_ref[at, :], weight_ref[...])
+        gn1_ref[at, :] = gn1.astype(BF16)
+        x = x_ref[at, :].astype(F32)
+        gain_ref[...] += jnp.sum(gn1 * (x * unit_rows(x)), axis=0, keepdims=True)
+        return 0
+
+    lax.fori_loop(0, count // 256, tokens, 0)
+
+    def columns(c, _):
+        at = pl.ds(pl.multiple_of(c * 256, 256), 256)
+        gheads_ref[at, :] = dot_tn(n1_ref[:, at], gpre_ref[...]).astype(BF16)
+        return 0
+
+    lax.fori_loop(0, width // 256, columns, 0)
+
+
+def heads_back(x, n1, pre, weight, gains, cosine, sine, gq, gkv):
+    count, width = x.shape
+    return pl.pallas_call(
+        heads_back_kernel,
+        out_shape=[
+            jax.ShapeDtypeStruct((count, width), BF16),
+            jax.ShapeDtypeStruct((width, 4 * HD), BF16),
+            jax.ShapeDtypeStruct((1, width), F32),
+            jax.ShapeDtypeStruct((2, 2 * HD), F32),
+        ],
+        in_specs=[IN_VMEM] * 9,
+        out_specs=[IN_VMEM] * 4,
+        scratch_shapes=[pltpu.VMEM((count, 4 * HD), BF16)],
+        compiler_params=pltpu.CompilerParams(vmem_limit_bytes=VMEM),
+        name="heads_back",
+    )(x, n1, pre, weight, gains, cosine, sine, gq, gkv)
 
 
 def local(
@@ -1082,8 +1197,10 @@
     index = block_start + jnp.arange(block, dtype=jnp.int32)
     positions = index - firsts(take(segments, block_start, block))
     freqs = THETA ** (-2.0 * jnp.arange(HD // 2, dtype=F32) / HD)
-    angles = positions.astype(F32)[:, None] * freqs[None, :]
-    cosine, sine = jnp.cos(angles), jnp.sin(angles)
+    angles = positions.astype(F32)[:, None] * jnp.tile(freqs, 4)[None, :]
+    side = jnp.tile(jnp.repeat(jnp.array([-1.0, 1.0], F32), HD // 2), 2)
+    cosine, sine = jnp.cos(angles), jnp.sin(angles) * side[None, :]
+    head_gains = jnp.stack([jnp.tile(gain_q, 2), jnp.tile(gain_k, 2)])
     shift = (HD**0.5 * LOG2E) * jnp.max(jnp.abs(gain_q)) * jnp.max(jnp.abs(gain_k))
     shift = shift.reshape(1)
 
@@ -1100,73 +1217,42 @@
     inner_high = jnp.maximum((q_first + 1) // KEYS, inner_low)
     ranges = jnp.stack([low, inner_low, inner_high, high, q_first])
 
-    x = x_block.astype(F32)
-    inverse_one = rms_scale(x)
-    n1 = (x * inverse_one * gain_one).astype(BF16)
-    pre = dot_nn(n1, heads_weight)
-    qp = pre[:, :per_head].reshape(block, H // KVH, HD)
-    kp = pre[:, per_head : per_head + HD]
-    value = pre[:, per_head + HD :].astype(BF16)
-    inverse_q = rms_scale(qp)
-    inverse_k = rms_scale(kp)
-    q = rotate(qp * inverse_q * gain_q, cosine[:, None, :], sine[:, None, :]).astype(BF16)
-    k = rotate(kp * inverse_k * gain_k, cosine, sine).astype(BF16)
+    n1, pre, q, kv = project_heads(
+        x_block, heads_weight, gain_one[None, :], head_gains, cosine, sine
+    )
     dy_block, kv, q = gather(
         "gather_keys",
         2,
         [(cotangent, 0, (0, 64))],
-        [(jnp.concatenate([k, value], axis=1), 0, (0, 512))],
-        [q.reshape(block, per_head)],
+        [(kv, 0, (0, 512))],
+        [q],
     )
 
     ob, o, totals = forward_attention(ranges, shift, q, first[:, None], kv)
-    ob_own, h1_own, n2, gate_up, down_w = gather_attended(
-        ob, wo, tokens, gain_two[None, :], gate_up, down_piece
+    ob_own, h1_own, branch, gh1, gb, gain_two_term, go, g_gate, g_up, g_down = hidden_block(
+        ob, wo, tokens, cotangent, gain_two[None, :], gate_up, down_piece, dy_block
     )
-    down_w = down_w.reshape(fsdp_count, PIECE, width)[:, :pieces].reshape(part, width)
-
-    gn2_part, branch, g_gate, g_up, g_down = feed_forward(n2, dy_block, gate_up, down_w)
     by_core = lambda array: array.reshape(8, 2, -1, array.shape[-1])
-    g_down = g_down.reshape(fsdp_count, pieces, width)
-    g_down = jnp.pad(g_down, ((0, 0), (0, PIECE - pieces), (0, 0)))
-    gh1, gb, gain_two_term, go, g_gate, g_up, g_down = scatter_hidden(
-        gn2_part.reshape(seq_count, rows, width),
-        h1_own,
-        cotangent,
-        gain_two[None, :],
-        wo,
-        by_core(g_gate),
-        by_core(g_up),
-        by_core(g_down.reshape(-1, width)),
-    )
     g_down = lax.ppermute(g_down, both, back_pairs)
     g_out = dot_tn(ob_own, gb).astype(BF16)
     gq, gkv = backward_attention(
         ranges, shift, q, go, o, totals, strip_first[:, None, :], kv
     )
-    layer_out, gkv, g_out, g_gate, g_up, g_down, gq = scatter_keys(
+    layer_out, gkv, g_out, g_gate, g_up, gq = scatter_keys(
         branch.reshape(seq_count, rows, width),
         h1_own,
         by_core(gkv),
         by_core(g_out),
         g_gate,
         g_up,
-        g_down,
         gq,
     )
-    gq = gq.astype(F32).reshape(block, H // KVH, HD)
-    gk = gkv[:, :HD].astype(F32)
-    gv = gkv[:, HD:]
-    gain_q_term, gqp = norm_back(
-        qp, inverse_q, gain_q, rotate(gq, cosine[:, None, :], -sine[:, None, :])
+    gn1_partial, g_heads, gain_one_term, head_terms = heads_back(
+        x_block, n1, pre, heads_weight, head_gains, cosine, sine, gq, gkv
     )
-    gain_k_term, gkp = norm_back(kp, inverse_k, gain_k, rotate(gk, cosine, -sine))
-    gpre = jnp.concatenate(
-        [gqp.reshape(block, per_head).astype(BF16), gkp.astype(BF16), gv], axis=1
-    )
-    gn1_partial = dot_nt(gpre, heads_weight)
-    gain_one_term = jnp.sum(gn1_partial * (x * inverse_one), axis=0)
-    g_heads = dot_tn(n1, gpre).astype(BF16).reshape(fsdp_count, shard, -1)
+    gain_q_term = head_terms[0, :HD] + head_terms[0, HD:]
+    gain_k_term = head_terms[1, :HD]
+    g_heads = g_heads.reshape(fsdp_count, shard, -1)
     terms = jnp.concatenate(
         [
             gain_one_term.reshape(fsdp_count, shard),
@@ -1178,18 +1264,19 @@
     ).astype(BF16)
     terms = jnp.pad(terms[:, None, :], ((0, 0), (0, 15), (0, g_heads.shape[2] - terms.shape[1])))
     pack = jnp.concatenate([g_heads, terms], axis=1)
-    input_grad, packs, g_out = scatter_input(
-        gn1_partial.astype(BF16).reshape(seq_count, rows, width),
+    input_grad, packs, g_down = scatter_input(
+        gn1_partial.reshape(seq_count, rows, width),
         tokens,
         gain_one[None, :],
         gh1,
         pack.reshape((8, 2) + pack.shape[1:]),
-        g_out,
+        g_out.reshape(seq_count, -1, pack.shape[2]),
+        g_down,
     )
-    packs = packs.reshape((seq_count,) + pack.shape[1:])
+    packs = packs.reshape(seq_count, -1, pack.shape[2])
     g_heads = packs[:, :shard]
     terms = jnp.sum(packs[:, shard].astype(F32), axis=0)
-    g_out = jnp.sum(g_out.reshape(seq_count, shard, width).astype(F32), axis=0)
+    g_out = packs[:, pack.shape[1] :].astype(F32).reshape(shard, width)
     g_down = g_down.reshape(seq_count, PIECE, width)[:, :pieces].reshape(-1, width)
     columns = lambda a: jnp.transpose(a.reshape(seq_count, shard, part), (1, 0, 2)).reshape(shard, hidden)
 

time: 414 us -> 405 us (0.978)
  Pallas kernels: 336 us -> 348 us
  local copies, waits for them, and re-layouts: 31.8 us -> 23.2 us
  other arithmetic: 21.7 us -> 15.3 us
  matrix products: 9.36 us -> 3.09 us
    pallas_call x3, Pallas kernels: 113 us -> 119 us  [the longest x1 102 us: hidden_block(): pl.pallas_call(hidden_kernel, out_shape=[jax.ShapeDtypeStruct((rows, widt...]
    pallas_call x1, Pallas kernels: 41.5 us -> 45.9 us  [scatter_input(): pl.pallas_call(input_kernel, out_shape=[jax.ShapeDtypeStruct((rows, width...]
    reduce_sum x8 -> x0, other arithmetic: 4.23 us -> none  [the longest x3 2.49 us: rms_scale(): jnp.mean(values * values, axis=-1, keepdims=True) + EPSILON]
  transfers between devices with their start and end apart: 2 -> 2, of which waited for: 0 -> 0; matrix products, arithmetic and copies ran while one was open for 7% -> 6% of each run, Pallas kernels for 30% -> 23%
where the time goes in v3:
time: 405 us; the launch traced here: 399 us
  Pallas kernels  348 us (86%)
  local copies, waits for them, and re-layouts  23.2 us (6%)
  other arithmetic  15.3 us (4%)
  starting transfers between devices  6.73 us (2%)
    pallas_call x1, Pallas kernels, hidden_block(): pl.pallas_call(hidden_kernel, out_shape=[jax.ShapeDtypeStruct((rows, widt...  102 us
    pallas_call x2, Pallas kernels, gather(): pl.pallas_call(kernel, out_shape=shapes, in_specs=[HBM] * every, out_spec...  61.6 us
    pallas_call x1, Pallas kernels, scatter_keys(): pl.pallas_call(keys_kernel, out_shape=[jax.ShapeDtypeStruct((rows, width)...  58.1 us
    pallas_call x1, Pallas kernels, scatter_input(): pl.pallas_call(input_kernel, out_shape=[jax.ShapeDtypeStruct((rows, width...  45.9 us
    pallas_call x1, Pallas kernels, backward_attention(): pl.pallas_call(backward_kernel, grid_spec=pltpu.PrefetchScalarGridSpec(nu...  40.7 us
    pallas_call x1, Pallas kernels, forward_attention(): pl.pallas_call(forward_kernel, grid_spec=pltpu.PrefetchScalarGridSpec(num...  23.2 us
    pallas_call x1, Pallas kernels, heads_back(): pl.pallas_call(heads_back_kernel, out_shape=[jax.ShapeDtypeStruct((count,...  10.2 us
  transfers between devices with their start and end apart: 2, of which 0 were waited for; matrix products, arithmetic and copies ran while one was open for 6% of the time, Pallas kernels for 23%

profile of v3, /device:TPU:8, one launch (start us, length us, event | category | flops | bytes accessed | tf_op | source)
XLA Modules:
  0.0 399.1 jit_solution(14454858911662031990)
XLA Ops:
  0.7 1.1 copy-done
  1.8 4.8 %collective-permute-start = (bf16[36,1024]{1,0:T(8,128)(2,1)S(1)}, bf16[36,1024]{1,0:T(8,128)(2,1)S(1)}, u32[]{:S(2)}, u32[]{:S(2)}) collective-permute-start(bf16[36,1024]{1,0:T(8,128)(2,1)S(1)} %constant_dynamic-slice_fusion), channel_id=1, source_target_pairs={{0,0},{2,16},{4,32},{6,48},{8,64},{10,80},{12,96},{14,112},{16,1},... | collective-permute-start | bytes 221192 | tf_op jit(solution)/shard_map/ppermute | solution.py:1168
  6.6 0.8 pad_maximum_fusion.3
  7.4 0.7 constant_dynamic-slice_fusion.3
  8.2 0.8 constant_dynamic-slice_fusion.1
  9.0 0.7 fusion.14.refs_1_
  9.7 30.7 %gather_inputs.1 = (bf16[1024,1024]{1,0:T(8,128)(2,1)}, bf16[1280,256]{1,0:T(8,128)(2,1)}, bf16[1024,1024]{1,0:T(8,128)(2,1)}) custom-call(bf16[128,1024]{1,0:T(8,128)(2,1)} %tokens.3, bf16[80,256]{1,0:T(8,128)(2,1)} %fusion.14.refs_1_, bf16[64,1024]{1,0:T(8,128)(2,1)} %refs_2_.1), custom_call_target="tpu_custom_call" | custom-call | tf_op jit(solution)/shard_map/gather_inputs/pallas_call | solution.py:537
  40.4 0.9 slice.89
  41.2 1.9 slice.92
  43.2 0.7 abs_reduce_fusion
  45.0 1.1 copy.61.first_ref
  46.0 0.7 broadcast_in_dim_reshape.12.gain
  47.0 0.7 broadcast_in_dim_reshape.11.gain_ref.gain
  49.6 1.1 dynamic-slice_bitcast_fusion
  50.7 3.1 fusion
  53.8 6.1 %project_heads.1 = (bf16[1024,1024]{1,0:T(8,128)(2,1)}, f32[1024,256]{1,0:T(8,128)}, bf16[1024,128]{1,0:T(8,128)(2,1)}, bf16[1024,128]{1,0:T(8,128)(2,1)}) custom-call(bf16[1024,1024]{1,0:T(8,128)(2,1)} %get-tuple-element.52.x_ref, bf16[1024,256]{1,0:T(8,128)(2,1)} %bitcast.68, f32[1,1024]{1,0:T(1,128)} %broadcast_in_dim_reshape.11.gain_ref.gain, ...), custom_call_target="tpu_custom_call" | custom-call | tf_op jit(solution)/shard_map/project_heads/pallas_call | solution.py:1044
  60.0 30.9 %gather_keys.1 = (bf16[1024,1024]{1,0:T(8,128)(2,1)}, bf16[16384,128]{1,0:T(8,128)(2,1)}, bf16[1024,128]{1,0:T(8,128)(2,1)}) custom-call(bf16[128,1024]{1,0:T(8,128)(2,1)} %dy_own.1, bf16[1024,128]{1,0:T(8,128)(2,1)} %get-tuple-element.53.refs_1_, bf16[1024,128]{1,0:T(8,128)(2,1)} %get-tuple-element.54.refs_2_), custom_call_target="tpu_custom_call" | custom-call | tf_op jit(solution)/shard_map/gather_keys/pallas_call | solution.py:537
  90.9 0.6 stack.20.ranges_ref
  91.5 23.2 %attention_forward.1 = (bf16[1024,128]{1,0:T(8,128)(2,1)}, f32[8,256,128]{2,1,0:T(8,128)}, f32[8,256,128]{2,1,0:T(8,128)}) custom-call(s32[5,8]{1,0:T(8,128)} %stack.20.ranges_ref, f32[1]{0:T(128)} %bitcast.8.shift_ref, bf16[1024,128]{1,0:T(8,128)(2,1)} %get-tuple-element.55.query_ref, s32[1024,1]{1,0:T(8,128)} %copy.61.first_ref, ...), custom_call_target="tpu_custom_call" | custom-call | flops 8000000000 | bytes 8000000 | tf_op jit(solution)/shard_map/attention_forward/pallas_call | solution.py:118
  114.7 0.7 pad_maximum_fusion.1.gate_up
  115.4 0.6 pad.13.down
  116.0 102.2 %scatter_hidden_block.1 = (bf16[128,1024]{1,0:T(8,128)(2,1)}, f32[128,1024]{1,0:T(8,128)}, bf16[1024,1024]{1,0:T(8,128)(2,1)}, f32[128,1024]{1,0:T(8,128)}, bf16...) custom-call(bf16[1024,128]{1,0:T(8,128)(2,1)} %get-tuple-element.57., ...), custom_call_target="tpu_custom_call" | custom-call | tf_op jit(solution)/shard_map/scatter_hidden_block/pallas_call | solution.py:855
  218.3 3.1 convolution_convert_fusion
  221.4 40.7 %attention_backward.1 = (bf16[1024,128]{1,0:T(8,128)(2,1)}, bf16[16384,128]{1,0:T(8,128)(2,1)}) custom-call(s32[5,8]{1,0:T(8,128)} %stack.20.ranges_ref, f32[1]{0:T(128)} %bitcast.8.shift_ref, bf16[1024,128]{1,0:T(8,128)(2,1)} %get-tuple-element.55.query_ref, bf16[1024,128]{1,0:T(8,128)(2,1)} %get-tuple-element.62.grad_ref, ...), custom_call_target="tpu_custom_call" | custom-call | flops 20000000000 | bytes 16000000 | tf_op jit(solution)/shard_map/attention_backward/pallas_call | solution.py:198
  262.0 58.1 %scatter_keys.1 = (bf16[128,1024]{1,0:T(8,128)(2,1)}, bf16[1024,128]{1,0:T(8,128)(2,1)}, bf16[64,1024]{1,0:T(8,128)(2,1)}, bf16[512,576]{1,0:T(8,128)(2,1)}, bf1...) custom-call(bf16[8,128,1024]{2,1,0:T(8,128)(2,1)} %bitcast.72, f32[128,1024]{1,0:T(8,128)} %get-tuple-element.61.h1, ...), custom_call_target="tpu_custom_call" | custom-call | tf_op jit(solution)/shard_map/scatter_keys/pallas_call | solution.py:921
  320.2 10.2 %heads_back.1 = (bf16[1024,1024]{1,0:T(8,128)(2,1)}, bf16[1024,256]{1,0:T(8,128)(2,1)}, f32[1,1024]{1,0:T(1,128)}, f32[2,128]{1,0:T(2,128)}) custom-call(bf16[1024,1024]{1,0:T(8,128)(2,1)} %get-tuple-element.52.x_ref, bf16[1024,1024]{1,0:T(8,128)(2,1)} %get-tuple-element.72.n1_ref, f32[1024,256]{1,0:T(8,128)} %get-tuple-element.73.pre_ref, ...), custom_call_target="tpu_custom_call" | custom-call | tf_op jit(solution)/shard_map/heads_back/pallas_call | solution.py:1101
  330.3 0.8 convert_reduce_fusion.3
  331.1 0.7 convert.35
  331.9 1.9 collective-permute-start.1
  333.9 0.7 convert_reduce_fusion.2
  334.9 0.8 reshape.496.gout
  335.7 0.8 copy.69
  336.5 1.3 reshape.507
  337.9 0.8 copy.70
  338.7 1.3 reshape.508
  340.2 0.9 pad_maximum_fusion.pack
  341.0 0.6 copy-done.8
  341.7 45.9 %scatter_input.1 = (f32[128,1024]{1,0:T(8,128)}, bf16[896,256]{1,0:T(8,128)(2,1)}, bf16[384,1024]{1,0:T(8,128)(2,1)}) custom-call(bf16[8,128,1024]{2,1,0:T(8,128)(2,1)} %bitcast.71, bf16[128,1024]{1,0:T(8,128)(2,1)} %tokens.3, f32[1,1024]{1,0:T(1,128)} %broadcast_in_dim_reshape.11.gain_ref.gain, f32[128,1024]{1,0:T(8,128)} %get-tuple-element.77.gh1, ...), custom_call_target="tpu_custom_call" | custom-call | tf_op jit(solution)/shard_map/scatter_input/pallas_call | solution.py:989
  387.6 0.8 fusion.15
  389.6 0.9 slice_convert_fusion.1
  390.5 1.6 copy_bitcast_fusion
  392.1 1.1 convert_bitcast_fusion.2
  393.2 0.8 reshape.506
  394.2 0.8 reshape.504
  395.1 0.8 reshape.503
  396.0 1.1 reshape.509
  397.2 0.7 copy.79
  397.9 0.8 copy.80
  (70 shorter events, 4.5 us)
Async XLA Ops:
  0.6 1.1 copy-start
  0.7 43.6 %copy-start.13 = (f32[2]{0:T(128)S(1)}, f32[2]{0:T(128)}, u32[]{:S(2)}) copy-start(f32[2]{0:T(128)} %constant.146.clone) | copy-start | bytes 28
  0.7 43.2 %copy-start.9 = (s32[16384]{0:T(1024)S(1)}, s32[16384]{0:T(1024)}, u32[]{:S(2)}) copy-start(s32[16384]{0:T(1024)} %param.16) | copy-start | bytes 196612
  1.8 113.6 %collective-permute-start = (bf16[36,1024]{1,0:T(8,128)(2,1)S(1)}, bf16[36,1024]{1,0:T(8,128)(2,1)S(1)}, u32[]{:S(2)}, u32[]{:S(2)}) collective-permute-start(bf16[36,1024]{1,0:T(8,128)(2,1)S(1)} %constant_dynamic-slice_fusion), channel_id=1, source_target_pairs={{0,0},{2,16},{4,32},{6,48},{8,64},{10,80},{12,96},{14,112},{16,1},... | collective-permute-start | bytes 221192 | tf_op jit(solution)/shard_map/ppermute | solution.py:1168
  44.7 15.2 %copy-start.10 = (s32[1024]{0:T(1024)}, s32[1024]{0:T(1024)S(1)}, u32[]{:S(2)}) copy-start(s32[1024]{0:T(1024)S(1)} %get-tuple-element.94) | copy-start | bytes 12292
  320.1 11.7 %copy-start.11 = (f32[1,1024]{1,0:T(1,128)S(1)}, f32[1,1024]{1,0:T(1,128)}, u32[]{:S(2)}) copy-start(f32[1,1024]{1,0:T(1,128)} %get-tuple-element.80) | copy-start | bytes 12292
  320.1 11.8 %copy-start.12 = (bf16[48,1024]{1,0:T(8,128)(2,1)S(1)}, bf16[48,1024]{1,0:T(8,128)(2,1)}, u32[]{:S(2)}) copy-start(bf16[48,1024]{1,0:T(8,128)(2,1)} %get-tuple-element.83) | copy-start | bytes 294916
  320.1 14.7 %copy-start.7 = (bf16[64,1024]{1,0:T(8,128)(2,1)S(1)}, bf16[64,1024]{1,0:T(8,128)(2,1)}, u32[]{:S(2)}) copy-start(bf16[64,1024]{1,0:T(8,128)(2,1)} %get-tuple-element.82) | copy-start | bytes 393220
  320.1 15.5 %copy-start.2 = (bf16[512,576]{1,0:T(8,128)(2,1)S(1)}, bf16[512,576]{1,0:T(8,128)(2,1)}, u32[]{:S(2)}) copy-start(bf16[512,576]{1,0:T(8,128)(2,1)} %get-tuple-element.86) | copy-start | bytes 1769476
  331.9 9.1 %collective-permute-start.1 = (bf16[48,1024]{1,0:T(8,128)(2,1)S(1)}, bf16[48,1024]{1,0:T(8,128)(2,1)S(1)}, u32[]{:S(2)}, u32[]{:S(2)}) collective-permute-start(bf16[48,1024]{1,0:T(8,128)(2,1)S(1)} %copy-done.12), channel_id=1, source_target_pairs={{0,0},{16,2},{32,4},{48,6},{64,8},{80,10},{96,12},{112,14},{1,16},... | collective-permute-start | bytes 294920 | tf_op jit(solution)/shard_map/ppermute | solution.py:1236
  336.5 1.3 copy-start.1
  338.7 1.4 copy-start.4
  341.0 0.6 copy-start.8
  393.2 2.6 copy-start.3
  396.0 1.2 copy-start.6
  396.0 1.9 copy-start.5

commit v4 on v3

--- a/solution.py
+++ b/solution.py
@@ -414,6 +414,52 @@
         pl.semaphore_wait(barrier, len(peers) + 2)
 
 
+class Move:
+    def __init__(self, src, dst, peer, stays, sem):
+        self.stays = stays
+        self.own = pltpu.make_async_remote_copy(
+            src_ref=src,
+            dst_ref=dst,
+            send_sem=sem.at[0],
+            recv_sem=sem.at[1],
+            device_id=peer,
+            device_id_type=MESH,
+        )
+        self.kept = pltpu.make_async_copy(src, dst, sem.at[2])
+
+        @pl.when(stays)
+        def _():
+            self.kept.start()
+
+        @pl.when(jnp.logical_not(stays))
+        def _():
+            self.own.start()
+
+    def wait(self):
+        @pl.when(self.stays)
+        def _():
+            self.kept.wait()
+
+        @pl.when(jnp.logical_not(self.stays))
+        def _():
+            self.own.wait()
+
+
+def greet_for_move(places, peers, sender):
+    barrier = pltpu.get_barrier_semaphore()
+    for peer in peers:
+        pl.semaphore_signal(barrier, inc=1, device_id=peer, device_id_type=MESH)
+
+    @pl.when(places.fixed)
+    def _():
+        pl.semaphore_wait(barrier, len(peers))
+
+    @pl.when(jnp.logical_not(places.fixed))
+    def _():
+        pl.semaphore_signal(barrier, inc=1, device_id=sender, device_id_type=MESH)
+        pl.semaphore_wait(barrier, len(peers) + 1)
+
+
 def strips_at(ref, index):
     return ref.at[pl.ds(pl.multiple_of(index * STRIP, STRIP), STRIP), :]
 
@@ -432,6 +478,9 @@
         self.sibling = pair_of(self.fsdp)
         self.across = lax.rem(self.fsdp + 8, 16)
         self.stays = self.chip == self.seq
+        self.piece_to = (self.chip, self.core * 8 + self.seq)
+        self.piece_from = (lax.rem(self.fsdp, 8), 2 * self.seq + lax.div(self.fsdp, 8))
+        self.fixed = (self.chip == self.seq) & (self.core * 8 + self.seq == self.fsdp)
 
     def on_seq(self, index):
         return (index, self.fsdp)
@@ -505,15 +554,21 @@
         self.kept.wait()
 
 
-def gather(name, name_id, seq_items, fsdp_items, strips=()):
+def gather(name, name_id, seq_items, fsdp_items, strips=(), pieces=None):
     items = seq_items + fsdp_items
     count = len(items)
     every = count + len(strips)
+    sources = [item[0] for item in items] + list(strips) + ([] if pieces is None else [pieces])
 
     def kernel(*refs):
-        srcs, outs = refs[:every], refs[every : 2 * every]
-        copies, places = Copies(*refs[2 * every :]), Places()
-        greet(places.gather_peers() + (places.strip_peers() if strips else []))
+        total = len(sources)
+        srcs, outs, rest = refs[:total], refs[total : 2 * total], refs[2 * total :]
+        copies, places = Copies(*rest[:3]), Places()
+        peers = places.gather_peers() + (places.strip_peers() if strips else [])
+        if pieces is None:
+            greet(peers)
+        else:
+            greet_for_move(places, peers, places.piece_from)
         stages = []
         order = list(range(count))
         for i in order[::-1] if strips else order:
@@ -522,6 +577,9 @@
             stages.append(make(copies, places, srcs[i], outs[i], axis, split))
             next(stages[-1])
         moved = [Strips(copies, places, srcs[i], outs[i]) for i in range(count, every)]
+        if pieces is not None:
+            at = pl.ds(pl.multiple_of(places.seq * PIECE, 16), PIECE)
+            moved.append(Move(srcs[-1].at[at], outs[-1], places.piece_to, places.fixed, rest[3]))
         run_stages(stages)
         for item in moved:
             item.wait()
@@ -533,16 +591,20 @@
         shape[axis] *= 8 if i < len(seq_items) else 16
         shapes.append(jax.ShapeDtypeStruct(tuple(shape), array.dtype))
     shapes += [jax.ShapeDtypeStruct(array.shape, array.dtype) for array in strips]
+    extra = []
+    if pieces is not None:
+        shapes.append(jax.ShapeDtypeStruct((PIECE,) + pieces.shape[1:], pieces.dtype))
+        extra = [pltpu.SemaphoreType.DMA((3,))]
     remote = 9 * len(seq_items) + 17 * len(fsdp_items) + 7 * len(strips)
     return pl.pallas_call(
         kernel,
         out_shape=shapes,
-        in_specs=[HBM] * every,
-        out_specs=[HBM] * every,
-        scratch_shapes=semaphores(remote, every),
+        in_specs=[HBM] * len(sources),
+        out_specs=[HBM] * len(sources),
+        scratch_shapes=semaphores(remote, every) + extra,
         compiler_params=params(name_id),
         name=name,
-    )(*[item[0] for item in items], *strips)
+    )(*sources)
 
 
 class RingSum:
@@ -786,26 +848,33 @@
     next(tokens_in)
     feed(2)
 
-    def columns(c, _):
+    sums = []
+
+    def weight_sum(c, part_ref, grads):
         at = pl.ds(pl.multiple_of(c * 256, 256), 256)
-        values = n2_all[:, at]
-        two = pl.ds(c * 2, 2)
-        shape = (2, 2) + gate_part.shape[2:]
-        gate_part[two] = dot_tn(values, ggate[...]).astype(BF16).reshape(shape)
-        up_part[two] = dot_tn(values, gup[...]).astype(BF16).reshape(shape)
+        shape = (2, 2) + part_ref.shape[2:]
+        part_ref[pl.ds(c * 2, 2)] = dot_tn(n2_all[:, at], grads[...]).astype(BF16).reshape(shape)
+        return 0
+
+    def down_sum(c, _):
+        at = pl.ds(pl.multiple_of(c * 256, 256), 256)
         g_down = dot_nn(matrix, dot_tn(act[...], dy[:, at]).astype(BF16)).astype(BF16)
         down_part[:, :, :, at] = g_down.reshape((8, 2, PIECE, 256))
         return 0
 
-    lax.fori_loop(0, width // 256, columns, 0)
-    sums = [
-        FsdpSum(copies, places, gate_part, sums_at[:5], 32),
-        FsdpSum(copies, places, up_part, sums_at[5:10], 32),
-        FsdpSum(copies, places, down_part, sums_at[10:15], 32),
-    ]
-    for item in sums:
+    lax.fori_loop(0, width // 256, lambda c, _: weight_sum(c, gate_part, ggate), 0)
+    sums.append(FsdpSum(copies, places, gate_part, sums_at[:5], 32))
+    lax.fori_loop(0, width // 256, lambda c, _: weight_sum(c, up_part, gup), 0)
+    sums.append(FsdpSum(copies, places, up_part, sums_at[5:10], 32))
+    sums[0].ready()
+    sums[0].send()
+    lax.fori_loop(0, width // 256, down_sum, 0)
+    sums.append(FsdpSum(copies, places, down_part, sums_at[10:15], 32))
+    for item in sums[1:]:
         item.ready()
         item.send()
+    for item in sums[:2]:
+        item.relay()
     gn2 = gn2_all[pl.ds(pl.multiple_of(places.seq * rows, rows), rows), :].astype(F32)
     for copy in arrivals:
         copy.wait_recv()
@@ -830,8 +899,7 @@
     landing = strips_at(go_ref, places.chip)
     sends = [(heads_at(go_own, head), landing, peer) for head, peer in zip(heads, workers)]
     swap_back = Swap(copies, tags_back, ends_back, places.chip, places.stays, sends)
-    for item in sums:
-        item.relay()
+    sums[2].relay()
     for item in sums:
         item.cross()
     for item, out in zip(sums, (gate_out, up_out, down_out)):
@@ -873,31 +941,34 @@
 
 
 def keys_kernel(
-    branch, h1, gkv, gout, gate, up, gq,
-    layer_ref, gkv_out, gout_out, gate_all, up_all, gq_out,
+    branch, h1, gkv, gout, gate, up, gq, down,
+    layer_ref, gkv_out, gout_out, gate_all, up_all, gq_out, down_out, ends,
     *scratch,
 ):
     copies, places = Copies(*scratch[14:]), Places()
-    greet(places.gather_peers() + places.strip_peers())
-    moved = Strips(copies, places, gq, gq_out)
+    greet_for_move(places, places.gather_peers() + places.strip_peers(), places.piece_to)
+    moved = Move(down, down_out, places.piece_from, places.fixed, ends)
+    stages = [
+        seq_gather(copies, places, gate, gate_all, 0, (0, 32)),
+        seq_gather(copies, places, up, up_all, 0, (0, 32)),
+    ]
+    for stage in stages:
+        next(stage)
     sums = [
         FsdpSum(copies, places, gkv, scratch[4:9], 512),
         FsdpSum(copies, places, gout, scratch[9:14], 32),
     ]
     hidden = SeqSum(copies, places, branch, scratch[:4], 64)
-    stages = [
-        seq_gather(copies, places, gate, gate_all, 0, (0, 32)),
-        seq_gather(copies, places, up, up_all, 0, (0, 32)),
-    ]
     items = [hidden] + sums
-    hidden.ready()
-    hidden.send()
-    for stage in stages:
-        next(stage)
-    for item in sums:
+    for item in items:
         item.ready()
         item.send()
-    for item in items:
+    strips = Strips(copies, places, gq, gq_out)
+    for _ in range(2):
+        for stage in stages:
+            next(stage)
+    hidden.relay()
+    for item in sums:
         item.relay()
     for stage in stages:
         next(stage)
@@ -907,14 +978,15 @@
     for item, out in zip(sums, (gkv_out, gout_out)):
         out[...] = item.total().astype(BF16)
     layer_ref[...] = (h1[...] + hidden.total()).astype(BF16)
+    strips.wait()
     moved.wait()
     copies.finish()
 
 
-def scatter_keys(branch, h1, gkv, gout, gate, up, gq):
+def scatter_keys(branch, h1, gkv, gout, gate, up, gq, down):
     rows, width = h1.shape
     shapes = [a.shape[2:] for a in (gkv, gout)]
-    scratch = seq_buffers((rows, width))
+    scratch = [pltpu.SemaphoreType.DMA((3,))] + seq_buffers((rows, width))
     for shape in shapes:
         scratch += fsdp_buffers(shape)
     wide = [jax.ShapeDtypeStruct((8 * a.shape[0],) + a.shape[1:], BF16) for a in (gate, up)]
@@ -923,13 +995,13 @@
         out_shape=[jax.ShapeDtypeStruct((rows, width), BF16)]
         + [jax.ShapeDtypeStruct(shape, BF16) for shape in shapes]
         + wide
-        + [jax.ShapeDtypeStruct(gq.shape, BF16)],
-        in_specs=[HBM, IN_VMEM] + [HBM] * 5,
-        out_specs=[IN_VMEM] * 3 + [HBM] * 3,
+        + [jax.ShapeDtypeStruct(gq.shape, BF16), jax.ShapeDtypeStruct(down.shape, BF16)],
+        in_specs=[HBM, IN_VMEM] + [HBM] * 6,
+        out_specs=[IN_VMEM] * 3 + [HBM] * 4,
         scratch_shapes=scratch + semaphores(SEQ_COPIES + 2 * FSDP_COPIES + 18 + 7, 6),
         compiler_params=params(5),
         name="scatter_keys",
-    )(branch, h1, gkv, gout, gate, up, gq)
+    )(branch, h1, gkv, gout, gate, up, gq, down)
 
 
 def input_kernel(
@@ -940,9 +1012,9 @@
     copies, places = Copies(*scratch[9:]), Places()
     steps = range(1, 8)
     greet(places.gather_peers() + [places.on_seq(places.other_seq(d)) for d in steps])
-    hidden = SeqSum(copies, places, part, scratch[:4], 64)
-    hidden.ready()
-    hidden.send()
+    packs = FsdpSum(copies, places, pack, scratch[4:9], 48)
+    stages = [seq_gather(copies, places, down, down_all, 0, (0, 16))]
+    next(stages[0])
     outs = [
         copies.remote(
             gout.at[places.other_seq(d)], gathered.at[d], places.on_seq(places.other_seq(d))
@@ -950,16 +1022,15 @@
         for d in steps
     ]
     own = copies.here(gout.at[places.seq], gathered.at[0])
-    packs = FsdpSum(copies, places, pack, scratch[4:9], 48)
+    hidden = SeqSum(copies, places, part, scratch[:4], 64)
     packs.ready()
     packs.send()
-    stages = [seq_gather(copies, places, down, down_all, 0, (0, 16))]
+    hidden.ready()
+    hidden.send()
     next(stages[0])
     packs.relay()
-    hidden.relay()
+    next(stages[0])
     packs.cross()
-    next(stages[0])
-    hidden.cross()
     own.wait()
     for copy in outs:
         copy.wait_recv()
@@ -971,6 +1042,11 @@
     small[:rows] = packs.total().astype(BF16)
     stages.append(seq_gather(copies, places, small, pack_all, 0, (0, 64)))
     next(stages[1])
+    hidden.relay()
+    next(stages[0])
+    next(stages[1])
+    next(stages[1])
+    hidden.cross()
     run_stages(stages)
     gn1 = hidden.total()
     value = tokens[...].astype(F32)
@@ -1142,18 +1218,6 @@
     block_start = fsdp * block
     take = lax.dynamic_slice_in_dim
 
-    ratio = fsdp_count // seq_count
-    pairs = [
-        (
-            f % seq_count * fsdp_count + ratio * s + f // (fsdp_count // ratio),
-            s * fsdp_count + f,
-        )
-        for f in range(fsdp_count)
-        for s in range(seq_count)
-    ]
-    back_pairs = [(b, a) for a, b in pairs]
-    both = ("seq", "fsdp")
-
     gains = jnp.concatenate([attention_gain, feedforward_gain, query_gain, key_gain])
     heads_weight = jnp.concatenate(
         [
@@ -1165,16 +1229,18 @@
     )
     gains = jnp.pad(gains[None, :], ((0, 15), (0, heads_weight.shape[1] - gains.shape[0])))
     pieces = down_weight.shape[0] // seq_count
-    down_piece = lax.ppermute(take(down_weight, seq * pieces, pieces, 0), both, pairs)
-    down_piece = jnp.pad(down_piece, ((0, PIECE - pieces), (0, 0)))
+    down_pieces = jnp.pad(
+        down_weight.reshape(seq_count, pieces, width), ((0, 0), (0, PIECE - pieces), (0, 0))
+    ).reshape(-1, width)
     gate_up = jnp.stack(
         [take(gate_weight, seq * part, part, 1), take(up_weight, seq * part, part, 1)]
     )
-    x_block, packs, wo = gather(
+    x_block, packs, wo, down_piece = gather(
         "gather_inputs",
         1,
         [(tokens, 0, (0, 64))],
         [(jnp.concatenate([heads_weight, gains]), 0, (0, 48)), (out_weight, 0, (0, 32))],
+        pieces=down_pieces,
     )
     packs = packs.reshape(fsdp_count, -1, packs.shape[1])
     heads_weight = packs[:, : width // fsdp_count].reshape(width, -1)
@@ -1233,12 +1299,11 @@
         ob, wo, tokens, cotangent, gain_two[None, :], gate_up, down_piece, dy_block
     )
     by_core = lambda array: array.reshape(8, 2, -1, array.shape[-1])
-    g_down = lax.ppermute(g_down, both, back_pairs)
     g_out = dot_tn(ob_own, gb).astype(BF16)
     gq, gkv = backward_attention(
         ranges, shift, q, go, o, totals, strip_first[:, None, :], kv
     )
-    layer_out, gkv, g_out, g_gate, g_up, gq = scatter_keys(
+    layer_out, gkv, g_out, g_gate, g_up, gq, g_down = scatter_keys(
         branch.reshape(seq_count, rows, width),
         h1_own,
         by_core(gkv),
@@ -1246,6 +1311,7 @@
         g_gate,
         g_up,
         gq,
+        g_down,
     )
     gn1_partial, g_heads, gain_one_term, head_terms = heads_back(
         x_block, n1, pre, heads_weight, head_gains, cosine, sine, gq, gkv

time: 405 us -> 395 us (0.975)
  starting transfers between devices: 6.73 us -> 0 us
    ppermute x2 -> x0, starting transfers between devices: 6.73 us -> none  [the longest x1 4.82 us: local(): lax.ppermute(take(down_weight, seq * pieces, pieces, 0), both, pairs)]
    pallas_call x1, Pallas kernels: 45.9 us -> 40.7 us  [scatter_input(): pl.pallas_call(input_kernel, out_shape=[jax.ShapeDtypeStruct((rows, width...]
  transfers between devices with their start and end apart: 2 -> 0, of which waited for: 0 -> 0; matrix products, arithmetic and copies ran while one was open for 6% -> 0% of each run, Pallas kernels for 23% -> 0%
where the time goes in v4:
time: 395 us; the launch traced here: 390 us
  Pallas kernels  345 us (87%)
  local copies, waits for them, and re-layouts  23.4 us (6%)
  other arithmetic  16.3 us (4%)
    pallas_call x1, Pallas kernels, hidden_block(): pl.pallas_call(hidden_kernel, out_shape=[jax.ShapeDtypeStruct((rows, widt...  101 us
    pallas_call x2, Pallas kernels, gather(): pl.pallas_call(kernel, out_shape=shapes, in_specs=[HBM] * len(sources), o...  63.2 us
    pallas_call x1, Pallas kernels, scatter_keys(): pl.pallas_call(keys_kernel, out_shape=[jax.ShapeDtypeStruct((rows, width)...  60.9 us
    pallas_call x1, Pallas kernels, scatter_input(): pl.pallas_call(input_kernel, out_shape=[jax.ShapeDtypeStruct((rows, width...  40.7 us
    pallas_call x1, Pallas kernels, backward_attention(): pl.pallas_call(backward_kernel, grid_spec=pltpu.PrefetchScalarGridSpec(nu...  40.5 us
    pallas_call x1, Pallas kernels, forward_attention(): pl.pallas_call(forward_kernel, grid_spec=pltpu.PrefetchScalarGridSpec(num...  23.2 us
    pallas_call x1, Pallas kernels, heads_back(): pl.pallas_call(heads_back_kernel, out_shape=[jax.ShapeDtypeStruct((count,...  10.1 us

profile of v4, /device:TPU:8, one launch (start us, length us, event | category | flops | bytes accessed | tf_op | source)
XLA Modules:
  0.0 389.8 jit_solution(15195905539861681368)
XLA Ops:
  0.7 1.2 convert_reduce_fusion
  2.0 0.8 pad_maximum_fusion.3
  2.8 0.7 broadcast_in_dim.7
  3.8 0.8 constant_dynamic-slice_fusion.3
  4.6 0.7 dynamic_slice.28
  5.6 0.6 stack.20.ranges_ref
  6.2 0.8 constant_dynamic-slice_fusion
  7.1 0.7 fusion.14.refs_1_
  7.8 1.1 dynamic-slice_bitcast_fusion
  8.8 0.7 pad_maximum_fusion.1.gate_up
  9.5 1.1 copy.61.first_ref
  10.7 1.0 pad.13
  11.7 3.1 fusion
  14.7 31.1 %gather_inputs.1 = (bf16[1024,1024]{1,0:T(8,128)(2,1)}, bf16[1280,256]{1,0:T(8,128)(2,1)}, bf16[1024,1024]{1,0:T(8,128)(2,1)}, bf16[48,1024]{1,0:T(8,128)(2,1)}) custom-call(bf16[128,1024]{1,0:T(8,128)(2,1)} %tokens.3, bf16[80,256]{1,0:T(8,128)(2,1)} %fusion.14.refs_1_, bf16[64,1024]{1,0:T(8,128)(2,1)} %refs_2_.1, bf16[384,1024]{1,0:T(8,128)(2,1)} %bitcast.72), custom_call_target="tpu_custom_call" | custom-call | tf_op jit(solution)/shard_map/gather_inputs/pallas_call | solution.py:599
  45.9 0.9 slice.89
  46.7 1.9 slice.92
  48.7 0.7 broadcast_in_dim_reshape.12.gain
  49.4 0.7 abs_reduce_fusion
  52.3 0.7 broadcast_in_dim_reshape.11.gain_ref.gain
  53.0 6.1 %project_heads.1 = (bf16[1024,1024]{1,0:T(8,128)(2,1)}, f32[1024,256]{1,0:T(8,128)}, bf16[1024,128]{1,0:T(8,128)(2,1)}, bf16[1024,128]{1,0:T(8,128)(2,1)}) custom-call(bf16[1024,1024]{1,0:T(8,128)(2,1)} %get-tuple-element.54.x_ref, bf16[1024,256]{1,0:T(8,128)(2,1)} %bitcast.69, f32[1,1024]{1,0:T(1,128)} %broadcast_in_dim_reshape.11.gain_ref.gain, ...), custom_call_target="tpu_custom_call" | custom-call | tf_op jit(solution)/shard_map/project_heads/pallas_call | solution.py:1120
  59.1 32.0 %gather_keys.1 = (bf16[1024,1024]{1,0:T(8,128)(2,1)}, bf16[16384,128]{1,0:T(8,128)(2,1)}, bf16[1024,128]{1,0:T(8,128)(2,1)}) custom-call(bf16[128,1024]{1,0:T(8,128)(2,1)} %dy_own.1, bf16[1024,128]{1,0:T(8,128)(2,1)} %get-tuple-element.55.refs_1_, bf16[1024,128]{1,0:T(8,128)(2,1)} %get-tuple-element.56.refs_2_), custom_call_target="tpu_custom_call" | custom-call | tf_op jit(solution)/shard_map/gather_keys/pallas_call | solution.py:599
  91.1 23.2 %attention_forward.1 = (bf16[1024,128]{1,0:T(8,128)(2,1)}, f32[8,256,128]{2,1,0:T(8,128)}, f32[8,256,128]{2,1,0:T(8,128)}) custom-call(s32[5,8]{1,0:T(8,128)} %stack.20.ranges_ref, f32[1]{0:T(128)} %bitcast.9.shift_ref, bf16[1024,128]{1,0:T(8,128)(2,1)} %get-tuple-element.57.query_ref, s32[1024,1]{1,0:T(8,128)} %copy.61.first_ref, ...), custom_call_target="tpu_custom_call" | custom-call | flops 8000000000 | bytes 8000000 | tf_op jit(solution)/shard_map/attention_forward/pallas_call | solution.py:118
  114.3 100.7 %scatter_hidden_block.1 = (bf16[128,1024]{1,0:T(8,128)(2,1)}, f32[128,1024]{1,0:T(8,128)}, bf16[1024,1024]{1,0:T(8,128)(2,1)}, f32[128,1024]{1,0:T(8,128)}, bf16...) custom-call(bf16[1024,128]{1,0:T(8,128)(2,1)} %get-tuple-element.59., ...), custom_call_target="tpu_custom_call" | custom-call | tf_op jit(solution)/shard_map/scatter_hidden_block/pallas_call | solution.py:923
  215.0 40.5 %attention_backward.1 = (bf16[1024,128]{1,0:T(8,128)(2,1)}, bf16[16384,128]{1,0:T(8,128)(2,1)}) custom-call(s32[5,8]{1,0:T(8,128)} %stack.20.ranges_ref, f32[1]{0:T(128)} %bitcast.9.shift_ref, bf16[1024,128]{1,0:T(8,128)(2,1)} %get-tuple-element.57.query_ref, bf16[1024,128]{1,0:T(8,128)(2,1)} %get-tuple-element.65.grad_ref, ...), custom_call_target="tpu_custom_call" | custom-call | flops 20000000000 | bytes 16000000 | tf_op jit(solution)/shard_map/attention_backward/pallas_call | solution.py:198
  255.6 2.1 convolution_convert_fusion
  257.7 60.9 %scatter_keys.1 = (bf16[128,1024]{1,0:T(8,128)(2,1)}, bf16[1024,128]{1,0:T(8,128)(2,1)}, bf16[64,1024]{1,0:T(8,128)(2,1)}, bf16[512,576]{1,0:T(8,128)(2,1)}, bf1...) custom-call(bf16[8,128,1024]{2,1,0:T(8,128)(2,1)} %bitcast.74, ...), custom_call_target="tpu_custom_call" | custom-call | tf_op jit(solution)/shard_map/scatter_keys/pallas_call | solution.py:993
  318.6 10.1 %heads_back.1 = (bf16[1024,1024]{1,0:T(8,128)(2,1)}, bf16[1024,256]{1,0:T(8,128)(2,1)}, f32[1,1024]{1,0:T(1,128)}, f32[2,128]{1,0:T(2,128)}) custom-call(bf16[1024,1024]{1,0:T(8,128)(2,1)} %get-tuple-element.54.x_ref, bf16[1024,1024]{1,0:T(8,128)(2,1)} %get-tuple-element.76.n1_ref, f32[1024,256]{1,0:T(8,128)} %get-tuple-element.77.pre_ref, ...), custom_call_target="tpu_custom_call" | custom-call | tf_op jit(solution)/shard_map/heads_back/pallas_call | solution.py:1177
  328.7 0.8 convert_reduce_fusion.3
  329.5 0.7 convert.35
  330.2 0.7 convert_reduce_fusion.2
  331.3 1.9 pad_maximum_fusion.pack
  333.2 0.7 reshape.504.gout
  334.0 40.7 %scatter_input.1 = (f32[128,1024]{1,0:T(8,128)}, bf16[896,256]{1,0:T(8,128)(2,1)}, bf16[384,1024]{1,0:T(8,128)(2,1)}) custom-call(bf16[8,128,1024]{2,1,0:T(8,128)(2,1)} %bitcast.73, bf16[128,1024]{1,0:T(8,128)(2,1)} %tokens.3, f32[1,1024]{1,0:T(1,128)} %broadcast_in_dim_reshape.11.gain_ref.gain, f32[128,1024]{1,0:T(8,128)} %get-tuple-element.81.gh1, ...), custom_call_target="tpu_custom_call" | custom-call | tf_op jit(solution)/shard_map/scatter_input/pallas_call | solution.py:1065
  374.7 0.8 fusion.15
  375.6 0.6 fusion.23
  376.2 0.6 fusion.24
  376.8 0.9 slice_convert_fusion.1
  377.7 0.8 reshape.514
  378.5 1.6 copy_bitcast_fusion
  380.4 0.8 reshape.512
  381.3 0.8 reshape.511
  382.2 1.1 reshape.517
  383.6 0.8 copy.69
  384.3 1.3 reshape.515
  385.8 0.8 copy.70
  386.6 1.3 reshape.516
  387.9 0.7 copy.79
  388.6 0.8 copy.80
  (63 shorter events, 3.3 us)
Async XLA Ops:
  0.6 5.6 %copy-start = (bf16[64,1024]{1,0:T(8,128)(2,1)S(1)}, bf16[64,1024]{1,0:T(8,128)(2,1)}, u32[]{:S(2)}) copy-start(bf16[64,1024]{1,0:T(8,128)(2,1)} %param.21) | copy-start | bytes 393220
  0.7 9.9 %copy-start.4 = (bf16[288,1024]{1,0:T(8,128)(2,1)S(1)}, bf16[288,1024]{1,0:T(8,128)(2,1)}, u32[]{:S(2)}) copy-start(bf16[288,1024]{1,0:T(8,128)(2,1)} %param.28) | copy-start | bytes 1769476
  5.4 5.3 %copy-start.11 = (s32[1024]{0:T(1024)}, s32[1024]{0:T(1024)S(1)}, u32[]{:S(2)}) copy-start(s32[1024]{0:T(1024)S(1)} %get-tuple-element.98) | copy-start | bytes 12292
  215.0 40.6 %copy-start.12 = (f32[1,1024]{1,0:T(1,128)S(1)}, f32[1,1024]{1,0:T(1,128)}, u32[]{:S(2)}) copy-start(f32[1,1024]{1,0:T(1,128)} %get-tuple-element.84) | copy-start | bytes 12292
  215.0 40.7 %copy-start.7 = (bf16[128,1024]{1,0:T(8,128)(2,1)S(1)}, bf16[128,1024]{1,0:T(8,128)(2,1)}, u32[]{:S(2)}) copy-start(bf16[128,1024]{1,0:T(8,128)(2,1)} %get-tuple-element.69) | copy-start | bytes 786436
  215.0 40.6 %copy-start.8 = (bf16[128,1024]{1,0:T(8,128)(2,1)S(1)}, bf16[128,1024]{1,0:T(8,128)(2,1)}, u32[]{:S(2)}) copy-start(bf16[128,1024]{1,0:T(8,128)(2,1)} %get-tuple-element.70) | copy-start | bytes 786436
  328.7 4.6 %copy-start.10 = (bf16[64,1024]{1,0:T(8,128)(2,1)S(1)}, bf16[64,1024]{1,0:T(8,128)(2,1)}, u32[]{:S(2)}) copy-start(bf16[64,1024]{1,0:T(8,128)(2,1)} %get-tuple-element.86) | copy-start | bytes 393220
  374.7 5.4 %copy-start.3 = (bf16[896,256]{1,0:T(8,128)(2,1)S(1)}, bf16[896,256]{1,0:T(8,128)(2,1)}, u32[]{:S(2)}) copy-start(bf16[896,256]{1,0:T(8,128)(2,1)} %get-tuple-element.89) | copy-start | bytes 1376260
  380.1 2.0 copy-start.5
  382.2 1.2 copy-start.2
  384.3 1.3 copy-start.1
  386.5 1.3 copy-start.9
  386.5 2.0 copy-start.6
